TPU v7x, 128 devices: a whole 4x4x4 slice. The times are simulated.
128 devices in a mesh: edp: 16 (over y, z_hi, core), ep: 8 (over x, z_lo).
Axes of the slice: x: 4, y: 4, z: 4 (z_hi: 2, z_lo: 2; z = z_hi * 2 + z_lo), core: 2. Of those that a mesh axis runs over, the one named last changes fastest.
Arguments:
- dense_input: bfloat16 [196608, 2048], P(('edp', 'ep')), may hold values from -24 to 24
- dense_cotangent: bfloat16 [196608, 1024], P(('edp', 'ep')), may hold values from -6 to 6
- expert_input: bfloat16 [8, 16384, 2048], P('ep', 'edp'), may hold values from -6 to 6
- expert_cotangent: bfloat16 [8, 16384, 768], P('ep', 'edp'), may hold values from -6 to 6
- dense_master: float32 [2048, 1024], P(('edp', 'ep')), may hold values from -0.125 to 0.125
- dense_first: float32 [2048, 1024], P(('edp', 'ep')), may hold values from -3 to 3
- dense_second: float32 [2048, 1024], P(('edp', 'ep')), may hold values from 0.01 to 1
- expert_master: float32 [8, 2048, 768], P('ep', 'edp'), may hold values from -0.125 to 0.125
- expert_first: float32 [8, 2048, 768], P('ep', 'edp'), may hold values from -3 to 3
- expert_second: float32 [8, 2048, 768], P('ep', 'edp'), may hold values from 0.01 to 1
Outputs:
- dense_param: float32 [2048, 1024], P(('edp', 'ep'))
- dense_first_new: float32 [2048, 1024], P(('edp', 'ep'))
- dense_second_new: float32 [2048, 1024], P(('edp', 'ep'))
- dense_weight: bfloat16 [2048, 1024], replicated
- expert_param: float32 [8, 2048, 768], P('ep', 'edp')
- expert_first_new: float32 [8, 2048, 768], P('ep', 'edp')
- expert_second_new: float32 [8, 2048, 768], P('ep', 'edp')
- expert_weight: bfloat16 [8, 2048, 768], P('ep')
All inputs are finite; a program needn't handle non-finite values.
Results may differ from a plain program's by a relative error of at most 0.001.
Values may be sent and summed in bfloat16 or wider, within the bound.
No kernel may reach another device: no remote copies, remote signals or barrier semaphores. Data moves between devices by JAX's collectives and lax.ppermute only.
A program may use at most 128 MiB of HBM per device.

v0:
```python
import math

import jax
import jax.numpy as jnp
from jax import lax
from jax.sharding import PartitionSpec as P

D = 2048
FF = 768
KVW = 1024
EXP_DEV = 1
STEP = 100


def adamw(param, first, second, grad, clip):
    scaled = clip * grad
    first_new = 0.9 * first + 0.1 * scaled
    second_new = 0.95 * second + 0.05 * scaled * scaled
    first_hat = first_new / (1.0 - 0.9**STEP)
    second_hat = second_new / (1.0 - 0.95**STEP)
    param_new = param - 0.001 * (first_hat / (jnp.sqrt(second_hat) + 1e-08) + 0.1 * param)
    return (param_new, first_new, second_new)


def column_term(inputs, cotangent):
    return lax.dot_general(
        inputs, cotangent, (((0,), (0,)), ((), ())), preferred_element_type=jnp.float32
    )


def per_device(
    dense_input,
    dense_cotangent,
    expert_input,
    expert_cotangent,
    dense_master,
    dense_first,
    dense_second,
    expert_master,
    expert_first,
    expert_second,
):
    dense_grad = lax.psum_scatter(
        column_term(dense_input, dense_cotangent), ("edp", "ep"), scatter_dimension=0, tiled=True
    )
    routed_rows = expert_input[0]
    routed_cotangent = expert_cotangent[0]
    expert_grad = lax.psum_scatter(
        column_term(routed_rows, routed_cotangent), "edp", scatter_dimension=0, tiled=True
    )[None]
    total = lax.psum(
        jnp.sum(dense_grad * dense_grad) + jnp.sum(expert_grad * expert_grad), ("edp", "ep")
    )
    limit = 10.0 * math.sqrt(D * KVW + lax.axis_size("ep") * EXP_DEV * D * FF)
    clip = jnp.minimum(1.0, limit / (jnp.sqrt(total) + 1e-06))
    dense_param, dense_first_new, dense_second_new = adamw(
        dense_master, dense_first, dense_second, dense_grad, clip
    )
    expert_param, expert_first_new, expert_second_new = adamw(
        expert_master, expert_first, expert_second, expert_grad, clip
    )
    dense_rounded = dense_param.astype(jnp.bfloat16)
    dense_weight = lax.all_gather(dense_rounded, ("edp", "ep"), axis=0, tiled=True)
    expert_weight = lax.all_gather(expert_param.astype(jnp.bfloat16), "edp", axis=1, tiled=True)
    return (
        dense_param,
        dense_first_new,
        dense_second_new,
        dense_weight,
        expert_param,
        expert_first_new,
        expert_second_new,
        expert_weight,
    )


def solution(mesh):
    placed = (
        P(("edp", "ep"), None),
        P(("edp", "ep"), None),
        P("ep", "edp", None),
        P("ep", "edp", None),
        P(("edp", "ep"), None),
        P(("edp", "ep"), None),
        P(("edp", "ep"), None),
        P("ep", "edp", None),
        P("ep", "edp", None),
        P("ep", "edp", None),
    )
    return jax.shard_map(
        per_device,
        mesh=mesh,
        in_specs=placed,
        out_specs=(
            P(("edp", "ep"), None),
            P(("edp", "ep"), None),
            P(("edp", "ep"), None),
            P(),
            P("ep", "edp", None),
            P("ep", "edp", None),
            P("ep", "edp", None),
            P("ep", None, None),
        ),
        check_vma=False,
    )
```

profile of v0, /device:TPU:1, one launch (start us, length us, event | category | flops | bytes accessed | tf_op | source)
XLA Modules:
  0.0 1200.2 jit_solution(2948494543933656158)
XLA Ops:
  7.2 0.0 copy-start
  7.2 0.0 reduce-scatter.5.cloned.1.call-start
  7.2 9.0 fusion
  16.3 0.0 reduce-scatter.5.cloned.1.call-update
  16.3 0.0 reduce-scatter.3.cloned.1.call-start
  16.3 0.0 copy-done
  16.4 10.8 fusion.10
  27.2 0.0 reduce-scatter.3.cloned.1.call-update
  27.2 0.0 all-gather.5.cloned.1.call-start
  27.3 80.8 %reduce-scatter.5.cloned.1.call-done = f32[128,768]{1,0:T(8,128)} async-done(((f32[2048,768]{1,0:T(8,128)}), f32[128,768]{1,0:T(8,128)}) %reduce-scatter.5.cloned.1.call-update) | async-done | bytes 393232 | tf_op jit(solution)/shard_map/reduce_scatter | solution.py:48
  108.1 1.7 multiply_reduce_fusion
  109.8 637.0 %reduce-scatter.3.cloned.1.call-done = f32[16,1024]{1,0:T(8,128)} async-done(((f32[2048,1024]{1,0:T(8,128)}), f32[16,1024]{1,0:T(8,128)}) %reduce-scatter.3.cloned.1.call-update) | async-done | bytes 65552 | tf_op jit(solution)/shard_map/reduce_scatter | solution.py:43
  746.8 1.5 multiply_reduce_fusion.1
  749.6 77.7 %psum.7 = f32[]{:T(128)} all-reduce(f32[]{:T(128)S(6)} %add.42), channel_id=1, replica_groups=mesh['edp'=16,'ep'=8] {'edp','ep'}, use_global_device_ids=true, to_apply=%region_4.0 | all-reduce | flops 1 | bytes 8 | tf_op jit(solution)/shard_map/psum | solution.py:51
  828.1 0.0 copy-done.2
  828.1 2.5 fusion.6
  830.6 0.0 all-gather.5.cloned.1.call-update
  830.6 0.0 all-gather.3.cloned.1.call-start
  830.6 1.6 fusion.8
  832.3 0.0 all-gather.3.cloned.1.call-update
  832.3 47.6 %all-gather.5.cloned.1.call-done = bf16[1,2048,768]{2,1,0:T(8,128)(2,1)} async-done(((bf16[1,128,768]{2,1,0:T(8,128)(2,1)}), bf16[1,2048,768]{2,1,0:T(8,128)(2,1)}) %all-gather.5.cloned.1.call-update) | async-done | bytes 3145744 | tf_op jit(solution)/shard_map/all_gather | solution.py:64
  879.9 307.3 %all-gather.3.cloned.1.call-done = bf16[2048,1024]{1,0:T(8,128)(2,1)} async-done(((bf16[16,1024]{1,0:T(8,128)(2,1)}), bf16[2048,1024]{1,0:T(8,128)(2,1)}) %all-gather.3.cloned.1.call-update) | async-done | bytes 4194320 | tf_op jit(solution)/shard_map/all_gather | solution.py:63
  1187.2 4.8 copy.20
  1192.0 1.7 copy.21
  (3 shorter events, 0.0 us)
Async XLA Ops:
  7.2 9.2 copy-start
  7.2 100.9 %reduce-scatter.5.cloned.1.call-start = ((), (), s32[]{:S(2)}) async-start(), calls=%async_computation.3 | async-start | bytes 6684672 | tf_op jit(solution)/shard_map/reduce_scatter | solution.py:48
  16.3 730.5 %reduce-scatter.3.cloned.1.call-start = ((), (), s32[]{:S(2)}) async-start(), calls=%async_computation.2 | async-start | bytes 8454144 | tf_op jit(solution)/shard_map/reduce_scatter | solution.py:43
  27.2 800.9 %copy-start.2 = (f32[1,128,768]{2,1,0:T(8,128)S(1)}, f32[1,128,768]{2,1,0:T(8,128)}, u32[]{:S(2)}) copy-start(f32[1,128,768]{2,1,0:T(8,128)} %param.17) | copy-start | bytes 1179652
  27.2 852.7 %all-gather.5.cloned.1.call-start = ((), (), s32[]{:S(2)}) async-start(), calls=%async_computation.5 | async-start | bytes 3342336 | tf_op jit(solution)/shard_map/all_gather | solution.py:64
  830.6 356.6 %all-gather.3.cloned.1.call-start = ((), (), s32[]{:S(2)}) async-start(), calls=%async_computation.4 | async-start | bytes 4227072 | tf_op jit(solution)/shard_map/all_gather | solution.py:63
  1187.2 4.8 copy-start.1
Sparse Core Ops, SparseCore 0:
  16.4 91.6 reduce-scatter.4
  110.5 636.3 reduce-scatter.2
  830.7 49.1 all-gather.4
  882.1 305.0 all-gather.2
where the time goes:
time: 1200 us
  waiting for transfers between devices  1070 us (89%)
  blocking collectives  77.7 us (6%)
  matrix products  19.9 us (2%)
  between operations  15.8 us (1%)
    reduce_scatter x1, waiting for transfers between devices, per_device(): lax.psum_scatter(column_term(dense_input, dense_cotangent), ('edp', 'ep')...  637 us
    all_gather x1, waiting for transfers between devices, per_device(): lax.all_gather(dense_rounded, ('edp', 'ep'), axis=0, tiled=True)  307 us
    reduce_scatter x1, waiting for transfers between devices, per_device(): lax.psum_scatter(column_term(routed_rows, routed_cotangent), 'edp', scatt...  80.8 us
    psum x1, blocking collectives, per_device(): lax.psum(jnp.sum(dense_grad * dense_grad) + jnp.sum(expert_grad * expert_...  77.7 us
    all_gather x1, waiting for transfers between devices, per_device(): lax.all_gather(expert_param.astype(jnp.bfloat16), 'edp', axis=1, tiled=True)  47.6 us
  transfers between devices with their start and end apart: 4, of which 4 were waited for; matrix products, arithmetic and copies ran while one was open for 1% of the time, Pallas kernels for 0%

commit v1 on v0

v1 whole, which is shorter than its diff:
```python
import math

import jax
import jax.numpy as jnp
import numpy as np
from jax import lax
from jax.sharding import PartitionSpec as P

STEP = 100
BOTH = ("edp", "ep")
DIMS = (4, 2, 2, 4, 2)
f16, f32, bf16 = jnp.float16, jnp.float32, jnp.bfloat16


def pairs(move):
    out = []
    for src in range(math.prod(DIMS)):
        at = [int(v) for v in np.unravel_index(src, DIMS)]
        out.append((src, int(np.ravel_multi_index(move(*at), DIMS))))
    return out


def along(axis_of_core, k):
    def move(y, zh, c, x, zl):
        axis, z = axis_of_core[c], zh * 2 + zl
        if axis == "x":
            x = (x + k) % 4
        elif axis == "y":
            y = (y + k) % 4
        else:
            z = (z + k) % 4
        return y, z // 2, c, x, z % 2

    return pairs(move)


CORE = pairs(lambda y, zh, c, x, zl: (y, zh, 1 - c, x, zl))
ZHI = pairs(lambda y, zh, c, x, zl: (y, 1 - zh, c, x, zl))
FIRST = [along("xz", k) for k in range(4)]
SECOND = [along("zx", k) for k in range(4)]
YS = [along("yy", k) for k in range(4)]


def send(value, pairing):
    return lax.ppermute(value, BOTH, pairing)


def at(value, index, axis):
    return lax.dynamic_index_in_dim(value, index, axis, keepdims=False)


def ordered(pieces, own):
    ring = [pieces[0], pieces[3], pieces[2], pieces[1]]
    return lax.dynamic_slice_in_dim(jnp.stack(ring + ring), (4 - own) % 4, 4, 0)


def adamw(param, first, second, grad, clip):
    scaled = clip * grad
    first_new = 0.9 * first + 0.1 * scaled
    second_new = 0.95 * second + 0.05 * scaled * scaled
    first_hat = first_new / (1.0 - 0.9**STEP)
    second_hat = second_new / (1.0 - 0.95**STEP)
    param_new = param - 0.001 * (first_hat / (jnp.sqrt(second_hat) + 1e-08) + 0.1 * param)
    return (param_new, first_new, second_new)


def column_term(inputs, cotangent):
    return lax.dot_general(
        inputs, cotangent, (((0,), (0,)), ((), ())), preferred_element_type=jnp.float32
    )


def per_device(
    dense_input,
    dense_cotangent,
    expert_input,
    expert_cotangent,
    dense_master,
    dense_first,
    dense_second,
    expert_master,
    expert_first,
    expert_second,
):
    edp, ep = lax.axis_index("edp"), lax.axis_index("ep")
    y, zh, c, x, zl = edp // 4, (edp // 2) % 2, edp % 2, ep // 2, ep % 2
    z = zh * 2 + zl
    even = c == 0
    b, a = jnp.where(even, x, z), jnp.where(even, z, x)
    kvw, ff = dense_cotangent.shape[1], expert_cotangent.shape[2]
    rows = dense_master.shape[0]
    erows = expert_master.shape[1]

    g = (column_term(dense_input, dense_cotangent) * 0.25).astype(f16)
    g = g.reshape(4, 2, 2, 4, 2, rows, kvw)
    away = send(at(g, 1 - c, 2), CORE)
    q = column_term(expert_input[0], expert_cotangent[0]).astype(f16)
    q = q.reshape(4, 2, 2, erows, ff)
    eaway = send(at(q, 1 - c, 2), CORE)

    h = at(g, c, 2)

    def pick(value, k):
        byx = at(value, (x + k) % 4, 2).reshape(4, 4, rows, kvw)
        zk = (z + k) % 4
        byz = at(at(value, zk // 2, 1), zk % 2, 2)
        return jnp.where(even, byx, byz)

    def first_piece(k):
        return (pick(h, k).astype(f32) + pick(away, k).astype(f32)) * 0.5

    got = [send(first_piece(k).astype(f16), FIRST[k]) for k in (1, 2, 3)]
    qh = at(q, c, 2)

    def efirst_piece(k):
        yk = (y + k) % 4
        return (at(qh, yk, 0).astype(f32) + at(eaway, yk, 0).astype(f32)) * 0.5

    egot = [send(efirst_piece(k).astype(f16), YS[k]) for k in (1, 2, 3)]

    t = (first_piece(0) + sum(v.astype(f32) for v in got)) * 0.25
    got = [send(at(t, (a + k) % 4, 1).astype(f16), SECOND[k]) for k in (1, 2, 3)]
    et = (efirst_piece(0) + sum(v.astype(f32) for v in egot)) * 0.25
    egot = send(at(et, 1 - zh, 0).astype(f16), ZHI)
    u = at(t, a, 1) + sum(v.astype(f32) for v in got)
    got = [send(at(u, (y + k) % 4, 0), YS[k]) for k in (1, 2, 3)]
    expert_grad = ((at(et, zh, 0) + egot.astype(f32)) * 8.0)[None]
    dense_grad = (at(u, y, 0) + sum(got)) * 32.0

    mine = jnp.sum(dense_grad * dense_grad) + jnp.sum(expert_grad * expert_grad)
    spread = lax.all_to_all(jnp.full((128, 1, 128), mine, f32), BOTH, 0, 0, tiled=True)
    total = jnp.sum(spread[:, :, 0])
    ep_size = lax.axis_size("ep")
    limit = 10.0 * math.sqrt(dense_input.shape[1] * (kvw + ep_size * ff))
    clip = jnp.minimum(1.0, limit / (jnp.sqrt(total) + 1e-06))

    dense_param, dense_first_new, dense_second_new = adamw(
        dense_master, dense_first, dense_second, dense_grad, clip
    )
    expert_param, expert_first_new, expert_second_new = adamw(
        expert_master, expert_first, expert_second, expert_grad, clip
    )

    w = dense_param.astype(bf16)
    ew = expert_param.astype(bf16)[0]
    w = ordered([w] + [send(w, YS[k]) for k in (1, 2, 3)], y)
    eo = send(ew, ZHI)
    ew = jnp.where(zh == 0, jnp.stack([ew, eo]), jnp.stack([eo, ew]))
    w = ordered([w] + [send(w, SECOND[k]) for k in (1, 2, 3)], a)
    ew = ordered([ew] + [send(ew, YS[k]) for k in (1, 2, 3)], y)
    w = ordered([w] + [send(w, FIRST[k]) for k in (1, 2, 3)], b)
    eo = send(ew, CORE)
    wo = send(w, CORE)
    ew = jnp.where(even, jnp.stack([ew, eo], 2), jnp.stack([eo, ew], 2))
    w0 = jnp.where(even, w, wo).reshape(4, 2, 2, 4, rows, kvw).transpose(3, 1, 0, 2, 4, 5)
    w1 = jnp.where(even, wo, w).reshape(2, 2, 4, 4, rows, kvw).transpose(3, 0, 2, 1, 4, 5)
    dense_weight = jnp.stack([w0, w1], 2).reshape(-1, kvw)
    expert_weight = ew.reshape(1, -1, ff)
    return (
        dense_param,
        dense_first_new,
        dense_second_new,
        dense_weight,
        expert_param,
        expert_first_new,
        expert_second_new,
        expert_weight,
    )


def solution(mesh):
    placed = (
        P(BOTH, None),
        P(BOTH, None),
        P("ep", "edp", None),
        P("ep", "edp", None),
        P(BOTH, None),
        P(BOTH, None),
        P(BOTH, None),
        P("ep", "edp", None),
        P("ep", "edp", None),
        P("ep", "edp", None),
    )
    return jax.shard_map(
        per_device,
        mesh=mesh,
        in_specs=placed,
        out_specs=(
            P(BOTH, None),
            P(BOTH, None),
            P(BOTH, None),
            P(),
            P("ep", "edp", None),
            P("ep", "edp", None),
            P("ep", "edp", None),
            P("ep", None, None),
        ),
        check_vma=False,
    )
```

time: 1200 us -> 158 us (0.13)
  waiting for transfers between devices: 1070 us -> 46.6 us
  blocking collectives: 77.7 us -> 20.4 us
  starting transfers between devices: 0.16 us -> 33.9 us
  between operations: 15.8 us -> 3.1 us
  other arithmetic: 7.3 us -> 19.3 us
    reduce_scatter x2 -> x0, waiting for transfers between devices: 718 us -> none  [the longest x1 637 us: per_device(): lax.psum_scatter(column_term(dense_input, dense_cotangent), ('edp', 'ep')...]
    all_gather x2 -> x0, waiting for transfers between devices: 355 us -> none  [the longest x1 307 us: per_device(): lax.all_gather(dense_rounded, ('edp', 'ep'), axis=0, tiled=True)]
    psum x1 -> x0, blocking collectives: 77.7 us -> none  [per_device(): lax.psum(jnp.sum(dense_grad * dense_grad) + jnp.sum(expert_grad * expert_...]
    ppermute x0 -> x30, waiting for transfers between devices: none -> 46.6 us  [send(): return lax.ppermute(value, BOTH, pairing)]
    ppermute x0 -> x30, starting transfers between devices: none -> 33.9 us  [send(): return lax.ppermute(value, BOTH, pairing)]
    all_to_all x0 -> x1, blocking collectives: none -> 20.4 us  [per_device(): lax.all_to_all(jnp.full((128, 1, 128), mine, f32), BOTH, 0, 0, tiled=True)]
  transfers between devices with their start and end apart: 4 -> 30, of which waited for: 4 -> 16; matrix products, arithmetic and copies ran while one was open for 1% -> 17% of each run, Pallas kernels for 0% -> 0%
where the time goes in v1:
time: 158 us; the launch traced here: 157 us
  waiting for transfers between devices  46.6 us (29%)
  starting transfers between devices  33.9 us (21%)
  blocking collectives  20.4 us (13%)
  other arithmetic  19.3 us (12%)
  local copies, waits for them, and re-layouts  17.8 us (11%)
  matrix products  16.3 us (10%)
  between operations  3.1 us (2%)
    ppermute x30, waiting for transfers between devices, send(): return lax.ppermute(value, BOTH, pairing)  46.6 us
    ppermute x30, starting transfers between devices, send(): return lax.ppermute(value, BOTH, pairing)  33.9 us
    all_to_all x1, blocking collectives, per_device(): lax.all_to_all(jnp.full((128, 1, 128), mine, f32), BOTH, 0, 0, tiled=True)  20.4 us
    dot_general x2, matrix products, column_term(): lax.dot_general(inputs, cotangent, (((0,), (0,)), ((), ())), preferred_el...  16.3 us
    squeeze x3, local copies, waits for them, and re-layouts, at(): return lax.dynamic_index_in_dim(value, index, axis, keepdims=False)  5.37 us
    unnamed x43, local copies, waits for them, and re-layouts  4.96 us
    dynamic_slice x2, local copies, waits for them, and re-layouts, at(): return lax.dynamic_index_in_dim(value, index, axis, keepdims=False)  4.45 us
    convert_element_type x1, other arithmetic, per_device(): got = [send(first_piece(k).astype(f16), FIRST[k]) for k in (1, 2, 3)]  3.9 us
  transfers between devices with their start and end apart: 30, of which 16 were waited for; matrix products, arithmetic and copies ran while one was open for 17% of the time, Pallas kernels for 0%

profile of v1, /device:TPU:1, one launch (start us, length us, event | category | flops | bytes accessed | tf_op | source)
XLA Modules:
  0.0 157.4 jit_solution(17221564751648995271)
XLA Ops:
  2.5 11.1 %multiply_convert_fusion = f16[2048,1024]{1,0:T(8,128)(2,1)} fusion(bf16[1536,2048]{1,0:T(8,128)(2,1)} %param.10, bf16[1536,1024]{1,0:T(8,128)(2,1)S(1)} %copy-done), kind=kOutput, calls=%fused_computation | convolution fusion | flops 6446645248 | bytes 13631488 | tf_op jit(solution)/shard_map/dot_general | solution.py:68
  13.6 3.9 %dynamic-slice_bitcast_fusion = f16[4,2,4,2,16,1024]{5,4,3,2,1,0:T(8,128)(2,1)} fusion(f16[4,2,2,4,2,16,1024]{6,5,4,3,2,1,0:T(8,128)(2,1)} %bitcast.217, s32[]{:T(128)S(6)} %select_n.420), kind=kLoop, calls=%fused_computation.8 | loop fusion | bytes 4194308 | tf_op jit(solution)/shard_map/jit(dynamic_index_in_dim)/squeeze | solution.py:49
  18.9 5.2 %fusion.2 = f16[2048,768]{1,0:T(8,128)(2,1)S(1)} fusion(bf16[1,1024,2048]{2,1,0:T(8,128)(2,1)S(1)} %copy-done.8, bf16[1,1024,768]{2,1,0:T(8,128)(2,1)} %param.13), kind=kOutput, calls=%fused_computation.4 | convolution fusion | flops 3222798336 | bytes 8912896 | tf_op jit(solution)/shard_map/dot_general | solution.py:68
  27.2 3.0 %constant_dynamic-slice_fusion.11 = (f16[4,2,1,1,2,16,1024]{6,5,4,3,2,1,0:T(8,128)(2,1)}, f16[4,2,1,1,2,16,1024]{6,5,4,3,2,1,0:T(8,128)(2,1)S(1)}, f16[4,2,1,1,2...) fusion(f16[4,2,2,4,2,16,1024]{6,5,4,3,2,1,0:T(8,128)(2,1)} %bitcast.218, s32[]{:T(128)S(6)} %select_n.404, ...), kind=kLoop, calls=%fused_computation.109 | loop fusion | bytes 4194324 | tf_op jit(solution)/shard_map/jit(dynamic_index_in_dim)/dynamic_slice | solution.py:49
  31.7 3.9 %multiply_convert_fusion.3 = (f16[4,4,16,1024]{3,2,1,0:T(8,128)(2,1)}, f16[4,4,16,1024]{3,2,1,0:T(8,128)(2,1)}, f16[4,4,16,1024]{3,2,1,0:T(8,128)(2,1)}) fusion(f16[4,4,16,1024]{3,2,1,0:T(8,128)(2,1)S(1)} %bitcast.236, f16[4,4,16,1024]{3,2,1,0:T(8,128)(2,1)S(1)} %bitcast.240, f16[4,2,4,2,16,1024]{5,4,3,2,1,0:T(8,128)(2,1)S(1)} %collective-permute-done, ...), kind=kLoop, calls=%fused_computation.16 | loop fusion | flops 5505024 | bytes 7864349 | tf_op jit(solution)/shard_map/convert_element_type | solution.py:112
  35.6 3.8 %collective-permute-start.3 = (f16[4,4,16,1024]{3,2,1,0:T(8,128)(2,1)}, f16[4,4,16,1024]{3,2,1,0:T(8,128)(2,1)S(1)}, u32[]{:S(2)}, u32[]{:S(2)}) collective-permute-start(f16[4,4,16,1024]{3,2,1,0:T(8,128)(2,1)} %get-tuple-element.24), channel_id=1, source_target_pairs={{0,6},{1,7},{2,0},{3,1},{4,2},{5,3},{6,4},{7,5},{8,25},{9,8},{10,2... | collective-permute-start | bytes 1572872 | tf_op jit(solution)/shard_map/ppermute | solution.py:45
  40.1 2.0 %fusion.11 = (f16[2,128,768]{2,1,0:T(8,128)(2,1)S(1)}, f16[2,128,768]{2,1,0:T(8,128)(2,1)S(1)}, f16[2,128,768]{2,1,0:T(8,128)(2,1)S(1)}) fusion(f16[4,2,128,768]{3,2,1,0:T(8,128)(2,1)} %collective-permute-done.10, s32[]{:T(128)S(6)} %select_n.469, f16[4,2,2,128,768]{4,3,2,1,0:T(8,128)(2,1)} %bitcast.231, s32[]{:T(128)S(6)} %select_n.477, s32[]{:T(128)S(6)} %select_n.404, ...), kind=kLoop, calls=%fused_computation.25 | loop fusion | flops 2949120 | bytes 3538972 | tf_op jit(solution)/shard_map/convert_element_type | solution.py:119
  42.2 3.0 %collective-permute-start.13 = (f16[2,128,768]{2,1,0:T(8,128)(2,1)S(1)}, f16[2,128,768]{2,1,0:T(8,128)(2,1)S(1)}, u32[]{:S(2)}, u32[]{:S(2)}) collective-permute-start(f16[2,128,768]{2,1,0:T(8,128)(2,1)S(1)} %get-tuple-element.27), channel_id=1, source_target_pairs={{0,96},{1,97},{2,98},{3,99},{4,100},{5,101},{6,102},{7,103},{8,104... | collective-permute-start | bytes 1179656 | tf_op jit(solution)/shard_map/ppermute | solution.py:45
  45.5 6.0 %collective-permute-done.3 = f16[4,4,16,1024]{3,2,1,0:T(8,128)(2,1)S(1)} collective-permute-done((f16[4,4,16,1024]{3,2,1,0:T(8,128)(2,1)}, f16[4,4,16,1024]{3,2,1,0:T(8,128)(2,1)S(1)}, u32[]{:S(2)}, u32[]{:S(2)}) %collective-permute-start.3) | collective-permute-done | bytes 524320 | tf_op jit(solution)/shard_map/ppermute | solution.py:45
  52.8 2.1 %collective-permute-done.1 = f16[4,4,16,1024]{3,2,1,0:T(8,128)(2,1)} collective-permute-done((f16[4,4,16,1024]{3,2,1,0:T(8,128)(2,1)}, f16[4,4,16,1024]{3,2,1,0:T(8,128)(2,1)}, u32[]{:S(2)}, u32[]{:S(2)}) %collective-permute-start.1) | collective-permute-done | bytes 524320 | tf_op jit(solution)/shard_map/ppermute | solution.py:45
  54.9 2.4 %add_multiply_fusion = f32[4,4,16,1024]{3,2,1,0:T(8,128)S(1)} fusion(f16[4,4,16,1024]{3,2,1,0:T(8,128)(2,1)} %copy-done.3, f16[4,4,16,1024]{3,2,1,0:T(8,128)(2,1)} %copy-done.4, f16[4,4,16,1024]{3,2,1,0:T(8,128)(2,1)} %collective-permute-done.1, f16[4,4,16,1024]{3,2,1,0:T(8,128)(2,1)} %bitcast.233, f16[4,4,16,1024]{3,2,1,0:T(8,128)(2,1)} %bitcast.234, ...), kind=kLoop, calls=%fused_computation.13 | loop fusion | flops 3407872 | bytes 4718605 | tf_op jit(solution)/shard_map/mul | solution.py:121
  57.4 2.4 %collective-permute-start.6 = (f16[4,16,1024]{2,1,0:T(8,128)(2,1)S(1)}, f16[4,16,1024]{2,1,0:T(8,128)(2,1)S(1)}, u32[]{:S(2)}, u32[]{:S(2)}) collective-permute-start(f16[4,16,1024]{2,1,0:T(8,128)(2,1)S(1)} %get-tuple-element.40), channel_id=1, source_target_pairs={{0,17},{1,0},{2,19},{3,2},{4,21},{5,4},{6,23},{7,6},{8,14},{9,15},... | collective-permute-start | bytes 393224 | tf_op jit(solution)/shard_map/ppermute | solution.py:45
  61.5 4.7 %collective-permute-done.11 = f16[2,128,768]{2,1,0:T(8,128)(2,1)S(1)} collective-permute-done((f16[2,128,768]{2,1,0:T(8,128)(2,1)S(1)}, f16[2,128,768]{2,1,0:T(8,128)(2,1)S(1)}, u32[]{:S(2)}, u32[]{:S(2)}) %collective-permute-start.11) | collective-permute-done | bytes 393248 | tf_op jit(solution)/shard_map/ppermute | solution.py:45
  72.0 3.3 %collective-permute-done.14 = f16[128,768]{1,0:T(8,128)(2,1)S(1)} collective-permute-done((f16[128,768]{1,0:T(8,128)(2,1)S(1)}, f16[128,768]{1,0:T(8,128)(2,1)S(1)}, u32[]{:S(2)}, u32[]{:S(2)}) %collective-permute-start.14) | collective-permute-done | bytes 196640 | tf_op jit(solution)/shard_map/ppermute | solution.py:45
  78.1 20.4 %all_to_all.5 = f32[128,1,128]{2,1,0:T(1,128)S(1)} all-to-all(f32[128,1,128]{2,1,0:T(1,128)S(1)} %broadcast_in_dim.4), channel_id=1, replica_groups=mesh['edp'=16,'ep'=8] {'edp','ep'}, dimensions={0} | all-to-all | bytes 131072 | tf_op jit(solution)/shard_map/all_to_all | solution.py:131
  104.3 2.3 %collective-permute-done.16 = bf16[16,1024]{1,0:T(8,128)(2,1)S(1)} collective-permute-done((bf16[16,1024]{1,0:T(8,128)(2,1)S(1)}, bf16[16,1024]{1,0:T(8,128)(2,1)S(1)}, u32[]{:S(2)}, u32[]{:S(2)}) %collective-permute-start.16) | collective-permute-done | bytes 32800 | tf_op jit(solution)/shard_map/ppermute | solution.py:45
  108.3 2.3 %fusion.22 = (bf16[1,128,768]{2,1,0:T(8,128)(2,1)S(1)}, f32[1,128,768]{2,1,0:T(8,128)}, f32[1,128,768]{2,1,0:T(8,128)}, f32[1,128,768]{2,1,0:T(8,128)}) fusion(f32[1,128,768]{2,1,0:T(8,128)S(1)} %copy-done.5, f32[]{:T(128)S(6)} %mul.191, f16[128,768]{1,0:T(8,128)(2,1)S(1)} %collective-permute-done.14, f32[2,128,768]{2,1,0:T(8,128)S(1)} %fusion.14, ...), kind=kLoop, calls=%fused_computation.110 | loop fusion | flops 1867776 | bytes 3145736 | tf_op jit(solution)/shard_map/convert_element_type | solution.py:145
  113.7 3.6 %collective-permute-done.19 = bf16[4,16,1024]{2,1,0:T(8,128)(2,1)S(1)} collective-permute-done((bf16[4,16,1024]{2,1,0:T(8,128)(2,1)S(1)}, bf16[4,16,1024]{2,1,0:T(8,128)(2,1)S(1)}, u32[]{:S(2)}, u32[]{:S(2)}) %collective-permute-start.19) | collective-permute-done | bytes 131104 | tf_op jit(solution)/shard_map/ppermute | solution.py:45
  123.5 2.3 %collective-permute-done.26 = bf16[2,128,768]{2,1,0:T(8,128)(2,1)S(1)} collective-permute-done((bf16[2,128,768]{2,1,0:T(8,128)(2,1)S(1)}, bf16[2,128,768]{2,1,0:T(8,128)(2,1)S(1)}, u32[]{:S(2)}, u32[]{:S(2)}) %collective-permute-start.26) | collective-permute-done | bytes 393248 | tf_op jit(solution)/shard_map/ppermute | solution.py:45
  125.9 2.4 %collective-permute-done.27 = bf16[2,128,768]{2,1,0:T(8,128)(2,1)S(1)} collective-permute-done((bf16[2,128,768]{2,1,0:T(8,128)(2,1)S(1)}, bf16[2,128,768]{2,1,0:T(8,128)(2,1)S(1)}, u32[]{:S(2)}, u32[]{:S(2)}) %collective-permute-start.27) | collective-permute-done | bytes 393248 | tf_op jit(solution)/shard_map/ppermute | solution.py:45
  128.3 9.2 %collective-permute-done.28 = bf16[2,128,768]{2,1,0:T(8,128)(2,1)S(1)} collective-permute-done((bf16[2,128,768]{2,1,0:T(8,128)(2,1)S(1)}, bf16[2,128,768]{2,1,0:T(8,128)(2,1)S(1)}, u32[]{:S(2)}, u32[]{:S(2)}) %collective-permute-start.28) | collective-permute-done | bytes 393248 | tf_op jit(solution)/shard_map/ppermute | solution.py:45
  138.5 6.3 %collective-permute-start.24 = (bf16[4,4,4,16,1024]{4,3,2,1,0:T(8,128)(2,1)S(1)}, bf16[4,4,4,16,1024]{4,3,2,1,0:T(8,128)(2,1)S(1)}, u32[]{:S(2)}, u32[]{:S(2)}) collective-permute-start(bf16[4,4,4,16,1024]{4,3,2,1,0:T(8,128)(2,1)S(1)} %constant_dynamic-slice_fusion.8), channel_id=1, source_target_pairs={{0,8},{1,9},{2,10},{3,11},{4,12},{5,13},{6,14},{7,15},{8,0},{9,1},... | collective-permute-start | bytes 6291464 | tf_op jit(solution)/shard_map/ppermute | solution.py:45
  145.1 5.7 %collective-permute-done.29 = bf16[4,2,128,768]{3,2,1,0:T(8,128)(2,1)S(1)} collective-permute-done((bf16[4,2,128,768]{3,2,1,0:T(8,128)(2,1)S(1)}, bf16[4,2,128,768]{3,2,1,0:T(8,128)(2,1)S(1)}, u32[]{:S(2)}, u32[]{:S(2)}) %collective-permute-start.29) | collective-permute-done | bytes 1572896 | tf_op jit(solution)/shard_map/ppermute | solution.py:45
  154.1 2.4 %pad_maximum_fusion = bf16[4,2,2,4,2,16,1024]{6,5,4,3,2,1,0:T(8,128)(2,1)} fusion(bf16[4,2,1,4,2,16,1024]{6,5,4,3,2,1,0:T(8,128)(2,1)S(1)} %bitcast.223, bf16[4,2,1,4,2,16,1024]{6,5,4,3,2,1,0:T(8,128)(2,1)S(1)} %bitcast.224), kind=kLoop, calls=%fused_computation.1 | loop fusion | flops 2097152 | bytes 8388608 | tf_op jit(solution)/shard_map/stack | solution.py:157
  (116 shorter events, 40.6 us)
Async XLA Ops:
  17.5 12.8 %collective-permute-start = (f16[4,2,4,2,16,1024]{5,4,3,2,1,0:T(8,128)(2,1)}, f16[4,2,4,2,16,1024]{5,4,3,2,1,0:T(8,128)(2,1)S(1)}, u32[]{:S(2)}, u32[]{:S(2)}) collective-permute-start(f16[4,2,4,2,16,1024]{5,4,3,2,1,0:T(8,128)(2,1)} %dynamic-slice_bitcast_fusion), channel_id=1, source_target_pairs={{0,8},{1,9},{2,10},{3,11},{4,12},{5,13},{6,14},{7,15},{8,0},{9,1},... | collective-permute-start | bytes 6291464 | tf_op jit(solution)/shard_map/ppermute | solution.py:45
  27.2 12.9 %collective-permute-start.10 = (f16[4,2,128,768]{3,2,1,0:T(8,128)(2,1)}, f16[4,2,128,768]{3,2,1,0:T(8,128)(2,1)}, u32[]{:S(2)}, u32[]{:S(2)}) collective-permute-start(f16[4,2,128,768]{3,2,1,0:T(8,128)(2,1)} %dynamic-slice_bitcast_fusion.1), channel_id=1, source_target_pairs={{0,8},{1,9},{2,10},{3,11},{4,12},{5,13},{6,14},{7,15},{8,0},{9,1},... | collective-permute-start | bytes 4718600 | tf_op jit(solution)/shard_map/ppermute | solution.py:45
  35.6 15.9 %collective-permute-start.3 = (f16[4,4,16,1024]{3,2,1,0:T(8,128)(2,1)}, f16[4,4,16,1024]{3,2,1,0:T(8,128)(2,1)S(1)}, u32[]{:S(2)}, u32[]{:S(2)}) collective-permute-start(f16[4,4,16,1024]{3,2,1,0:T(8,128)(2,1)} %get-tuple-element.24), channel_id=1, source_target_pairs={{0,6},{1,7},{2,0},{3,1},{4,2},{5,3},{6,4},{7,5},{8,25},{9,8},{10,2... | collective-permute-start | bytes 1572872 | tf_op jit(solution)/shard_map/ppermute | solution.py:45
  39.4 13.4 %collective-permute-start.2 = (f16[4,4,16,1024]{3,2,1,0:T(8,128)(2,1)}, f16[4,4,16,1024]{3,2,1,0:T(8,128)(2,1)S(1)}, u32[]{:S(2)}, u32[]{:S(2)}) collective-permute-start(f16[4,4,16,1024]{3,2,1,0:T(8,128)(2,1)} %get-tuple-element.25), channel_id=1, source_target_pairs={{0,4},{1,5},{2,6},{3,7},{4,0},{5,1},{6,2},{7,3},{8,24},{9,25},{10,... | collective-permute-start | bytes 1572872 | tf_op jit(solution)/shard_map/ppermute | solution.py:45
  39.4 15.5 %collective-permute-start.1 = (f16[4,4,16,1024]{3,2,1,0:T(8,128)(2,1)}, f16[4,4,16,1024]{3,2,1,0:T(8,128)(2,1)}, u32[]{:S(2)}, u32[]{:S(2)}) collective-permute-start(f16[4,4,16,1024]{3,2,1,0:T(8,128)(2,1)} %get-tuple-element.23), channel_id=1, source_target_pairs={{0,2},{1,3},{2,4},{3,5},{4,6},{5,7},{6,0},{7,1},{8,9},{9,24},{10,1... | collective-permute-start | bytes 1572872 | tf_op jit(solution)/shard_map/ppermute | solution.py:45
  42.2 19.3 %collective-permute-start.13 = (f16[2,128,768]{2,1,0:T(8,128)(2,1)S(1)}, f16[2,128,768]{2,1,0:T(8,128)(2,1)S(1)}, u32[]{:S(2)}, u32[]{:S(2)}) collective-permute-start(f16[2,128,768]{2,1,0:T(8,128)(2,1)S(1)} %get-tuple-element.27), channel_id=1, source_target_pairs={{0,96},{1,97},{2,98},{3,99},{4,100},{5,101},{6,102},{7,103},{8,104... | collective-permute-start | bytes 1179656 | tf_op jit(solution)/shard_map/ppermute | solution.py:45
  45.2 16.3 %collective-permute-start.12 = (f16[2,128,768]{2,1,0:T(8,128)(2,1)S(1)}, f16[2,128,768]{2,1,0:T(8,128)(2,1)S(1)}, u32[]{:S(2)}, u32[]{:S(2)}) collective-permute-start(f16[2,128,768]{2,1,0:T(8,128)(2,1)S(1)} %get-tuple-element.28), channel_id=1, source_target_pairs={{0,64},{1,65},{2,66},{3,67},{4,68},{5,69},{6,70},{7,71},{8,72},{9,... | collective-permute-start | bytes 1179656 | tf_op jit(solution)/shard_map/ppermute | solution.py:45
  51.5 14.7 %collective-permute-start.11 = (f16[2,128,768]{2,1,0:T(8,128)(2,1)S(1)}, f16[2,128,768]{2,1,0:T(8,128)(2,1)S(1)}, u32[]{:S(2)}, u32[]{:S(2)}) collective-permute-start(f16[2,128,768]{2,1,0:T(8,128)(2,1)S(1)} %get-tuple-element.26), channel_id=1, source_target_pairs={{0,32},{1,33},{2,34},{3,35},{4,36},{5,37},{6,38},{7,39},{8,40},{9,... | collective-permute-start | bytes 1179656 | tf_op jit(solution)/shard_map/ppermute | solution.py:45
  57.4 11.5 %collective-permute-start.6 = (f16[4,16,1024]{2,1,0:T(8,128)(2,1)S(1)}, f16[4,16,1024]{2,1,0:T(8,128)(2,1)S(1)}, u32[]{:S(2)}, u32[]{:S(2)}) collective-permute-start(f16[4,16,1024]{2,1,0:T(8,128)(2,1)S(1)} %get-tuple-element.40), channel_id=1, source_target_pairs={{0,17},{1,0},{2,19},{3,2},{4,21},{5,4},{6,23},{7,6},{8,14},{9,15},... | collective-permute-start | bytes 393224 | tf_op jit(solution)/shard_map/ppermute | solution.py:45
  59.9 9.1 %collective-permute-start.5 = (f16[4,16,1024]{2,1,0:T(8,128)(2,1)S(1)}, f16[4,16,1024]{2,1,0:T(8,128)(2,1)S(1)}, u32[]{:S(2)}, u32[]{:S(2)}) collective-permute-start(f16[4,16,1024]{2,1,0:T(8,128)(2,1)S(1)} %get-tuple-element.41), channel_id=1, source_target_pairs={{0,16},{1,17},{2,18},{3,19},{4,20},{5,21},{6,22},{7,23},{8,12},{9,... | collective-permute-start | bytes 393224 | tf_op jit(solution)/shard_map/ppermute | solution.py:45
  61.5 7.5 %collective-permute-start.4 = (f16[4,16,1024]{2,1,0:T(8,128)(2,1)S(1)}, f16[4,16,1024]{2,1,0:T(8,128)(2,1)S(1)}, u32[]{:S(2)}, u32[]{:S(2)}) collective-permute-start(f16[4,16,1024]{2,1,0:T(8,128)(2,1)S(1)} %get-tuple-element.39), channel_id=1, source_target_pairs={{0,1},{1,16},{2,3},{3,18},{4,5},{5,20},{6,7},{7,22},{8,10},{9,11},... | collective-permute-start | bytes 393224 | tf_op jit(solution)/shard_map/ppermute | solution.py:45
  67.7 7.6 %collective-permute-start.14 = (f16[128,768]{1,0:T(8,128)(2,1)S(1)}, f16[128,768]{1,0:T(8,128)(2,1)S(1)}, u32[]{:S(2)}, u32[]{:S(2)}) collective-permute-start(f16[128,768]{1,0:T(8,128)(2,1)S(1)} %fusion.17), channel_id=1, source_target_pairs={{0,16},{1,17},{2,18},{3,19},{4,20},{5,21},{6,22},{7,23},{8,24},{9,... | collective-permute-start | bytes 589832 | tf_op jit(solution)/shard_map/ppermute | solution.py:45
  69.1 6.9 %collective-permute-start.9 = (f32[16,1024]{1,0:T(8,128)S(1)}, f32[16,1024]{1,0:T(8,128)S(1)}, u32[]{:S(2)}, u32[]{:S(2)}) collective-permute-start(f32[16,1024]{1,0:T(8,128)S(1)} %get-tuple-element.43), channel_id=1, source_target_pairs={{0,96},{1,97},{2,98},{3,99},{4,100},{5,101},{6,102},{7,103},{8,104... | collective-permute-start | bytes 196616 | tf_op jit(solution)/shard_map/ppermute | solution.py:45
  70.8 5.3 %collective-permute-start.7 = (f32[16,1024]{1,0:T(8,128)S(1)}, f32[16,1024]{1,0:T(8,128)S(1)}, u32[]{:S(2)}, u32[]{:S(2)}) collective-permute-start(f32[16,1024]{1,0:T(8,128)S(1)} %get-tuple-element.44), channel_id=1, source_target_pairs={{0,32},{1,33},{2,34},{3,35},{4,36},{5,37},{6,38},{7,39},{8,40},{9,... | collective-permute-start | bytes 196616 | tf_op jit(solution)/shard_map/ppermute | solution.py:45
  108.0 5.7 %collective-permute-start.18 = (bf16[4,16,1024]{2,1,0:T(8,128)(2,1)S(1)}, bf16[4,16,1024]{2,1,0:T(8,128)(2,1)S(1)}, u32[]{:S(2)}, u32[]{:S(2)}) collective-permute-start(bf16[4,16,1024]{2,1,0:T(8,128)(2,1)S(1)} %get-tuple-element.15), channel_id=1, source_target_pairs={{0,17},{1,0},{2,19},{3,2},{4,21},{5,4},{6,23},{7,6},{8,14},{9,15},... | collective-permute-start | bytes 393224 | tf_op jit(solution)/shard_map/ppermute | solution.py:45
  110.6 8.4 %collective-permute-start.25 = (bf16[128,768]{1,0:T(8,128)(2,1)S(1)}, bf16[128,768]{1,0:T(8,128)(2,1)S(1)}, u32[]{:S(2)}, u32[]{:S(2)}) collective-permute-start(bf16[128,768]{1,0:T(8,128)(2,1)S(1)} %bitcast.227), channel_id=1, source_target_pairs={{0,16},{1,17},{2,18},{3,19},{4,20},{5,21},{6,22},{7,23},{8,24},{9,... | collective-permute-start | bytes 589832 | tf_op jit(solution)/shard_map/ppermute | solution.py:45
  119.1 6.7 %collective-permute-start.26 = (bf16[2,128,768]{2,1,0:T(8,128)(2,1)S(1)}, bf16[2,128,768]{2,1,0:T(8,128)(2,1)S(1)}, u32[]{:S(2)}, u32[]{:S(2)}) collective-permute-start(bf16[2,128,768]{2,1,0:T(8,128)(2,1)S(1)} %maximum_select_fusion.2), channel_id=1, source_target_pairs={{0,96},{1,97},{2,98},{3,99},{4,100},{5,101},{6,102},{7,103},{8,104... | collective-permute-start | bytes 1179656 | tf_op jit(solution)/shard_map/ppermute | solution.py:45
  120.0 8.2 %collective-permute-start.27 = (bf16[2,128,768]{2,1,0:T(8,128)(2,1)S(1)}, bf16[2,128,768]{2,1,0:T(8,128)(2,1)S(1)}, u32[]{:S(2)}, u32[]{:S(2)}) collective-permute-start(bf16[2,128,768]{2,1,0:T(8,128)(2,1)S(1)} %maximum_select_fusion.2), channel_id=1, source_target_pairs={{0,64},{1,65},{2,66},{3,67},{4,68},{5,69},{6,70},{7,71},{8,72},{9,... | collective-permute-start | bytes 1179656 | tf_op jit(solution)/shard_map/ppermute | solution.py:45
  120.8 16.9 %collective-permute-start.21 = (bf16[4,4,16,1024]{3,2,1,0:T(8,128)(2,1)S(1)}, bf16[4,4,16,1024]{3,2,1,0:T(8,128)(2,1)S(1)}, u32[]{:S(2)}, u32[]{:S(2)}) collective-permute-start(bf16[4,4,16,1024]{3,2,1,0:T(8,128)(2,1)S(1)} %get-tuple-element.13), channel_id=1, source_target_pairs={{0,6},{1,7},{2,0},{3,1},{4,2},{5,3},{6,4},{7,5},{8,25},{9,8},{10,2... | collective-permute-start | bytes 1572872 | tf_op jit(solution)/shard_map/ppermute | solution.py:45
  122.7 15.0 %collective-permute-start.22 = (bf16[4,4,16,1024]{3,2,1,0:T(8,128)(2,1)S(1)}, bf16[4,4,16,1024]{3,2,1,0:T(8,128)(2,1)S(1)}, u32[]{:S(2)}, u32[]{:S(2)}) collective-permute-start(bf16[4,4,16,1024]{3,2,1,0:T(8,128)(2,1)S(1)} %get-tuple-element.13), channel_id=1, source_target_pairs={{0,4},{1,5},{2,6},{3,7},{4,0},{5,1},{6,2},{7,3},{8,24},{9,25},{10,... | collective-permute-start | bytes 1572872 | tf_op jit(solution)/shard_map/ppermute | solution.py:45
  122.9 15.2 %collective-permute-start.23 = (bf16[4,4,16,1024]{3,2,1,0:T(8,128)(2,1)S(1)}, bf16[4,4,16,1024]{3,2,1,0:T(8,128)(2,1)S(1)}, u32[]{:S(2)}, u32[]{:S(2)}) collective-permute-start(bf16[4,4,16,1024]{3,2,1,0:T(8,128)(2,1)S(1)} %get-tuple-element.13), channel_id=1, source_target_pairs={{0,2},{1,3},{2,4},{3,5},{4,6},{5,7},{6,0},{7,1},{8,9},{9,24},{10,1... | collective-permute-start | bytes 1572872 | tf_op jit(solution)/shard_map/ppermute | solution.py:45
  125.8 11.6 %collective-permute-start.28 = (bf16[2,128,768]{2,1,0:T(8,128)(2,1)S(1)}, bf16[2,128,768]{2,1,0:T(8,128)(2,1)S(1)}, u32[]{:S(2)}, u32[]{:S(2)}) collective-permute-start(bf16[2,128,768]{2,1,0:T(8,128)(2,1)S(1)} %maximum_select_fusion.2), channel_id=1, source_target_pairs={{0,32},{1,33},{2,34},{3,35},{4,36},{5,37},{6,38},{7,39},{8,40},{9,... | collective-permute-start | bytes 1179656 | tf_op jit(solution)/shard_map/ppermute | solution.py:45
  138.5 14.7 %collective-permute-start.24 = (bf16[4,4,4,16,1024]{4,3,2,1,0:T(8,128)(2,1)S(1)}, bf16[4,4,4,16,1024]{4,3,2,1,0:T(8,128)(2,1)S(1)}, u32[]{:S(2)}, u32[]{:S(2)}) collective-permute-start(bf16[4,4,4,16,1024]{4,3,2,1,0:T(8,128)(2,1)S(1)} %constant_dynamic-slice_fusion.8), channel_id=1, source_target_pairs={{0,8},{1,9},{2,10},{3,11},{4,12},{5,13},{6,14},{7,15},{8,0},{9,1},... | collective-permute-start | bytes 6291464 | tf_op jit(solution)/shard_map/ppermute | solution.py:45
  144.9 5.9 %collective-permute-start.29 = (bf16[4,2,128,768]{3,2,1,0:T(8,128)(2,1)S(1)}, bf16[4,2,128,768]{3,2,1,0:T(8,128)(2,1)S(1)}, u32[]{:S(2)}, u32[]{:S(2)}) collective-permute-start(bf16[4,2,128,768]{3,2,1,0:T(8,128)(2,1)S(1)} %constant_dynamic-slice_fusion.3), channel_id=1, source_target_pairs={{0,8},{1,9},{2,10},{3,11},{4,12},{5,13},{6,14},{7,15},{8,0},{9,1},... | collective-permute-start | bytes 4718600 | tf_op jit(solution)/shard_map/ppermute | solution.py:45
  (15 other events, 176.9 us)

commit v2 on v1

v2 whole, which is shorter than its diff:
```python
import functools
import math

import jax
import jax.numpy as jnp
import numpy as np
from jax import lax
from jax.experimental import pallas as pl
from jax.experimental.pallas import tpu as pltpu
from jax.sharding import PartitionSpec as P

STEP = 100
VMEM = 24 * 1024 * 1024
BOTH = ("edp", "ep")
DIMS = (4, 2, 2, 4, 2)
LIGHT = pl.CostEstimate(flops=1, bytes_accessed=1, transcendentals=0)
f16, f32, bf16 = jnp.float16, jnp.float32, jnp.bfloat16


def pairs(move):
    out = []
    for src in range(math.prod(DIMS)):
        at = [int(v) for v in np.unravel_index(src, DIMS)]
        out.append((src, int(np.ravel_multi_index(move(*at), DIMS))))
    return out


def along(axis_of_core, k):
    def move(y, zh, c, x, zl):
        axis, z = axis_of_core[c], zh * 2 + zl
        if axis == "x":
            x = (x + k) % 4
        elif axis == "y":
            y = (y + k) % 4
        else:
            z = (z + k) % 4
        return y, z // 2, c, x, z % 2

    return pairs(move)


CORE = pairs(lambda y, zh, c, x, zl: (y, zh, 1 - c, x, zl))
ZHI = pairs(lambda y, zh, c, x, zl: (y, 1 - zh, c, x, zl))
FIRST = [along("xz", k) for k in range(4)]
SECOND = [along("zx", k) for k in range(4)]
YS = [along("yy", k) for k in range(4)]


def send(value, pairing):
    return lax.ppermute(value, BOTH, pairing)


def after(values, event):
    return lax.optimization_barrier((values, event))[0]


def ahead(own, received):
    return jnp.stack([own, received[2], received[1], received[0]])


def in_order(own, received, at):
    pieces = [own, *received]
    out = []
    for m in range(4):
        away = (at - m + 4) % 4
        out.append(jnp.where(away == 0, pieces[0], jnp.where(away == 1, pieces[1], jnp.where(away == 2, pieces[2], pieces[3]))))
    return jnp.stack(out)


def ring(value, pairings):
    return ahead(value, [send(value, p) for p in pairings[1:]])


def relative(pos, core, y, zh, x, zl):
    dx, dz, dy = (x - pos[3]) % 4, (zh * 2 + zl - pos[4]) % 4, (y - pos[0]) % 4
    even = core == 0
    return jnp.where(even, dx, dz), jnp.where(even, dz, dx), dy


def half_kernel(store, other, pos, inputs, cotangent, out, columns, held, sems):
    step = pl.program_id(0)
    core = (pos[2] + other) % 2
    width = columns.shape[2]

    def load(block):
        start = pl.multiple_of((2 * block + core) * width, width)
        return pltpu.make_async_copy(
            inputs.at[:, pl.ds(start, width)], columns.at[block], sems.at[block]
        )

    whole = pltpu.make_async_copy(cotangent, held, sems.at[8])

    @pl.when(step == 0)
    def _():
        whole.start()
        for block in range(8):
            load(block).start()
        whole.wait()

    for half in range(2):
        load(2 * step + half).wait()
    terms = column_term(
        jnp.concatenate([columns[2 * step], columns[2 * step + 1]], axis=1), held[...]
    )
    store(pos, core, step, terms, out)


def store_dense(pos, core, step, terms, out):
    rows = out.shape[3]
    for block in range(16):
        zh, x, zl = block // 8, block // 2 % 4, block % 2
        first, second, _ = relative(pos, core, step, zh, x, zl)
        out[first, second, 0] = terms[block * rows : (block + 1) * rows]


def store_expert(pos, core, step, terms, out):
    rows = out.shape[2]
    for zh in range(2):
        out[0, (zh + pos[1]) % 2] = terms[zh * rows : (zh + 1) * rows]


def half_terms(store, other, pos, inputs, cotangent, shape, block, at, name, vmem):
    depth, width = inputs.shape
    hbm = pl.BlockSpec(memory_space=pltpu.MemorySpace.HBM)
    return pl.pallas_call(
        functools.partial(half_kernel, store, other),
        out_shape=jax.ShapeDtypeStruct(shape, f32),
        grid_spec=pltpu.PrefetchScalarGridSpec(
            num_scalar_prefetch=1,
            grid=(4,),
            in_specs=[hbm, hbm],
            out_specs=pl.BlockSpec(block, at),
            scratch_shapes=[
                pltpu.VMEM((8, depth, width // 16), bf16),
                pltpu.VMEM(cotangent.shape, bf16),
                pltpu.SemaphoreType.DMA((9,)),
            ],
        ),
        compiler_params=pltpu.CompilerParams(vmem_limit_bytes=vmem),
        cost_estimate=pl.CostEstimate(
            flops=2 * depth * width * cotangent.shape[1], bytes_accessed=1, transcendentals=0
        ),
        name=name,
    )(pos, inputs, cotangent)


def dense_half(other, pos, inputs, cotangent):
    rows, kvw = inputs.shape[1] // 128, cotangent.shape[1]
    return half_terms(
        store_dense, other, pos, inputs, cotangent,
        (4, 4, 4, rows, kvw), (4, 4, 1, rows, kvw),
        lambda step, pos: (0, 0, (step - pos[0] + 4) % 4, 0, 0), "dense_terms",
        VMEM,
    )


def expert_half(other, pos, inputs, cotangent):
    rows, ff = inputs.shape[1] // 16, cotangent.shape[1]
    return half_terms(
        store_expert, other, pos, inputs, cotangent,
        (4, 2, rows, ff), (1, 2, rows, ff),
        lambda step, pos: ((step - pos[0] + 4) % 4, 0, 0, 0), "expert_terms",
        VMEM,
    )


def place_kernel(names, pos, *refs):
    pieces, (dense_out, expert_out, sems) = refs[: len(names)], refs[-3:]
    copies = []
    for (kind, other, first), piece in zip(names, pieces):
        core = (pos[2] + other) % 2
        even = core == 0
        if kind == "expert":
            for dy in range(4):
                for dz in range(2):
                    block = ((pos[0] + dy) % 4 * 2 + (pos[1] + dz) % 2) * 2 + core
                    copies.append((piece.at[dy, dz], expert_out.at[block]))
        else:
            for second in range(4):
                x = (pos[3] + jnp.where(even, first, second)) % 4
                z = (pos[4] + jnp.where(even, second, first)) % 4
                copies.append((piece.at[second], dense_out.at[:, z // 2, core, x, z % 2]))
    started = [pltpu.make_async_copy(*c, sems.at[i]) for i, c in enumerate(copies)]
    for copy in started:
        copy.start()
    for copy in started:
        copy.wait()


def place(pos, pieces, shapes, into=()):
    names = list(pieces)
    anywhere = pl.BlockSpec(memory_space=pl.ANY)
    count = sum(8 if n[0] == "expert" else 4 for n in names)
    return pl.pallas_call(
        functools.partial(place_kernel, names),
        out_shape=shapes,
        in_specs=[pl.BlockSpec(memory_space=pltpu.SMEM)]
        + [pl.BlockSpec(memory_space=pltpu.VMEM)] * len(names)
        + [anywhere] * len(into),
        out_specs=(anywhere, anywhere),
        scratch_shapes=[pltpu.SemaphoreType.DMA((count,))],
        input_output_aliases={1 + len(names) + i: i for i in range(len(into))},
        compiler_params=pltpu.CompilerParams(vmem_limit_bytes=VMEM),
        cost_estimate=LIGHT,
        name="place",
    )(pos, *pieces.values(), *into)


def adamw(param, first, second, grad, clip):
    scaled = clip * grad
    first_new = 0.9 * first + 0.1 * scaled
    second_new = 0.95 * second + 0.05 * scaled * scaled
    first_hat = first_new / (1.0 - 0.9**STEP)
    second_hat = second_new / (1.0 - 0.95**STEP)
    param_new = param - 0.001 * (first_hat / (jnp.sqrt(second_hat) + 1e-08) + 0.1 * param)
    return (param_new, first_new, second_new)


def column_term(inputs, cotangent):
    return lax.dot_general(
        inputs, cotangent, (((0,), (0,)), ((), ())), preferred_element_type=jnp.float32
    )


def per_device(
    dense_input,
    dense_cotangent,
    expert_input,
    expert_cotangent,
    dense_master,
    dense_first,
    dense_second,
    expert_master,
    expert_first,
    expert_second,
):
    edp, ep = lax.axis_index("edp"), lax.axis_index("ep")
    zh, zl = edp // 2 % 2, ep % 2
    pos = jnp.stack([edp // 4, zh, edp % 2, ep // 2, zh * 2 + zl]).astype(jnp.int32)
    kvw, ff = dense_cotangent.shape[1], expert_cotangent.shape[2]

    routed = expert_input[0], expert_cotangent[0]
    tokens = dense_input, dense_cotangent
    terms = expert_half(1, pos, *routed)
    eaway = send(terms, CORE)
    eown = expert_half(0, pos, *after(routed, terms))
    efirst = [eown[k] + eaway[k] for k in range(4)]
    epieces = [(efirst[k] * 0.5).astype(f16) for k in (1, 2, 3)]
    egot = [send(epieces[k - 1], YS[k]) for k in (1, 2, 3)]
    terms = dense_half(1, pos, *after(tokens, epieces))
    away = send(terms, CORE)
    own = dense_half(0, pos, *after(tokens, terms))
    first = [own[k] + away[k] for k in range(4)]
    pieces = [(first[k] * 0.125).astype(f16) for k in (1, 2, 3)]
    got = [send(pieces[k - 1], FIRST[k]) for k in (1, 2, 3)]
    egot = after(egot, pieces)
    esecond = efirst[0] * 0.5 + sum(v.astype(f32) for v in egot)
    egot = send((esecond[1] * 0.25).astype(f16), ZHI)
    second = first[0] * 0.125 + sum(v.astype(f32) for v in got)
    got = [send((second[k] * 0.25).astype(f16), SECOND[k]) for k in (1, 2, 3)]
    third = second[0] * 0.25 + sum(v.astype(f32) for v in got)
    got = [send(third[k], YS[k]) for k in (1, 2, 3)]
    expert_grad = ((esecond[0] * 0.25 + egot.astype(f32)) * 8.0)[None]
    dense_grad = (third[0] + sum(got)) * 32.0

    mine = jnp.sum(dense_grad * dense_grad) + jnp.sum(expert_grad * expert_grad)
    spread = lax.all_to_all(jnp.full((128, 1, 128), mine, f32), BOTH, 0, 0, tiled=True)
    total = jnp.sum(spread[:, :, 0])
    ep_size = lax.axis_size("ep")
    limit = 10.0 * math.sqrt(dense_input.shape[1] * (kvw + ep_size * ff))
    clip = jnp.minimum(1.0, limit / (jnp.sqrt(total) + 1e-06))

    dense_param, dense_first_new, dense_second_new = adamw(
        dense_master, dense_first, dense_second, dense_grad, clip
    )
    expert_param, expert_first_new, expert_second_new = adamw(
        expert_master, expert_first, expert_second, expert_grad, clip
    )

    w = dense_param.astype(bf16)
    w = in_order(w, [send(w, YS[k]) for k in (1, 2, 3)], edp // 4)
    ew = expert_param.astype(bf16)[0]
    ew = jnp.stack([ew, send(ew, ZHI)])
    w, ew = lax.optimization_barrier((w, ew))
    w, ew = lax.optimization_barrier((ring(w, SECOND), ring(ew, YS)))
    shapes = (
        jax.ShapeDtypeStruct(DIMS + w.shape[2:], bf16),
        jax.ShapeDtypeStruct((16,) + ew.shape[2:], bf16),
    )
    late = {("dense", 0, m): send(w, FIRST[4 - m]) for m in (1, 2, 3)}
    early = {("dense", 0, 0): w, ("dense", 1, 0): send(w, CORE)}
    early |= {("expert", 0, 0): ew, ("expert", 1, 0): send(ew, CORE)}
    placed = place(pos, early, shapes)
    late, placed = lax.optimization_barrier((list(late.values()), placed))
    late = {("dense", 0, m + 1): v for m, v in enumerate(late)}
    late |= {("dense", 1, m): send(v, CORE) for (_, _, m), v in late.items()}
    dense_weight, expert_weight = place(pos, late, shapes, placed)
    dense_weight = dense_weight.reshape(-1, kvw)
    expert_weight = expert_weight.reshape(1, -1, ff)
    return (
        dense_param,
        dense_first_new,
        dense_second_new,
        dense_weight,
        expert_param,
        expert_first_new,
        expert_second_new,
        expert_weight,
    )


def solution(mesh):
    placed = (
        P(BOTH, None),
        P(BOTH, None),
        P("ep", "edp", None),
        P("ep", "edp", None),
        P(BOTH, None),
        P(BOTH, None),
        P(BOTH, None),
        P("ep", "edp", None),
        P("ep", "edp", None),
        P("ep", "edp", None),
    )
    return jax.shard_map(
        per_device,
        mesh=mesh,
        in_specs=placed,
        out_specs=(
            P(BOTH, None),
            P(BOTH, None),
            P(BOTH, None),
            P(),
            P("ep", "edp", None),
            P("ep", "edp", None),
            P("ep", "edp", None),
            P("ep", None, None),
        ),
        check_vma=False,
    )
```

time: 158 us -> 152 us (0.962)
  Pallas kernels: 0 us -> 25.2 us
  blocking collectives: 20.4 us -> 0 us
  waiting for transfers between devices: 46.6 us -> 65.9 us
  matrix products: 16.3 us -> 0 us
  local copies, waits for them, and re-layouts: 17.8 us -> 4.47 us
  other arithmetic: 19.3 us -> 6.39 us
  starting transfers between devices: 33.9 us -> 46.8 us
    pallas_call x0 -> x6, Pallas kernels: none -> 25.2 us  [the longest x4 20 us: half_terms(): pl.pallas_call(functools.partial(half_kernel, store, other), out_shape=ja...]
    all_to_all x1 -> x0, blocking collectives: 20.4 us -> none  [per_device(): lax.all_to_all(jnp.full((128, 1, 128), mine, f32), BOTH, 0, 0, tiled=True)]
    dot_general x2 -> x0, matrix products: 16.3 us -> none  [column_term(): lax.dot_general(inputs, cotangent, (((0,), (0,)), ((), ())), preferred_el...]
    all_to_all x0 -> x1, starting transfers between devices: none -> 11.6 us  [per_device(): lax.all_to_all(jnp.full((128, 1, 128), mine, f32), BOTH, 0, 0, tiled=True)]
    ppermute x30 -> x33, waiting for transfers between devices: 46.6 us -> 56.3 us  [send(): return lax.ppermute(value, BOTH, pairing)]
    all_to_all x0 -> x1, waiting for transfers between devices: none -> 9.54 us  [per_device(): lax.all_to_all(jnp.full((128, 1, 128), mine, f32), BOTH, 0, 0, tiled=True)]
    squeeze x3 -> x1, local copies, waits for them, and re-layouts: 5.37 us -> 0.02 us  [per_device(): got = [send(third[k], YS[k]) for k in (1, 2, 3)]]
    dynamic_slice x4 -> x0, local copies, waits for them, and re-layouts: 4.75 us -> none  [the longest x2 4.45 us: at(): return lax.dynamic_index_in_dim(value, index, axis, keepdims=False)]
  transfers between devices with their start and end apart: 30 -> 34, of which waited for: 16 -> 22; matrix products, arithmetic and copies ran while one was open for 17% -> 2% of each run, Pallas kernels for 0% -> 8%
where the time goes in v2:
time: 152 us
  waiting for transfers between devices  65.9 us (43%)
  starting transfers between devices  46.8 us (31%)
  Pallas kernels  25.2 us (17%)
  other arithmetic  6.39 us (4%)
  local copies, waits for them, and re-layouts  4.47 us (3%)
  between operations  3.25 us (2%)
    ppermute x33, waiting for transfers between devices, send(): return lax.ppermute(value, BOTH, pairing)  56.3 us
    ppermute x33, starting transfers between devices, send(): return lax.ppermute(value, BOTH, pairing)  35.2 us
    pallas_call x4, Pallas kernels, half_terms(): pl.pallas_call(functools.partial(half_kernel, store, other), out_shape=ja...  20 us
    all_to_all x1, starting transfers between devices, per_device(): lax.all_to_all(jnp.full((128, 1, 128), mine, f32), BOTH, 0, 0, tiled=True)  11.6 us
    all_to_all x1, waiting for transfers between devices, per_device(): lax.all_to_all(jnp.full((128, 1, 128), mine, f32), BOTH, 0, 0, tiled=True)  9.54 us
    pallas_call x2, Pallas kernels, place(): pl.pallas_call(functools.partial(place_kernel, names), out_shape=shapes,...  5.17 us
    unnamed x22, local copies, waits for them, and re-layouts  3.71 us
  transfers between devices with their start and end apart: 34, of which 22 were waited for; matrix products, arithmetic and copies ran while one was open for 2% of the time, Pallas kernels for 8%

profile of v2, /device:TPU:1, one launch (start us, length us, event | category | flops | bytes accessed | tf_op | source)
XLA Modules:
  0.0 152.0 jit_solution(9628900844447402361)
XLA Ops:
  0.8 2.2 %copy-done = bf16[1,1024,2048]{2,1,0:T(8,128)(2,1)S(1)} copy-done((bf16[1,1024,2048]{2,1,0:T(8,128)(2,1)S(1)}, bf16[1,1024,2048]{2,1,0:T(8,128)(2,1)}, u32[]{:S(2)}) %copy-start) | copy-done | bytes 4194328
  4.4 3.9 %expert_terms.2 = f32[4,2,128,768]{3,2,1,0:T(8,128)S(1)} custom-call(s32[5]{0:T(128)S(1)} %stack.74.pos, bf16[1024,2048]{1,0:T(8,128)(2,1)S(1)} %bitcast.92, bf16[1024,768]{1,0:T(8,128)(2,1)S(1)} %bitcast.94), custom_call_target="tpu_custom_call" | custom-call | flops 3221225472 | bytes 1 | tf_op jit(solution)/shard_map/expert_terms/pallas_call | solution.py:125
  9.8 3.8 %expert_terms.3 = f32[4,2,128,768]{3,2,1,0:T(8,128)S(1)} custom-call(s32[5]{0:T(128)S(1)} %stack.74.pos, bf16[1024,2048]{1,0:T(8,128)(2,1)S(1)} %bitcast.93, bf16[1024,768]{1,0:T(8,128)(2,1)S(1)} %bitcast.95), custom_call_target="tpu_custom_call" | custom-call | flops 3221225472 | bytes 1 | tf_op jit(solution)/shard_map/expert_terms/pallas_call | solution.py:125
  15.5 6.2 %dense_terms.2 = f32[4,4,4,16,1024]{4,3,2,1,0:T(8,128)S(1)} custom-call(s32[5]{0:T(128)S(1)} %stack.74.pos, bf16[1536,2048]{1,0:T(8,128)(2,1)S(1)} %bitcast.91, bf16[1536,1024]{1,0:T(8,128)(2,1)S(1)} %copy-done.1), custom_call_target="tpu_custom_call" | custom-call | flops 6442450944 | bytes 1 | tf_op jit(solution)/shard_map/dense_terms/pallas_call | solution.py:125
  23.4 2.6 %collective-permute-start.12 = (f16[2,128,768]{2,1,0:T(8,128)(2,1)S(1)}, f16[2,128,768]{2,1,0:T(8,128)(2,1)S(1)}, u32[]{:S(2)}, u32[]{:S(2)}) collective-permute-start(f16[2,128,768]{2,1,0:T(8,128)(2,1)S(1)} %get-tuple-element.66), channel_id=1, source_target_pairs={{0,64},{1,65},{2,66},{3,67},{4,68},{5,69},{6,70},{7,71},{8,72},{9,... | collective-permute-start | bytes 1179656 | tf_op jit(solution)/shard_map/ppermute | solution.py:50
  27.1 6.1 %dense_terms.3 = f32[4,4,4,16,1024]{4,3,2,1,0:T(8,128)S(1)} custom-call(s32[5]{0:T(128)S(1)} %stack.74.pos, bf16[1536,2048]{1,0:T(8,128)(2,1)S(1)} %bitcast.91, bf16[1536,1024]{1,0:T(8,128)(2,1)S(1)} %copy-done.1), custom_call_target="tpu_custom_call" | custom-call | flops 6442450944 | bytes 1 | tf_op jit(solution)/shard_map/dense_terms/pallas_call | solution.py:125
  34.1 3.9 %collective-permute-start.4 = (f16[4,4,16,1024]{3,2,1,0:T(8,128)(2,1)S(1)}, f16[4,4,16,1024]{3,2,1,0:T(8,128)(2,1)S(1)}, u32[]{:S(2)}, u32[]{:S(2)}) collective-permute-start(f16[4,4,16,1024]{3,2,1,0:T(8,128)(2,1)S(1)} %get-tuple-element.63), channel_id=1, source_target_pairs={{0,6},{1,7},{2,0},{3,1},{4,2},{5,3},{6,4},{7,5},{8,25},{9,8},{10,2... | collective-permute-start | bytes 1572872 | tf_op jit(solution)/shard_map/ppermute | solution.py:50
  38.6 4.9 %collective-permute-done.12 = f16[2,128,768]{2,1,0:T(8,128)(2,1)S(1)} collective-permute-done((f16[2,128,768]{2,1,0:T(8,128)(2,1)S(1)}, f16[2,128,768]{2,1,0:T(8,128)(2,1)S(1)}, u32[]{:S(2)}, u32[]{:S(2)}) %collective-permute-start.12) | collective-permute-done | bytes 393248 | tf_op jit(solution)/shard_map/ppermute | solution.py:50
  43.8 5.9 %collective-permute-done.4 = f16[4,4,16,1024]{3,2,1,0:T(8,128)(2,1)S(1)} collective-permute-done((f16[4,4,16,1024]{3,2,1,0:T(8,128)(2,1)S(1)}, f16[4,4,16,1024]{3,2,1,0:T(8,128)(2,1)S(1)}, u32[]{:S(2)}, u32[]{:S(2)}) %collective-permute-start.4) | collective-permute-done | bytes 524320 | tf_op jit(solution)/shard_map/ppermute | solution.py:50
  49.7 3.4 %collective-permute-done.2 = f16[4,4,16,1024]{3,2,1,0:T(8,128)(2,1)S(1)} collective-permute-done((f16[4,4,16,1024]{3,2,1,0:T(8,128)(2,1)S(1)}, f16[4,4,16,1024]{3,2,1,0:T(8,128)(2,1)S(1)}, u32[]{:S(2)}, u32[]{:S(2)}) %collective-permute-start.2) | collective-permute-done | bytes 524320 | tf_op jit(solution)/shard_map/ppermute | solution.py:50
  53.7 2.2 %collective-permute-start.7 = (f16[4,16,1024]{2,1,0:T(8,128)(2,1)S(1)}, f16[4,16,1024]{2,1,0:T(8,128)(2,1)S(1)}, u32[]{:S(2)}, u32[]{:S(2)}) collective-permute-start(f16[4,16,1024]{2,1,0:T(8,128)(2,1)S(1)} %get-tuple-element.69), channel_id=1, source_target_pairs={{0,17},{1,0},{2,19},{3,2},{4,21},{5,4},{6,23},{7,6},{8,14},{9,15},... | collective-permute-start | bytes 393224 | tf_op jit(solution)/shard_map/ppermute | solution.py:50
  59.3 2.1 %collective-permute-done.6 = f16[4,16,1024]{2,1,0:T(8,128)(2,1)S(1)} collective-permute-done((f16[4,16,1024]{2,1,0:T(8,128)(2,1)S(1)}, f16[4,16,1024]{2,1,0:T(8,128)(2,1)S(1)}, u32[]{:S(2)}, u32[]{:S(2)}) %collective-permute-start.6) | collective-permute-done | bytes 131104 | tf_op jit(solution)/shard_map/ppermute | solution.py:50
  71.5 11.6 %all-to-all-start = ((f32[128,1,128]{2,1,0:T(1,128)}), f32[128,1,128]{2,1,0:T(1,128)S(1)}, u32[]{:S(2)}, u32[]{:S(2)}) async-start(f32[128,1,128]{2,1,0:T(1,128)} %broadcast_in_dim.4), calls=%async_computation | async-start | bytes 131072 | tf_op jit(solution)/shard_map/all_to_all | solution.py:267
  83.3 9.5 %all-to-all-done = f32[128,1,128]{2,1,0:T(1,128)S(1)} async-done(((f32[128,1,128]{2,1,0:T(1,128)}), f32[128,1,128]{2,1,0:T(1,128)S(1)}, u32[]{:S(2)}, u32[]{:S(2)}) %all-to-all-start) | async-done | bytes 65568 | tf_op jit(solution)/shard_map/all_to_all | solution.py:267
  100.4 4.6 %collective-permute-done.18 = bf16[128,768]{1,0:T(8,128)(2,1)S(1)} collective-permute-done((bf16[128,768]{1,0:T(8,128)(2,1)S(1)}, bf16[128,768]{1,0:T(8,128)(2,1)S(1)}, u32[]{:S(2)}, u32[]{:S(2)}) %collective-permute-start.18) | collective-permute-done | bytes 196640 | tf_op jit(solution)/shard_map/ppermute | solution.py:50
  108.0 2.0 %collective-permute-start.22 = (bf16[2,128,768]{2,1,0:T(8,128)(2,1)S(1)}, bf16[2,128,768]{2,1,0:T(8,128)(2,1)S(1)}, u32[]{:S(2)}, u32[]{:S(2)}) collective-permute-start(bf16[2,128,768]{2,1,0:T(8,128)(2,1)S(1)} %pad_maximum_fusion.2), channel_id=1, source_target_pairs={{0,96},{1,97},{2,98},{3,99},{4,100},{5,101},{6,102},{7,103},{8,104... | collective-permute-start | bytes 1179656 | tf_op jit(solution)/shard_map/ppermute | solution.py:50
  111.5 5.2 %collective-permute-done.21 = bf16[4,16,1024]{2,1,0:T(8,128)(2,1)S(1)} collective-permute-done((bf16[4,16,1024]{2,1,0:T(8,128)(2,1)S(1)}, bf16[4,16,1024]{2,1,0:T(8,128)(2,1)S(1)}, u32[]{:S(2)}, u32[]{:S(2)}) %collective-permute-start.21) | collective-permute-done | bytes 131104 | tf_op jit(solution)/shard_map/ppermute | solution.py:50
  116.7 4.1 %collective-permute-done.19 = bf16[4,16,1024]{2,1,0:T(8,128)(2,1)S(1)} collective-permute-done((bf16[4,16,1024]{2,1,0:T(8,128)(2,1)S(1)}, bf16[4,16,1024]{2,1,0:T(8,128)(2,1)S(1)}, u32[]{:S(2)}, u32[]{:S(2)}) %collective-permute-start.19) | collective-permute-done | bytes 131104 | tf_op jit(solution)/shard_map/ppermute | solution.py:50
  120.9 2.4 %collective-permute-done.23 = bf16[2,128,768]{2,1,0:T(8,128)(2,1)S(1)} collective-permute-done((bf16[2,128,768]{2,1,0:T(8,128)(2,1)S(1)}, bf16[2,128,768]{2,1,0:T(8,128)(2,1)S(1)}, u32[]{:S(2)}, u32[]{:S(2)}) %collective-permute-start.23) | collective-permute-done | bytes 393248 | tf_op jit(solution)/shard_map/ppermute | solution.py:50
  131.0 2.8 %place.2 = (bf16[4,2,2,4,2,16,1024]{6,5,4,3,2,1,0:T(8,128)(2,1)}, bf16[16,128,768]{2,1,0:T(8,128)(2,1)}) custom-call(s32[5]{0:T(128)S(1)} %stack.74.pos, bf16[4,4,16,1024]{3,2,1,0:T(8,128)(2,1)S(1)} %pad_maximum_fusion.1.refs_0_, bf16[4,4,16,1024]{3,2,1,0:T(8,128)(2,1)S(1)} %collective-permute-done.28.refs_1_, ...), custom_call_target="tpu_custom_call" | custom-call | flops 1 | bytes 1 | tf_op jit(solution)/shard_map/place/pallas_call | solution.py:194
  133.8 6.8 %collective-permute-done.25.refs_0_ = bf16[4,4,16,1024]{3,2,1,0:T(8,128)(2,1)S(1)} collective-permute-done((bf16[4,4,16,1024]{3,2,1,0:T(8,128)(2,1)S(1)}, bf16[4,4,16,1024]{3,2,1,0:T(8,128)(2,1)S(1)}, u32[]{:S(2)}, u32[]{:S(2)}) %collective-permute-start.25) | collective-permute-done | bytes 524320 | tf_op jit(solution)/shard_map/ppermute | solution.py:50
  140.6 3.7 %collective-permute-done.27.refs_2_ = bf16[4,4,16,1024]{3,2,1,0:T(8,128)(2,1)S(1)} collective-permute-done((bf16[4,4,16,1024]{3,2,1,0:T(8,128)(2,1)S(1)}, bf16[4,4,16,1024]{3,2,1,0:T(8,128)(2,1)S(1)}, u32[]{:S(2)}, u32[]{:S(2)}) %collective-permute-start.27) | collective-permute-done | bytes 524320 | tf_op jit(solution)/shard_map/ppermute | solution.py:50
  144.3 2.1 %collective-permute-start.30 = (bf16[4,4,16,1024]{3,2,1,0:T(8,128)(2,1)S(1)}, bf16[4,4,16,1024]{3,2,1,0:T(8,128)(2,1)S(1)}, u32[]{:S(2)}, u32[]{:S(2)}) collective-permute-start(bf16[4,4,16,1024]{3,2,1,0:T(8,128)(2,1)S(1)} %collective-permute-done.25.refs_0_), channel_id=1, source_target_pairs={{0,8},{1,9},{2,10},{3,11},{4,12},{5,13},{6,14},{7,15},{8,0},{9,1},... | collective-permute-start | bytes 1572872 | tf_op jit(solution)/shard_map/ppermute | solution.py:50
  149.4 2.4 %place.3 = (bf16[4,2,2,4,2,16,1024]{6,5,4,3,2,1,0:T(8,128)(2,1)}, bf16[16,128,768]{2,1,0:T(8,128)(2,1)}) custom-call(s32[5]{0:T(128)S(1)} %stack.74.pos, bf16[4,4,16,1024]{3,2,1,0:T(8,128)(2,1)S(1)} %collective-permute-done.25.refs_0_, bf16[4,4,16,1024]{3,2,1,0:T(8,128)(2,1)S(1)} %collective-permute-done.26.refs_1_, ...), custom_call_target="tpu_custom_call", output_to_operand_aliasing={{0}: (7, {}), {1}: (8, {})} | custom-call | flops 1 | bytes 1 | tf_op jit(solution)/shard_map/place/pallas_call | solution.py:194
  (93 shorter events, 44.2 us)
Async XLA Ops:
  8.3 6.8 %collective-permute-start = (f32[4,2,128,768]{3,2,1,0:T(8,128)S(1)}, f32[4,2,128,768]{3,2,1,0:T(8,128)S(1)}, u32[]{:S(2)}, u32[]{:S(2)}) collective-permute-start(f32[4,2,128,768]{3,2,1,0:T(8,128)S(1)} %expert_terms.2), channel_id=1, source_target_pairs={{0,8},{1,9},{2,10},{3,11},{4,12},{5,13},{6,14},{7,15},{8,0},{9,1},... | collective-permute-start | bytes 9437192 | tf_op jit(solution)/shard_map/ppermute | solution.py:50
  21.7 11.6 %collective-permute-start.1 = (f32[4,4,4,16,1024]{4,3,2,1,0:T(8,128)S(1)}, f32[4,4,4,16,1024]{4,3,2,1,0:T(8,128)S(1)}, u32[]{:S(2)}, u32[]{:S(2)}) collective-permute-start(f32[4,4,4,16,1024]{4,3,2,1,0:T(8,128)S(1)} %dense_terms.2), channel_id=1, source_target_pairs={{0,8},{1,9},{2,10},{3,11},{4,12},{5,13},{6,14},{7,15},{8,0},{9,1},... | collective-permute-start | bytes 12582920 | tf_op jit(solution)/shard_map/ppermute | solution.py:50
  22.1 15.9 %collective-permute-start.11 = (f16[2,128,768]{2,1,0:T(8,128)(2,1)S(1)}, f16[2,128,768]{2,1,0:T(8,128)(2,1)S(1)}, u32[]{:S(2)}, u32[]{:S(2)}) collective-permute-start(f16[2,128,768]{2,1,0:T(8,128)(2,1)S(1)} %get-tuple-element.67), channel_id=1, source_target_pairs={{0,32},{1,33},{2,34},{3,35},{4,36},{5,37},{6,38},{7,39},{8,40},{9,... | collective-permute-start | bytes 1179656 | tf_op jit(solution)/shard_map/ppermute | solution.py:50
  23.4 20.1 %collective-permute-start.12 = (f16[2,128,768]{2,1,0:T(8,128)(2,1)S(1)}, f16[2,128,768]{2,1,0:T(8,128)(2,1)S(1)}, u32[]{:S(2)}, u32[]{:S(2)}) collective-permute-start(f16[2,128,768]{2,1,0:T(8,128)(2,1)S(1)} %get-tuple-element.66), channel_id=1, source_target_pairs={{0,64},{1,65},{2,66},{3,67},{4,68},{5,69},{6,70},{7,71},{8,72},{9,... | collective-permute-start | bytes 1179656 | tf_op jit(solution)/shard_map/ppermute | solution.py:50
  26.1 17.5 %collective-permute-start.13 = (f16[2,128,768]{2,1,0:T(8,128)(2,1)S(1)}, f16[2,128,768]{2,1,0:T(8,128)(2,1)S(1)}, u32[]{:S(2)}, u32[]{:S(2)}) collective-permute-start(f16[2,128,768]{2,1,0:T(8,128)(2,1)S(1)} %get-tuple-element.65), channel_id=1, source_target_pairs={{0,96},{1,97},{2,98},{3,99},{4,100},{5,101},{6,102},{7,103},{8,104... | collective-permute-start | bytes 1179656 | tf_op jit(solution)/shard_map/ppermute | solution.py:50
  34.1 15.6 %collective-permute-start.4 = (f16[4,4,16,1024]{3,2,1,0:T(8,128)(2,1)S(1)}, f16[4,4,16,1024]{3,2,1,0:T(8,128)(2,1)S(1)}, u32[]{:S(2)}, u32[]{:S(2)}) collective-permute-start(f16[4,4,16,1024]{3,2,1,0:T(8,128)(2,1)S(1)} %get-tuple-element.63), channel_id=1, source_target_pairs={{0,6},{1,7},{2,0},{3,1},{4,2},{5,3},{6,4},{7,5},{8,25},{9,8},{10,2... | collective-permute-start | bytes 1572872 | tf_op jit(solution)/shard_map/ppermute | solution.py:50
  38.0 11.7 %collective-permute-start.3 = (f16[4,4,16,1024]{3,2,1,0:T(8,128)(2,1)S(1)}, f16[4,4,16,1024]{3,2,1,0:T(8,128)(2,1)S(1)}, u32[]{:S(2)}, u32[]{:S(2)}) collective-permute-start(f16[4,4,16,1024]{3,2,1,0:T(8,128)(2,1)S(1)} %get-tuple-element.64), channel_id=1, source_target_pairs={{0,4},{1,5},{2,6},{3,7},{4,0},{5,1},{6,2},{7,3},{8,24},{9,25},{10,... | collective-permute-start | bytes 1572872 | tf_op jit(solution)/shard_map/ppermute | solution.py:50
  38.0 15.2 %collective-permute-start.2 = (f16[4,4,16,1024]{3,2,1,0:T(8,128)(2,1)S(1)}, f16[4,4,16,1024]{3,2,1,0:T(8,128)(2,1)S(1)}, u32[]{:S(2)}, u32[]{:S(2)}) collective-permute-start(f16[4,4,16,1024]{3,2,1,0:T(8,128)(2,1)S(1)} %get-tuple-element.62), channel_id=1, source_target_pairs={{0,2},{1,3},{2,4},{3,5},{4,6},{5,7},{6,0},{7,1},{8,9},{9,24},{10,1... | collective-permute-start | bytes 1572872 | tf_op jit(solution)/shard_map/ppermute | solution.py:50
  53.7 5.5 %collective-permute-start.7 = (f16[4,16,1024]{2,1,0:T(8,128)(2,1)S(1)}, f16[4,16,1024]{2,1,0:T(8,128)(2,1)S(1)}, u32[]{:S(2)}, u32[]{:S(2)}) collective-permute-start(f16[4,16,1024]{2,1,0:T(8,128)(2,1)S(1)} %get-tuple-element.69), channel_id=1, source_target_pairs={{0,17},{1,0},{2,19},{3,2},{4,21},{5,4},{6,23},{7,6},{8,14},{9,15},... | collective-permute-start | bytes 393224 | tf_op jit(solution)/shard_map/ppermute | solution.py:50
  56.0 5.4 %collective-permute-start.6 = (f16[4,16,1024]{2,1,0:T(8,128)(2,1)S(1)}, f16[4,16,1024]{2,1,0:T(8,128)(2,1)S(1)}, u32[]{:S(2)}, u32[]{:S(2)}) collective-permute-start(f16[4,16,1024]{2,1,0:T(8,128)(2,1)S(1)} %get-tuple-element.70), channel_id=1, source_target_pairs={{0,16},{1,17},{2,18},{3,19},{4,20},{5,21},{6,22},{7,23},{8,12},{9,... | collective-permute-start | bytes 393224 | tf_op jit(solution)/shard_map/ppermute | solution.py:50
  56.5 6.2 %collective-permute-start.5 = (f16[4,16,1024]{2,1,0:T(8,128)(2,1)S(1)}, f16[4,16,1024]{2,1,0:T(8,128)(2,1)S(1)}, u32[]{:S(2)}, u32[]{:S(2)}) collective-permute-start(f16[4,16,1024]{2,1,0:T(8,128)(2,1)S(1)} %get-tuple-element.68), channel_id=1, source_target_pairs={{0,1},{1,16},{2,3},{3,18},{4,5},{5,20},{6,7},{7,22},{8,10},{9,11},... | collective-permute-start | bytes 393224 | tf_op jit(solution)/shard_map/ppermute | solution.py:50
  57.1 7.9 %collective-permute-start.14 = (f16[128,768]{1,0:T(8,128)(2,1)S(1)}, f16[128,768]{1,0:T(8,128)(2,1)S(1)}, u32[]{:S(2)}, u32[]{:S(2)}) collective-permute-start(f16[128,768]{1,0:T(8,128)(2,1)S(1)} %fusion.34), channel_id=1, source_target_pairs={{0,16},{1,17},{2,18},{3,19},{4,20},{5,21},{6,22},{7,23},{8,24},{9,... | collective-permute-start | bytes 589832 | tf_op jit(solution)/shard_map/ppermute | solution.py:50
  71.5 21.3 %all-to-all-start = ((f32[128,1,128]{2,1,0:T(1,128)}), f32[128,1,128]{2,1,0:T(1,128)S(1)}, u32[]{:S(2)}, u32[]{:S(2)}) async-start(f32[128,1,128]{2,1,0:T(1,128)} %broadcast_in_dim.4), calls=%async_computation | async-start | bytes 131072 | tf_op jit(solution)/shard_map/all_to_all | solution.py:267
  95.0 5.3 %collective-permute-start.15 = (bf16[16,1024]{1,0:T(8,128)(2,1)S(1)}, bf16[16,1024]{1,0:T(8,128)(2,1)S(1)}, u32[]{:S(2)}, u32[]{:S(2)}) collective-permute-start(bf16[16,1024]{1,0:T(8,128)(2,1)S(1)} %get-tuple-element.56), channel_id=1, source_target_pairs={{0,32},{1,33},{2,34},{3,35},{4,36},{5,37},{6,38},{7,39},{8,40},{9,... | collective-permute-start | bytes 98312 | tf_op jit(solution)/shard_map/ppermute | solution.py:50
  99.0 6.0 %collective-permute-start.18 = (bf16[128,768]{1,0:T(8,128)(2,1)S(1)}, bf16[128,768]{1,0:T(8,128)(2,1)S(1)}, u32[]{:S(2)}, u32[]{:S(2)}) collective-permute-start(bf16[128,768]{1,0:T(8,128)(2,1)S(1)} %bitcast.99), channel_id=1, source_target_pairs={{0,16},{1,17},{2,18},{3,19},{4,20},{5,21},{6,22},{7,23},{8,24},{9,... | collective-permute-start | bytes 589832 | tf_op jit(solution)/shard_map/ppermute | solution.py:50
  105.1 15.8 %collective-permute-start.24 = (bf16[2,128,768]{2,1,0:T(8,128)(2,1)S(1)}, bf16[2,128,768]{2,1,0:T(8,128)(2,1)S(1)}, u32[]{:S(2)}, u32[]{:S(2)}) collective-permute-start(bf16[2,128,768]{2,1,0:T(8,128)(2,1)S(1)} %pad_maximum_fusion.2), channel_id=1, source_target_pairs={{0,32},{1,33},{2,34},{3,35},{4,36},{5,37},{6,38},{7,39},{8,40},{9,... | collective-permute-start | bytes 1179656 | tf_op jit(solution)/shard_map/ppermute | solution.py:50
  106.3 17.0 %collective-permute-start.23 = (bf16[2,128,768]{2,1,0:T(8,128)(2,1)S(1)}, bf16[2,128,768]{2,1,0:T(8,128)(2,1)S(1)}, u32[]{:S(2)}, u32[]{:S(2)}) collective-permute-start(bf16[2,128,768]{2,1,0:T(8,128)(2,1)S(1)} %pad_maximum_fusion.2), channel_id=1, source_target_pairs={{0,64},{1,65},{2,66},{3,67},{4,68},{5,69},{6,70},{7,71},{8,72},{9,... | collective-permute-start | bytes 1179656 | tf_op jit(solution)/shard_map/ppermute | solution.py:50
  108.0 17.3 %collective-permute-start.22 = (bf16[2,128,768]{2,1,0:T(8,128)(2,1)S(1)}, bf16[2,128,768]{2,1,0:T(8,128)(2,1)S(1)}, u32[]{:S(2)}, u32[]{:S(2)}) collective-permute-start(bf16[2,128,768]{2,1,0:T(8,128)(2,1)S(1)} %pad_maximum_fusion.2), channel_id=1, source_target_pairs={{0,96},{1,97},{2,98},{3,99},{4,100},{5,101},{6,102},{7,103},{8,104... | collective-permute-start | bytes 1179656 | tf_op jit(solution)/shard_map/ppermute | solution.py:50
  109.9 6.7 %collective-permute-start.21 = (bf16[4,16,1024]{2,1,0:T(8,128)(2,1)S(1)}, bf16[4,16,1024]{2,1,0:T(8,128)(2,1)S(1)}, u32[]{:S(2)}, u32[]{:S(2)}) collective-permute-start(bf16[4,16,1024]{2,1,0:T(8,128)(2,1)S(1)} %pad_maximum_fusion.3), channel_id=1, source_target_pairs={{0,1},{1,16},{2,3},{3,18},{4,5},{5,20},{6,7},{7,22},{8,10},{9,11},... | collective-permute-start | bytes 393224 | tf_op jit(solution)/shard_map/ppermute | solution.py:50
  110.5 6.1 %collective-permute-start.20 = (bf16[4,16,1024]{2,1,0:T(8,128)(2,1)S(1)}, bf16[4,16,1024]{2,1,0:T(8,128)(2,1)S(1)}, u32[]{:S(2)}, u32[]{:S(2)}) collective-permute-start(bf16[4,16,1024]{2,1,0:T(8,128)(2,1)S(1)} %pad_maximum_fusion.3), channel_id=1, source_target_pairs={{0,16},{1,17},{2,18},{3,19},{4,20},{5,21},{6,22},{7,23},{8,12},{9,... | collective-permute-start | bytes 393224 | tf_op jit(solution)/shard_map/ppermute | solution.py:50
  125.5 5.6 %collective-permute-start.29 = (bf16[4,2,128,768]{3,2,1,0:T(8,128)(2,1)S(1)}, bf16[4,2,128,768]{3,2,1,0:T(8,128)(2,1)S(1)}, u32[]{:S(2)}, u32[]{:S(2)}) collective-permute-start(bf16[4,2,128,768]{3,2,1,0:T(8,128)(2,1)S(1)} %pad_maximum_fusion.refs_2_), channel_id=1, source_target_pairs={{0,8},{1,9},{2,10},{3,11},{4,12},{5,13},{6,14},{7,15},{8,0},{9,1},... | collective-permute-start | bytes 4718600 | tf_op jit(solution)/shard_map/ppermute | solution.py:50
  127.3 13.3 %collective-permute-start.25 = (bf16[4,4,16,1024]{3,2,1,0:T(8,128)(2,1)S(1)}, bf16[4,4,16,1024]{3,2,1,0:T(8,128)(2,1)S(1)}, u32[]{:S(2)}, u32[]{:S(2)}) collective-permute-start(bf16[4,4,16,1024]{3,2,1,0:T(8,128)(2,1)S(1)} %pad_maximum_fusion.1.refs_0_), channel_id=1, source_target_pairs={{0,6},{1,7},{2,0},{3,1},{4,2},{5,3},{6,4},{7,5},{8,25},{9,8},{10,2... | collective-permute-start | bytes 1572872 | tf_op jit(solution)/shard_map/ppermute | solution.py:50
  128.9 11.7 %collective-permute-start.26 = (bf16[4,4,16,1024]{3,2,1,0:T(8,128)(2,1)S(1)}, bf16[4,4,16,1024]{3,2,1,0:T(8,128)(2,1)S(1)}, u32[]{:S(2)}, u32[]{:S(2)}) collective-permute-start(bf16[4,4,16,1024]{3,2,1,0:T(8,128)(2,1)S(1)} %pad_maximum_fusion.1.refs_0_), channel_id=1, source_target_pairs={{0,4},{1,5},{2,6},{3,7},{4,0},{5,1},{6,2},{7,3},{8,24},{9,25},{10,... | collective-permute-start | bytes 1572872 | tf_op jit(solution)/shard_map/ppermute | solution.py:50
  129.7 14.6 %collective-permute-start.27 = (bf16[4,4,16,1024]{3,2,1,0:T(8,128)(2,1)S(1)}, bf16[4,4,16,1024]{3,2,1,0:T(8,128)(2,1)S(1)}, u32[]{:S(2)}, u32[]{:S(2)}) collective-permute-start(bf16[4,4,16,1024]{3,2,1,0:T(8,128)(2,1)S(1)} %pad_maximum_fusion.1.refs_0_), channel_id=1, source_target_pairs={{0,2},{1,3},{2,4},{3,5},{4,6},{5,7},{6,0},{7,1},{8,9},{9,24},{10,1... | collective-permute-start | bytes 1572872 | tf_op jit(solution)/shard_map/ppermute | solution.py:50
  (21 other events, 316.3 us)

commit v3 on v2

--- a/solution.py
+++ b/solution.py
@@ -171,10 +171,10 @@
         core = (pos[2] + other) % 2
         even = core == 0
         if kind == "expert":
-            for dy in range(4):
+            for n, dy in enumerate(first):
                 for dz in range(2):
                     block = ((pos[0] + dy) % 4 * 2 + (pos[1] + dz) % 2) * 2 + core
-                    copies.append((piece.at[dy, dz], expert_out.at[block]))
+                    copies.append((piece.at[n, dz], expert_out.at[block]))
         else:
             for second in range(4):
                 x = (pos[3] + jnp.where(even, first, second)) % 4
@@ -190,7 +190,7 @@
 def place(pos, pieces, shapes, into=()):
     names = list(pieces)
     anywhere = pl.BlockSpec(memory_space=pl.ANY)
-    count = sum(8 if n[0] == "expert" else 4 for n in names)
+    count = sum(2 * len(n[2]) if n[0] == "expert" else 4 for n in names)
     return pl.pallas_call(
         functools.partial(place_kernel, names),
         out_shape=shapes,
@@ -278,23 +278,28 @@
     )
 
     w = dense_param.astype(bf16)
-    w = in_order(w, [send(w, YS[k]) for k in (1, 2, 3)], edp // 4)
     ew = expert_param.astype(bf16)[0]
-    ew = jnp.stack([ew, send(ew, ZHI)])
     w, ew = lax.optimization_barrier((w, ew))
-    w, ew = lax.optimization_barrier((ring(w, SECOND), ring(ew, YS)))
+    got = [send(w, YS[k]) for k in (1, 2, 3)], send(ew, ZHI)
+    got, other = lax.optimization_barrier(got)
+    w = in_order(w, got, edp // 4)
+    ew = jnp.stack([ew, other])
+    w, near = lax.optimization_barrier((ring(w, SECOND), [send(ew, YS[3]), send(ew, YS[1])]))
+    far = send(ew, YS[2])[None]
+    near = jnp.stack([ew, *near])
     shapes = (
         jax.ShapeDtypeStruct(DIMS + w.shape[2:], bf16),
-        jax.ShapeDtypeStruct((16,) + ew.shape[2:], bf16),
-    )
-    late = {("dense", 0, m): send(w, FIRST[4 - m]) for m in (1, 2, 3)}
+        jax.ShapeDtypeStruct((16,) + ew.shape[1:], bf16),
+    )
+    late = [send(w, FIRST[4 - m]) for m in (1, 2, 3)]
     early = {("dense", 0, 0): w, ("dense", 1, 0): send(w, CORE)}
-    early |= {("expert", 0, 0): ew, ("expert", 1, 0): send(ew, CORE)}
+    early |= {("expert", 0, (0, 1, 3)): near, ("expert", 1, (0, 1, 3)): send(near, CORE)}
     placed = place(pos, early, shapes)
-    late, placed = lax.optimization_barrier((list(late.values()), placed))
-    late = {("dense", 0, m + 1): v for m, v in enumerate(late)}
-    late |= {("dense", 1, m): send(v, CORE) for (_, _, m), v in late.items()}
-    dense_weight, expert_weight = place(pos, late, shapes, placed)
+    late, far, placed = lax.optimization_barrier((late, far, placed))
+    late = {("dense", 0, m + 1): v for m, v in enumerate(late)} | {("expert", 0, (2,)): far}
+    swaps = {(d, 1, m): send(v, CORE) for (d, _, m), v in late.items()}
+    placed = place(pos, late, shapes, placed)
+    dense_weight, expert_weight = place(pos, swaps, shapes, placed)
     dense_weight = dense_weight.reshape(-1, kvw)
     expert_weight = expert_weight.reshape(1, -1, ff)
     return (

time: 152 us -> 141 us (0.928)
  blocking collectives: 0 us -> 21.2 us
  waiting for transfers between devices: 65.9 us -> 45.5 us
  starting transfers between devices: 46.8 us -> 34.4 us
    all_to_all x0 -> x1, blocking collectives: none -> 21.2 us  [per_device(): lax.all_to_all(jnp.full((128, 1, 128), mine, f32), BOTH, 0, 0, tiled=True)]
    all_to_all x1 -> x0, starting transfers between devices: 11.6 us -> none  [per_device(): lax.all_to_all(jnp.full((128, 1, 128), mine, f32), BOTH, 0, 0, tiled=True)]
    ppermute x33 -> x34, waiting for transfers between devices: 56.3 us -> 45.5 us  [send(): return lax.ppermute(value, BOTH, pairing)]
    all_to_all x1 -> x0, waiting for transfers between devices: 9.54 us -> none  [per_device(): lax.all_to_all(jnp.full((128, 1, 128), mine, f32), BOTH, 0, 0, tiled=True)]
    pallas_call x2 -> x3, Pallas kernels: 5.17 us -> 6.36 us  [place(): pl.pallas_call(functools.partial(place_kernel, names), out_shape=shapes,...]
    ppermute x33 -> x34, starting transfers between devices: 35.2 us -> 34.4 us  [send(): return lax.ppermute(value, BOTH, pairing)]
  transfers between devices with their start and end apart: 34 -> 34, of which waited for: 22 -> 22; matrix products, arithmetic and copies ran while one was open for 2% -> 1% of each run, Pallas kernels for 8% -> 10%
where the time goes in v3:
time: 141 us
  waiting for transfers between devices  45.5 us (32%)
  starting transfers between devices  34.4 us (24%)
  Pallas kernels  26.3 us (19%)
  blocking collectives  21.2 us (15%)
  other arithmetic  6.34 us (4%)
  local copies, waits for them, and re-layouts  3.84 us (3%)
  between operations  3.16 us (2%)
    ppermute x34, waiting for transfers between devices, send(): return lax.ppermute(value, BOTH, pairing)  45.5 us
    ppermute x34, starting transfers between devices, send(): return lax.ppermute(value, BOTH, pairing)  34.4 us
    all_to_all x1, blocking collectives, per_device(): lax.all_to_all(jnp.full((128, 1, 128), mine, f32), BOTH, 0, 0, tiled=True)  21.2 us
    pallas_call x4, Pallas kernels, half_terms(): pl.pallas_call(functools.partial(half_kernel, store, other), out_shape=ja...  20 us
    pallas_call x3, Pallas kernels, place(): pl.pallas_call(functools.partial(place_kernel, names), out_shape=shapes,...  6.36 us
    unnamed x22, local copies, waits for them, and re-layouts  3.7 us
  transfers between devices with their start and end apart: 34, of which 22 were waited for; matrix products, arithmetic and copies ran while one was open for 1% of the time, Pallas kernels for 10%

profile of v3, /device:TPU:1, one launch (start us, length us, event | category | flops | bytes accessed | tf_op | source)
XLA Modules:
  0.0 140.8 jit_solution(11215711001994274527)
XLA Ops:
  0.8 2.2 %copy-done = bf16[1,1024,2048]{2,1,0:T(8,128)(2,1)S(1)} copy-done((bf16[1,1024,2048]{2,1,0:T(8,128)(2,1)S(1)}, bf16[1,1024,2048]{2,1,0:T(8,128)(2,1)}, u32[]{:S(2)}) %copy-start) | copy-done | bytes 4194328
  4.4 3.8 %expert_terms.2 = f32[4,2,128,768]{3,2,1,0:T(8,128)S(1)} custom-call(s32[5]{0:T(128)S(1)} %stack.74.pos, bf16[1024,2048]{1,0:T(8,128)(2,1)S(1)} %bitcast.98, bf16[1024,768]{1,0:T(8,128)(2,1)S(1)} %bitcast.100), custom_call_target="tpu_custom_call" | custom-call | flops 3221225472 | bytes 1 | tf_op jit(solution)/shard_map/expert_terms/pallas_call | solution.py:125
  8.2 1.5 %collective-permute-start = (f32[4,2,128,768]{3,2,1,0:T(8,128)S(1)}, f32[4,2,128,768]{3,2,1,0:T(8,128)S(1)}, u32[]{:S(2)}, u32[]{:S(2)}) collective-permute-start(f32[4,2,128,768]{3,2,1,0:T(8,128)S(1)} %expert_terms.2), channel_id=1, source_target_pairs={{0,8},{1,9},{2,10},{3,11},{4,12},{5,13},{6,14},{7,15},{8,0},{9,1},... | collective-permute-start | bytes 9437192 | tf_op jit(solution)/shard_map/ppermute | solution.py:50
  9.8 3.8 %expert_terms.3 = f32[4,2,128,768]{3,2,1,0:T(8,128)S(1)} custom-call(s32[5]{0:T(128)S(1)} %stack.74.pos, bf16[1024,2048]{1,0:T(8,128)(2,1)S(1)} %bitcast.99, bf16[1024,768]{1,0:T(8,128)(2,1)S(1)} %bitcast.101), custom_call_target="tpu_custom_call" | custom-call | flops 3221225472 | bytes 1 | tf_op jit(solution)/shard_map/expert_terms/pallas_call | solution.py:125
  15.5 6.2 %dense_terms.2 = f32[4,4,4,16,1024]{4,3,2,1,0:T(8,128)S(1)} custom-call(s32[5]{0:T(128)S(1)} %stack.74.pos, bf16[1536,2048]{1,0:T(8,128)(2,1)S(1)} %bitcast.97, bf16[1536,1024]{1,0:T(8,128)(2,1)S(1)} %copy-done.1), custom_call_target="tpu_custom_call" | custom-call | flops 6442450944 | bytes 1 | tf_op jit(solution)/shard_map/dense_terms/pallas_call | solution.py:125
  23.5 2.6 %collective-permute-start.12 = (f16[2,128,768]{2,1,0:T(8,128)(2,1)S(1)}, f16[2,128,768]{2,1,0:T(8,128)(2,1)S(1)}, u32[]{:S(2)}, u32[]{:S(2)}) collective-permute-start(f16[2,128,768]{2,1,0:T(8,128)(2,1)S(1)} %get-tuple-element.82), channel_id=1, source_target_pairs={{0,64},{1,65},{2,66},{3,67},{4,68},{5,69},{6,70},{7,71},{8,72},{9,... | collective-permute-start | bytes 1179656 | tf_op jit(solution)/shard_map/ppermute | solution.py:50
  27.1 6.2 %dense_terms.3 = f32[4,4,4,16,1024]{4,3,2,1,0:T(8,128)S(1)} custom-call(s32[5]{0:T(128)S(1)} %stack.74.pos, bf16[1536,2048]{1,0:T(8,128)(2,1)S(1)} %bitcast.97, bf16[1536,1024]{1,0:T(8,128)(2,1)S(1)} %copy-done.1), custom_call_target="tpu_custom_call" | custom-call | flops 6442450944 | bytes 1 | tf_op jit(solution)/shard_map/dense_terms/pallas_call | solution.py:125
  34.1 3.9 %collective-permute-start.4 = (f16[4,4,16,1024]{3,2,1,0:T(8,128)(2,1)S(1)}, f16[4,4,16,1024]{3,2,1,0:T(8,128)(2,1)S(1)}, u32[]{:S(2)}, u32[]{:S(2)}) collective-permute-start(f16[4,4,16,1024]{3,2,1,0:T(8,128)(2,1)S(1)} %get-tuple-element.79), channel_id=1, source_target_pairs={{0,6},{1,7},{2,0},{3,1},{4,2},{5,3},{6,4},{7,5},{8,25},{9,8},{10,2... | collective-permute-start | bytes 1572872 | tf_op jit(solution)/shard_map/ppermute | solution.py:50
  38.7 4.9 %collective-permute-done.12 = f16[2,128,768]{2,1,0:T(8,128)(2,1)S(1)} collective-permute-done((f16[2,128,768]{2,1,0:T(8,128)(2,1)S(1)}, f16[2,128,768]{2,1,0:T(8,128)(2,1)S(1)}, u32[]{:S(2)}, u32[]{:S(2)}) %collective-permute-start.12) | collective-permute-done | bytes 393248 | tf_op jit(solution)/shard_map/ppermute | solution.py:50
  43.8 5.9 %collective-permute-done.4 = f16[4,4,16,1024]{3,2,1,0:T(8,128)(2,1)S(1)} collective-permute-done((f16[4,4,16,1024]{3,2,1,0:T(8,128)(2,1)S(1)}, f16[4,4,16,1024]{3,2,1,0:T(8,128)(2,1)S(1)}, u32[]{:S(2)}, u32[]{:S(2)}) %collective-permute-start.4) | collective-permute-done | bytes 524320 | tf_op jit(solution)/shard_map/ppermute | solution.py:50
  49.7 3.4 %collective-permute-done.2 = f16[4,4,16,1024]{3,2,1,0:T(8,128)(2,1)S(1)} collective-permute-done((f16[4,4,16,1024]{3,2,1,0:T(8,128)(2,1)S(1)}, f16[4,4,16,1024]{3,2,1,0:T(8,128)(2,1)S(1)}, u32[]{:S(2)}, u32[]{:S(2)}) %collective-permute-start.2) | collective-permute-done | bytes 524320 | tf_op jit(solution)/shard_map/ppermute | solution.py:50
  53.8 2.2 %collective-permute-start.7 = (f16[4,16,1024]{2,1,0:T(8,128)(2,1)S(1)}, f16[4,16,1024]{2,1,0:T(8,128)(2,1)S(1)}, u32[]{:S(2)}, u32[]{:S(2)}) collective-permute-start(f16[4,16,1024]{2,1,0:T(8,128)(2,1)S(1)} %get-tuple-element.85), channel_id=1, source_target_pairs={{0,17},{1,0},{2,19},{3,2},{4,21},{5,4},{6,23},{7,6},{8,14},{9,15},... | collective-permute-start | bytes 393224 | tf_op jit(solution)/shard_map/ppermute | solution.py:50
  59.3 2.1 %collective-permute-done.6 = f16[4,16,1024]{2,1,0:T(8,128)(2,1)S(1)} collective-permute-done((f16[4,16,1024]{2,1,0:T(8,128)(2,1)S(1)}, f16[4,16,1024]{2,1,0:T(8,128)(2,1)S(1)}, u32[]{:S(2)}, u32[]{:S(2)}) %collective-permute-start.6) | collective-permute-done | bytes 131104 | tf_op jit(solution)/shard_map/ppermute | solution.py:50
  71.0 21.2 %all_to_all.5 = f32[128,1,128]{2,1,0:T(1,128)S(1)} all-to-all(f32[128,1,128]{2,1,0:T(1,128)S(1)} %broadcast_in_dim.7), channel_id=1, replica_groups=mesh['edp'=16,'ep'=8] {'edp','ep'}, dimensions={0} | all-to-all | bytes 131072 | tf_op jit(solution)/shard_map/all_to_all | solution.py:267
  97.3 1.7 %collective-permute-start.16 = (bf16[16,1024]{1,0:T(8,128)(2,1)S(1)}, bf16[16,1024]{1,0:T(8,128)(2,1)S(1)}, u32[]{:S(2)}, u32[]{:S(2)}) collective-permute-start(bf16[16,1024]{1,0:T(8,128)(2,1)S(1)} %get-tuple-element.47), channel_id=1, source_target_pairs={{0,64},{1,65},{2,66},{3,67},{4,68},{5,69},{6,70},{7,71},{8,72},{9,... | collective-permute-start | bytes 98312 | tf_op jit(solution)/shard_map/ppermute | solution.py:50
  106.4 1.8 %collective-permute-start.19 = (bf16[4,16,1024]{2,1,0:T(8,128)(2,1)S(1)}, bf16[4,16,1024]{2,1,0:T(8,128)(2,1)S(1)}, u32[]{:S(2)}, u32[]{:S(2)}) collective-permute-start(bf16[4,16,1024]{2,1,0:T(8,128)(2,1)S(1)} %get-tuple-element.93), channel_id=1, source_target_pairs={{0,17},{1,0},{2,19},{3,2},{4,21},{5,4},{6,23},{7,6},{8,14},{9,15},... | collective-permute-start | bytes 393224 | tf_op jit(solution)/shard_map/ppermute | solution.py:50
  108.2 3.2 %collective-permute-done.21 = bf16[4,16,1024]{2,1,0:T(8,128)(2,1)S(1)} collective-permute-done((bf16[4,16,1024]{2,1,0:T(8,128)(2,1)S(1)}, bf16[4,16,1024]{2,1,0:T(8,128)(2,1)S(1)}, u32[]{:S(2)}, u32[]{:S(2)}) %collective-permute-start.21) | collective-permute-done | bytes 131104 | tf_op jit(solution)/shard_map/ppermute | solution.py:50
  112.2 1.6 %collective-permute-done.23 = bf16[2,128,768]{2,1,0:T(8,128)(2,1)S(1)} collective-permute-done((bf16[2,128,768]{2,1,0:T(8,128)(2,1)S(1)}, bf16[2,128,768]{2,1,0:T(8,128)(2,1)S(1)}, u32[]{:S(2)}, u32[]{:S(2)}) %collective-permute-start.23) | collective-permute-done | bytes 393248 | tf_op jit(solution)/shard_map/ppermute | solution.py:50
  113.9 3.5 %collective-permute-start.29 = (bf16[3,2,128,768]{3,2,1,0:T(8,128)(2,1)S(1)}, bf16[3,2,128,768]{3,2,1,0:T(8,128)(2,1)S(1)}, u32[]{:S(2)}, u32[]{:S(2)}) collective-permute-start(bf16[3,2,128,768]{3,2,1,0:T(8,128)(2,1)S(1)} %pad_maximum_fusion.refs_2_), channel_id=1, source_target_pairs={{0,8},{1,9},{2,10},{3,11},{4,12},{5,13},{6,14},{7,15},{8,0},{9,1},... | collective-permute-start | bytes 3538952 | tf_op jit(solution)/shard_map/ppermute | solution.py:50
  120.7 2.5 %place.3 = (bf16[4,2,2,4,2,16,1024]{6,5,4,3,2,1,0:T(8,128)(2,1)}, bf16[16,128,768]{2,1,0:T(8,128)(2,1)}) custom-call(s32[5]{0:T(128)S(1)} %stack.74.pos, bf16[4,4,16,1024]{3,2,1,0:T(8,128)(2,1)S(1)} %pad_maximum_fusion.1.refs_0_, bf16[4,4,16,1024]{3,2,1,0:T(8,128)(2,1)S(1)} %collective-permute-done.28.refs_1_, ...), custom_call_target="tpu_custom_call" | custom-call | flops 1 | bytes 1 | tf_op jit(solution)/shard_map/place/pallas_call | solution.py:194
  123.1 9.4 %collective-permute-done.27 = bf16[2,128,768]{2,1,0:T(8,128)(2,1)S(1)} collective-permute-done((bf16[2,128,768]{2,1,0:T(8,128)(2,1)S(1)}, bf16[2,128,768]{2,1,0:T(8,128)(2,1)S(1)}, u32[]{:S(2)}, u32[]{:S(2)}) %collective-permute-start.27) | collective-permute-done | bytes 393248 | tf_op jit(solution)/shard_map/ppermute | solution.py:50
  132.5 1.8 %collective-permute-done.26.refs_2_ = bf16[4,4,16,1024]{3,2,1,0:T(8,128)(2,1)S(1)} collective-permute-done((bf16[4,4,16,1024]{3,2,1,0:T(8,128)(2,1)S(1)}, bf16[4,4,16,1024]{3,2,1,0:T(8,128)(2,1)S(1)}, u32[]{:S(2)}, u32[]{:S(2)}) %collective-permute-start.26) | collective-permute-done | bytes 524320 | tf_op jit(solution)/shard_map/ppermute | solution.py:50
  135.6 1.9 %place.4 = (bf16[4,2,2,4,2,16,1024]{6,5,4,3,2,1,0:T(8,128)(2,1)}, bf16[16,128,768]{2,1,0:T(8,128)(2,1)}) custom-call(s32[5]{0:T(128)S(1)} %stack.74.pos, bf16[4,4,16,1024]{3,2,1,0:T(8,128)(2,1)S(1)} %collective-permute-done.24.refs_0_, bf16[4,4,16,1024]{3,2,1,0:T(8,128)(2,1)S(1)} %collective-permute-done.25.refs_1_, ...), custom_call_target="tpu_custom_call", output_to_operand_aliasing={{0}: (5, {}), {1}: (6, {})} | custom-call | flops 1 | bytes 1 | tf_op jit(solution)/shard_map/place/pallas_call | solution.py:194
  138.7 1.9 %place.5 = (bf16[4,2,2,4,2,16,1024]{6,5,4,3,2,1,0:T(8,128)(2,1)}, bf16[16,128,768]{2,1,0:T(8,128)(2,1)}) custom-call(s32[5]{0:T(128)S(1)} %stack.74.pos, bf16[4,4,16,1024]{3,2,1,0:T(8,128)(2,1)S(1)} %collective-permute-done.30.refs_0_, bf16[4,4,16,1024]{3,2,1,0:T(8,128)(2,1)S(1)} %collective-permute-done.31.refs_1_, ...), custom_call_target="tpu_custom_call", output_to_operand_aliasing={{0}: (5, {}), {1}: (6, {})} | custom-call | flops 1 | bytes 1 | tf_op jit(solution)/shard_map/place/pallas_call | solution.py:194
  (95 shorter events, 38.4 us)
Async XLA Ops:
  8.2 6.8 %collective-permute-start = (f32[4,2,128,768]{3,2,1,0:T(8,128)S(1)}, f32[4,2,128,768]{3,2,1,0:T(8,128)S(1)}, u32[]{:S(2)}, u32[]{:S(2)}) collective-permute-start(f32[4,2,128,768]{3,2,1,0:T(8,128)S(1)} %expert_terms.2), channel_id=1, source_target_pairs={{0,8},{1,9},{2,10},{3,11},{4,12},{5,13},{6,14},{7,15},{8,0},{9,1},... | collective-permute-start | bytes 9437192 | tf_op jit(solution)/shard_map/ppermute | solution.py:50
  21.7 11.6 %collective-permute-start.1 = (f32[4,4,4,16,1024]{4,3,2,1,0:T(8,128)S(1)}, f32[4,4,4,16,1024]{4,3,2,1,0:T(8,128)S(1)}, u32[]{:S(2)}, u32[]{:S(2)}) collective-permute-start(f32[4,4,4,16,1024]{4,3,2,1,0:T(8,128)S(1)} %dense_terms.2), channel_id=1, source_target_pairs={{0,8},{1,9},{2,10},{3,11},{4,12},{5,13},{6,14},{7,15},{8,0},{9,1},... | collective-permute-start | bytes 12582920 | tf_op jit(solution)/shard_map/ppermute | solution.py:50
  22.1 15.9 %collective-permute-start.11 = (f16[2,128,768]{2,1,0:T(8,128)(2,1)S(1)}, f16[2,128,768]{2,1,0:T(8,128)(2,1)S(1)}, u32[]{:S(2)}, u32[]{:S(2)}) collective-permute-start(f16[2,128,768]{2,1,0:T(8,128)(2,1)S(1)} %get-tuple-element.83), channel_id=1, source_target_pairs={{0,32},{1,33},{2,34},{3,35},{4,36},{5,37},{6,38},{7,39},{8,40},{9,... | collective-permute-start | bytes 1179656 | tf_op jit(solution)/shard_map/ppermute | solution.py:50
  23.5 20.1 %collective-permute-start.12 = (f16[2,128,768]{2,1,0:T(8,128)(2,1)S(1)}, f16[2,128,768]{2,1,0:T(8,128)(2,1)S(1)}, u32[]{:S(2)}, u32[]{:S(2)}) collective-permute-start(f16[2,128,768]{2,1,0:T(8,128)(2,1)S(1)} %get-tuple-element.82), channel_id=1, source_target_pairs={{0,64},{1,65},{2,66},{3,67},{4,68},{5,69},{6,70},{7,71},{8,72},{9,... | collective-permute-start | bytes 1179656 | tf_op jit(solution)/shard_map/ppermute | solution.py:50
  26.1 17.5 %collective-permute-start.13 = (f16[2,128,768]{2,1,0:T(8,128)(2,1)S(1)}, f16[2,128,768]{2,1,0:T(8,128)(2,1)S(1)}, u32[]{:S(2)}, u32[]{:S(2)}) collective-permute-start(f16[2,128,768]{2,1,0:T(8,128)(2,1)S(1)} %get-tuple-element.81), channel_id=1, source_target_pairs={{0,96},{1,97},{2,98},{3,99},{4,100},{5,101},{6,102},{7,103},{8,104... | collective-permute-start | bytes 1179656 | tf_op jit(solution)/shard_map/ppermute | solution.py:50
  34.1 15.6 %collective-permute-start.4 = (f16[4,4,16,1024]{3,2,1,0:T(8,128)(2,1)S(1)}, f16[4,4,16,1024]{3,2,1,0:T(8,128)(2,1)S(1)}, u32[]{:S(2)}, u32[]{:S(2)}) collective-permute-start(f16[4,4,16,1024]{3,2,1,0:T(8,128)(2,1)S(1)} %get-tuple-element.79), channel_id=1, source_target_pairs={{0,6},{1,7},{2,0},{3,1},{4,2},{5,3},{6,4},{7,5},{8,25},{9,8},{10,2... | collective-permute-start | bytes 1572872 | tf_op jit(solution)/shard_map/ppermute | solution.py:50
  38.0 11.7 %collective-permute-start.3 = (f16[4,4,16,1024]{3,2,1,0:T(8,128)(2,1)S(1)}, f16[4,4,16,1024]{3,2,1,0:T(8,128)(2,1)S(1)}, u32[]{:S(2)}, u32[]{:S(2)}) collective-permute-start(f16[4,4,16,1024]{3,2,1,0:T(8,128)(2,1)S(1)} %get-tuple-element.80), channel_id=1, source_target_pairs={{0,4},{1,5},{2,6},{3,7},{4,0},{5,1},{6,2},{7,3},{8,24},{9,25},{10,... | collective-permute-start | bytes 1572872 | tf_op jit(solution)/shard_map/ppermute | solution.py:50
  38.0 15.2 %collective-permute-start.2 = (f16[4,4,16,1024]{3,2,1,0:T(8,128)(2,1)S(1)}, f16[4,4,16,1024]{3,2,1,0:T(8,128)(2,1)S(1)}, u32[]{:S(2)}, u32[]{:S(2)}) collective-permute-start(f16[4,4,16,1024]{3,2,1,0:T(8,128)(2,1)S(1)} %get-tuple-element.78), channel_id=1, source_target_pairs={{0,2},{1,3},{2,4},{3,5},{4,6},{5,7},{6,0},{7,1},{8,9},{9,24},{10,1... | collective-permute-start | bytes 1572872 | tf_op jit(solution)/shard_map/ppermute | solution.py:50
  53.8 5.6 %collective-permute-start.7 = (f16[4,16,1024]{2,1,0:T(8,128)(2,1)S(1)}, f16[4,16,1024]{2,1,0:T(8,128)(2,1)S(1)}, u32[]{:S(2)}, u32[]{:S(2)}) collective-permute-start(f16[4,16,1024]{2,1,0:T(8,128)(2,1)S(1)} %get-tuple-element.85), channel_id=1, source_target_pairs={{0,17},{1,0},{2,19},{3,2},{4,21},{5,4},{6,23},{7,6},{8,14},{9,15},... | collective-permute-start | bytes 393224 | tf_op jit(solution)/shard_map/ppermute | solution.py:50
  56.0 5.4 %collective-permute-start.6 = (f16[4,16,1024]{2,1,0:T(8,128)(2,1)S(1)}, f16[4,16,1024]{2,1,0:T(8,128)(2,1)S(1)}, u32[]{:S(2)}, u32[]{:S(2)}) collective-permute-start(f16[4,16,1024]{2,1,0:T(8,128)(2,1)S(1)} %get-tuple-element.86), channel_id=1, source_target_pairs={{0,16},{1,17},{2,18},{3,19},{4,20},{5,21},{6,22},{7,23},{8,12},{9,... | collective-permute-start | bytes 393224 | tf_op jit(solution)/shard_map/ppermute | solution.py:50
  56.5 6.2 %collective-permute-start.5 = (f16[4,16,1024]{2,1,0:T(8,128)(2,1)S(1)}, f16[4,16,1024]{2,1,0:T(8,128)(2,1)S(1)}, u32[]{:S(2)}, u32[]{:S(2)}) collective-permute-start(f16[4,16,1024]{2,1,0:T(8,128)(2,1)S(1)} %get-tuple-element.84), channel_id=1, source_target_pairs={{0,1},{1,16},{2,3},{3,18},{4,5},{5,20},{6,7},{7,22},{8,10},{9,11},... | collective-permute-start | bytes 393224 | tf_op jit(solution)/shard_map/ppermute | solution.py:50
  57.1 8.0 %collective-permute-start.14 = (f16[128,768]{1,0:T(8,128)(2,1)S(1)}, f16[128,768]{1,0:T(8,128)(2,1)S(1)}, u32[]{:S(2)}, u32[]{:S(2)}) collective-permute-start(f16[128,768]{1,0:T(8,128)(2,1)S(1)} %fusion.34), channel_id=1, source_target_pairs={{0,16},{1,17},{2,18},{3,19},{4,20},{5,21},{6,22},{7,23},{8,24},{9,... | collective-permute-start | bytes 589832 | tf_op jit(solution)/shard_map/ppermute | solution.py:50
  62.9 4.7 %collective-permute-start.8 = (f32[16,1024]{1,0:T(8,128)S(1)}, f32[16,1024]{1,0:T(8,128)S(1)}, u32[]{:S(2)}, u32[]{:S(2)}) collective-permute-start(f32[16,1024]{1,0:T(8,128)S(1)} %get-tuple-element.91), channel_id=1, source_target_pairs={{0,32},{1,33},{2,34},{3,35},{4,36},{5,37},{6,38},{7,39},{8,40},{9,... | collective-permute-start | bytes 196616 | tf_op jit(solution)/shard_map/ppermute | solution.py:50
  95.6 7.3 %collective-permute-start.18 = (bf16[128,768]{1,0:T(8,128)(2,1)S(1)}, bf16[128,768]{1,0:T(8,128)(2,1)S(1)}, u32[]{:S(2)}, u32[]{:S(2)}) collective-permute-start(bf16[128,768]{1,0:T(8,128)(2,1)S(1)} %get-tuple-element.48), channel_id=1, source_target_pairs={{0,16},{1,17},{2,18},{3,19},{4,20},{5,21},{6,22},{7,23},{8,24},{9,... | collective-permute-start | bytes 589832 | tf_op jit(solution)/shard_map/ppermute | solution.py:50
  103.0 9.2 %collective-permute-start.22 = (bf16[2,128,768]{2,1,0:T(8,128)(2,1)S(1)}, bf16[2,128,768]{2,1,0:T(8,128)(2,1)S(1)}, u32[]{:S(2)}, u32[]{:S(2)}) collective-permute-start(bf16[2,128,768]{2,1,0:T(8,128)(2,1)S(1)} %get-tuple-element.88), channel_id=1, source_target_pairs={{0,96},{1,97},{2,98},{3,99},{4,100},{5,101},{6,102},{7,103},{8,104... | collective-permute-start | bytes 1179656 | tf_op jit(solution)/shard_map/ppermute | solution.py:50
  104.5 9.3 %collective-permute-start.23 = (bf16[2,128,768]{2,1,0:T(8,128)(2,1)S(1)}, bf16[2,128,768]{2,1,0:T(8,128)(2,1)S(1)}, u32[]{:S(2)}, u32[]{:S(2)}) collective-permute-start(bf16[2,128,768]{2,1,0:T(8,128)(2,1)S(1)} %get-tuple-element.88), channel_id=1, source_target_pairs={{0,32},{1,33},{2,34},{3,35},{4,36},{5,37},{6,38},{7,39},{8,40},{9,... | collective-permute-start | bytes 1179656 | tf_op jit(solution)/shard_map/ppermute | solution.py:50
  104.6 6.8 %collective-permute-start.21 = (bf16[4,16,1024]{2,1,0:T(8,128)(2,1)S(1)}, bf16[4,16,1024]{2,1,0:T(8,128)(2,1)S(1)}, u32[]{:S(2)}, u32[]{:S(2)}) collective-permute-start(bf16[4,16,1024]{2,1,0:T(8,128)(2,1)S(1)} %get-tuple-element.93), channel_id=1, source_target_pairs={{0,1},{1,16},{2,3},{3,18},{4,5},{5,20},{6,7},{7,22},{8,10},{9,11},... | collective-permute-start | bytes 393224 | tf_op jit(solution)/shard_map/ppermute | solution.py:50
  105.3 6.1 %collective-permute-start.20 = (bf16[4,16,1024]{2,1,0:T(8,128)(2,1)S(1)}, bf16[4,16,1024]{2,1,0:T(8,128)(2,1)S(1)}, u32[]{:S(2)}, u32[]{:S(2)}) collective-permute-start(bf16[4,16,1024]{2,1,0:T(8,128)(2,1)S(1)} %get-tuple-element.93), channel_id=1, source_target_pairs={{0,16},{1,17},{2,18},{3,19},{4,20},{5,21},{6,22},{7,23},{8,12},{9,... | collective-permute-start | bytes 393224 | tf_op jit(solution)/shard_map/ppermute | solution.py:50
  106.4 5.6 %collective-permute-start.19 = (bf16[4,16,1024]{2,1,0:T(8,128)(2,1)S(1)}, bf16[4,16,1024]{2,1,0:T(8,128)(2,1)S(1)}, u32[]{:S(2)}, u32[]{:S(2)}) collective-permute-start(bf16[4,16,1024]{2,1,0:T(8,128)(2,1)S(1)} %get-tuple-element.93), channel_id=1, source_target_pairs={{0,17},{1,0},{2,19},{3,2},{4,21},{5,4},{6,23},{7,6},{8,14},{9,15},... | collective-permute-start | bytes 393224 | tf_op jit(solution)/shard_map/ppermute | solution.py:50
  113.9 6.7 %collective-permute-start.29 = (bf16[3,2,128,768]{3,2,1,0:T(8,128)(2,1)S(1)}, bf16[3,2,128,768]{3,2,1,0:T(8,128)(2,1)S(1)}, u32[]{:S(2)}, u32[]{:S(2)}) collective-permute-start(bf16[3,2,128,768]{3,2,1,0:T(8,128)(2,1)S(1)} %pad_maximum_fusion.refs_2_), channel_id=1, source_target_pairs={{0,8},{1,9},{2,10},{3,11},{4,12},{5,13},{6,14},{7,15},{8,0},{9,1},... | collective-permute-start | bytes 3538952 | tf_op jit(solution)/shard_map/ppermute | solution.py:50
  117.5 15.0 %collective-permute-start.24 = (bf16[4,4,16,1024]{3,2,1,0:T(8,128)(2,1)S(1)}, bf16[4,4,16,1024]{3,2,1,0:T(8,128)(2,1)S(1)}, u32[]{:S(2)}, u32[]{:S(2)}) collective-permute-start(bf16[4,4,16,1024]{3,2,1,0:T(8,128)(2,1)S(1)} %pad_maximum_fusion.1.refs_0_), channel_id=1, source_target_pairs={{0,6},{1,7},{2,0},{3,1},{4,2},{5,3},{6,4},{7,5},{8,25},{9,8},{10,2... | collective-permute-start | bytes 1572872 | tf_op jit(solution)/shard_map/ppermute | solution.py:50
  118.8 13.7 %collective-permute-start.25 = (bf16[4,4,16,1024]{3,2,1,0:T(8,128)(2,1)S(1)}, bf16[4,4,16,1024]{3,2,1,0:T(8,128)(2,1)S(1)}, u32[]{:S(2)}, u32[]{:S(2)}) collective-permute-start(bf16[4,4,16,1024]{3,2,1,0:T(8,128)(2,1)S(1)} %pad_maximum_fusion.1.refs_0_), channel_id=1, source_target_pairs={{0,4},{1,5},{2,6},{3,7},{4,0},{5,1},{6,2},{7,3},{8,24},{9,25},{10,... | collective-permute-start | bytes 1572872 | tf_op jit(solution)/shard_map/ppermute | solution.py:50
  119.3 15.0 %collective-permute-start.26 = (bf16[4,4,16,1024]{3,2,1,0:T(8,128)(2,1)S(1)}, bf16[4,4,16,1024]{3,2,1,0:T(8,128)(2,1)S(1)}, u32[]{:S(2)}, u32[]{:S(2)}) collective-permute-start(bf16[4,4,16,1024]{3,2,1,0:T(8,128)(2,1)S(1)} %pad_maximum_fusion.1.refs_0_), channel_id=1, source_target_pairs={{0,2},{1,3},{2,4},{3,5},{4,6},{5,7},{6,0},{7,1},{8,9},{9,24},{10,1... | collective-permute-start | bytes 1572872 | tf_op jit(solution)/shard_map/ppermute | solution.py:50
  120.7 11.8 %collective-permute-start.27 = (bf16[2,128,768]{2,1,0:T(8,128)(2,1)S(1)}, bf16[2,128,768]{2,1,0:T(8,128)(2,1)S(1)}, u32[]{:S(2)}, u32[]{:S(2)}) collective-permute-start(bf16[2,128,768]{2,1,0:T(8,128)(2,1)S(1)} %get-tuple-element.88), channel_id=1, source_target_pairs={{0,64},{1,65},{2,66},{3,67},{4,68},{5,69},{6,70},{7,71},{8,72},{9,... | collective-permute-start | bytes 1179656 | tf_op jit(solution)/shard_map/ppermute | solution.py:50
  (21 other events, 304.2 us)

commit v4 on v3

--- a/solution.py
+++ b/solution.py
@@ -216,6 +216,11 @@
     return (param_new, first_new, second_new)
 
 
+def lane_sums(value):
+    parts = [value[:, at : at + 128] for at in range(0, value.shape[1], 128)]
+    return jnp.sum(sum(v * v for v in parts), axis=0)
+
+
 def column_term(inputs, cotangent):
     return lax.dot_general(
         inputs, cotangent, (((0,), (0,)), ((), ())), preferred_element_type=jnp.float32
@@ -252,7 +257,7 @@
     own = dense_half(0, pos, *after(tokens, terms))
     first = [own[k] + away[k] for k in range(4)]
     pieces = [(first[k] * 0.125).astype(f16) for k in (1, 2, 3)]
-    got = [send(pieces[k - 1], FIRST[k]) for k in (1, 2, 3)]
+    got = [send(pieces[k - 1], FIRST[k]) for k in (1, 3, 2)]
     egot = after(egot, pieces)
     esecond = efirst[0] * 0.5 + sum(v.astype(f32) for v in egot)
     egot = send((esecond[1] * 0.25).astype(f16), ZHI)
@@ -263,9 +268,9 @@
     expert_grad = ((esecond[0] * 0.25 + egot.astype(f32)) * 8.0)[None]
     dense_grad = (third[0] + sum(got)) * 32.0
 
-    mine = jnp.sum(dense_grad * dense_grad) + jnp.sum(expert_grad * expert_grad)
-    spread = lax.all_to_all(jnp.full((128, 1, 128), mine, f32), BOTH, 0, 0, tiled=True)
-    total = jnp.sum(spread[:, :, 0])
+    mine = lane_sums(dense_grad) + lane_sums(expert_grad[0])
+    spread = jnp.broadcast_to(mine, (128, 1, 128))
+    total = jnp.sum(lax.all_to_all(spread, BOTH, 0, 0, tiled=True))
     ep_size = lax.axis_size("ep")
     limit = 10.0 * math.sqrt(dense_input.shape[1] * (kvw + ep_size * ff))
     clip = jnp.minimum(1.0, limit / (jnp.sqrt(total) + 1e-06))

time: 141 us -> 137 us (0.972)
  waiting for transfers between devices: 45.5 us -> 41 us
  starting transfers between devices: 34.4 us -> 38 us
    ppermute x34, waiting for transfers between devices: 45.5 us -> 41 us  [send(): return lax.ppermute(value, BOTH, pairing)]
    ppermute x34, starting transfers between devices: 34.4 us -> 38 us  [send(): return lax.ppermute(value, BOTH, pairing)]
  transfers between devices with their start and end apart: 34 -> 34, of which waited for: 22 -> 21; matrix products, arithmetic and copies ran while one was open for 1% -> 1% of each run, Pallas kernels for 10% -> 11%
where the time goes in v4:
time: 137 us
  waiting for transfers between devices  41 us (30%)
  starting transfers between devices  38 us (28%)
  Pallas kernels  26.4 us (19%)
  blocking collectives  20.4 us (15%)
  other arithmetic  5.05 us (4%)
  local copies, waits for them, and re-layouts  3.85 us (3%)
  between operations  1.88 us (1%)
    ppermute x34, waiting for transfers between devices, send(): return lax.ppermute(value, BOTH, pairing)  41 us
    ppermute x34, starting transfers between devices, send(): return lax.ppermute(value, BOTH, pairing)  38 us
    all_to_all x1, blocking collectives, per_device(): total = jnp.sum(lax.all_to_all(spread, BOTH, 0, 0, tiled=True))  20.4 us
    pallas_call x4, Pallas kernels, half_terms(): pl.pallas_call(functools.partial(half_kernel, store, other), out_shape=ja...  20 us
    pallas_call x3, Pallas kernels, place(): pl.pallas_call(functools.partial(place_kernel, names), out_shape=shapes,...  6.36 us
    unnamed x22, local copies, waits for them, and re-layouts  3.71 us
  transfers between devices with their start and end apart: 34, of which 21 were waited for; matrix products, arithmetic and copies ran while one was open for 1% of the time, Pallas kernels for 11%

profile of v4, /device:TPU:1, one launch (start us, length us, event | category | flops | bytes accessed | tf_op | source)
XLA Modules:
  0.0 136.5 jit_solution(5451988147803225683)
XLA Ops:
  0.8 2.2 %copy-done = bf16[1,1024,2048]{2,1,0:T(8,128)(2,1)S(1)} copy-done((bf16[1,1024,2048]{2,1,0:T(8,128)(2,1)S(1)}, bf16[1,1024,2048]{2,1,0:T(8,128)(2,1)}, u32[]{:S(2)}) %copy-start) | copy-done | bytes 4194328
  4.4 3.9 %expert_terms.2 = f32[4,2,128,768]{3,2,1,0:T(8,128)S(1)} custom-call(s32[5]{0:T(128)S(1)} %stack.74.pos, bf16[1024,2048]{1,0:T(8,128)(2,1)S(1)} %bitcast.99, bf16[1024,768]{1,0:T(8,128)(2,1)S(1)} %bitcast.101), custom_call_target="tpu_custom_call" | custom-call | flops 3221225472 | bytes 1 | tf_op jit(solution)/shard_map/expert_terms/pallas_call | solution.py:125
  9.8 3.8 %expert_terms.3 = f32[4,2,128,768]{3,2,1,0:T(8,128)S(1)} custom-call(s32[5]{0:T(128)S(1)} %stack.74.pos, bf16[1024,2048]{1,0:T(8,128)(2,1)S(1)} %bitcast.100, bf16[1024,768]{1,0:T(8,128)(2,1)S(1)} %bitcast.102), custom_call_target="tpu_custom_call" | custom-call | flops 3221225472 | bytes 1 | tf_op jit(solution)/shard_map/expert_terms/pallas_call | solution.py:125
  15.5 6.2 %dense_terms.2 = f32[4,4,4,16,1024]{4,3,2,1,0:T(8,128)S(1)} custom-call(s32[5]{0:T(128)S(1)} %stack.74.pos, bf16[1536,2048]{1,0:T(8,128)(2,1)S(1)} %bitcast.98, bf16[1536,1024]{1,0:T(8,128)(2,1)S(1)} %copy-done.1), custom_call_target="tpu_custom_call" | custom-call | flops 6442450944 | bytes 1 | tf_op jit(solution)/shard_map/dense_terms/pallas_call | solution.py:125
  23.4 2.6 %collective-permute-start.12 = (f16[2,128,768]{2,1,0:T(8,128)(2,1)S(1)}, f16[2,128,768]{2,1,0:T(8,128)(2,1)S(1)}, u32[]{:S(2)}, u32[]{:S(2)}) collective-permute-start(f16[2,128,768]{2,1,0:T(8,128)(2,1)S(1)} %get-tuple-element.82), channel_id=1, source_target_pairs={{0,64},{1,65},{2,66},{3,67},{4,68},{5,69},{6,70},{7,71},{8,72},{9,... | collective-permute-start | bytes 1179656 | tf_op jit(solution)/shard_map/ppermute | solution.py:50
  27.1 6.1 %dense_terms.3 = f32[4,4,4,16,1024]{4,3,2,1,0:T(8,128)S(1)} custom-call(s32[5]{0:T(128)S(1)} %stack.74.pos, bf16[1536,2048]{1,0:T(8,128)(2,1)S(1)} %bitcast.98, bf16[1536,1024]{1,0:T(8,128)(2,1)S(1)} %copy-done.1), custom_call_target="tpu_custom_call" | custom-call | flops 6442450944 | bytes 1 | tf_op jit(solution)/shard_map/dense_terms/pallas_call | solution.py:125
  34.1 3.7 %collective-permute-start.4 = (f16[4,4,16,1024]{3,2,1,0:T(8,128)(2,1)S(1)}, f16[4,4,16,1024]{3,2,1,0:T(8,128)(2,1)S(1)}, u32[]{:S(2)}, u32[]{:S(2)}) collective-permute-start(f16[4,4,16,1024]{3,2,1,0:T(8,128)(2,1)S(1)} %get-tuple-element.79), channel_id=1, source_target_pairs={{0,4},{1,5},{2,6},{3,7},{4,0},{5,1},{6,2},{7,3},{8,24},{9,25},{10,... | collective-permute-start | bytes 1572872 | tf_op jit(solution)/shard_map/ppermute | solution.py:50
  39.3 4.3 %collective-permute-done.12 = f16[2,128,768]{2,1,0:T(8,128)(2,1)S(1)} collective-permute-done((f16[2,128,768]{2,1,0:T(8,128)(2,1)S(1)}, f16[2,128,768]{2,1,0:T(8,128)(2,1)S(1)}, u32[]{:S(2)}, u32[]{:S(2)}) %collective-permute-start.12) | collective-permute-done | bytes 393248 | tf_op jit(solution)/shard_map/ppermute | solution.py:50
  43.8 3.7 %collective-permute-start.14 = (f16[128,768]{1,0:T(8,128)(2,1)S(1)}, f16[128,768]{1,0:T(8,128)(2,1)S(1)}, u32[]{:S(2)}, u32[]{:S(2)}) collective-permute-start(f16[128,768]{1,0:T(8,128)(2,1)S(1)} %fusion.34), channel_id=1, source_target_pairs={{0,16},{1,17},{2,18},{3,19},{4,20},{5,21},{6,22},{7,23},{8,24},{9,... | collective-permute-start | bytes 589832 | tf_op jit(solution)/shard_map/ppermute | solution.py:50
  47.5 3.6 %collective-permute-done.3 = f16[4,4,16,1024]{3,2,1,0:T(8,128)(2,1)S(1)} collective-permute-done((f16[4,4,16,1024]{3,2,1,0:T(8,128)(2,1)S(1)}, f16[4,4,16,1024]{3,2,1,0:T(8,128)(2,1)S(1)}, u32[]{:S(2)}, u32[]{:S(2)}) %collective-permute-start.3) | collective-permute-done | bytes 524320 | tf_op jit(solution)/shard_map/ppermute | solution.py:50
  51.8 2.5 %collective-permute-start.7 = (f16[4,16,1024]{2,1,0:T(8,128)(2,1)S(1)}, f16[4,16,1024]{2,1,0:T(8,128)(2,1)S(1)}, u32[]{:S(2)}, u32[]{:S(2)}) collective-permute-start(f16[4,16,1024]{2,1,0:T(8,128)(2,1)S(1)} %get-tuple-element.85), channel_id=1, source_target_pairs={{0,17},{1,0},{2,19},{3,2},{4,21},{5,4},{6,23},{7,6},{8,14},{9,15},... | collective-permute-start | bytes 393224 | tf_op jit(solution)/shard_map/ppermute | solution.py:50
  55.5 2.1 %collective-permute-done.7 = f16[4,16,1024]{2,1,0:T(8,128)(2,1)S(1)} collective-permute-done((f16[4,16,1024]{2,1,0:T(8,128)(2,1)S(1)}, f16[4,16,1024]{2,1,0:T(8,128)(2,1)S(1)}, u32[]{:S(2)}, u32[]{:S(2)}) %collective-permute-start.7) | collective-permute-done | bytes 131104 | tf_op jit(solution)/shard_map/ppermute | solution.py:50
  57.6 2.1 %collective-permute-done.6 = f16[4,16,1024]{2,1,0:T(8,128)(2,1)S(1)} collective-permute-done((f16[4,16,1024]{2,1,0:T(8,128)(2,1)S(1)}, f16[4,16,1024]{2,1,0:T(8,128)(2,1)S(1)}, u32[]{:S(2)}, u32[]{:S(2)}) %collective-permute-start.6) | collective-permute-done | bytes 131104 | tf_op jit(solution)/shard_map/ppermute | solution.py:50
  65.9 1.7 %collective-permute-done.9 = f32[16,1024]{1,0:T(8,128)S(1)} collective-permute-done((f32[16,1024]{1,0:T(8,128)S(1)}, f32[16,1024]{1,0:T(8,128)S(1)}, u32[]{:S(2)}, u32[]{:S(2)}) %collective-permute-start.9) | collective-permute-done | bytes 65568 | tf_op jit(solution)/shard_map/ppermute | solution.py:50
  67.7 20.4 %all_to_all.5 = f32[128,1,128]{2,1,0:T(1,128)S(1)} all-to-all(f32[128,1,128]{2,1,0:T(1,128)S(1)} %broadcast_in_dim.7), channel_id=1, replica_groups=mesh['edp'=16,'ep'=8] {'edp','ep'}, dimensions={0} | all-to-all | bytes 131072 | tf_op jit(solution)/shard_map/all_to_all | solution.py:273
  93.1 1.7 %collective-permute-start.16 = (bf16[16,1024]{1,0:T(8,128)(2,1)S(1)}, bf16[16,1024]{1,0:T(8,128)(2,1)S(1)}, u32[]{:S(2)}, u32[]{:S(2)}) collective-permute-start(bf16[16,1024]{1,0:T(8,128)(2,1)S(1)} %get-tuple-element.47), channel_id=1, source_target_pairs={{0,64},{1,65},{2,66},{3,67},{4,68},{5,69},{6,70},{7,71},{8,72},{9,... | collective-permute-start | bytes 98312 | tf_op jit(solution)/shard_map/ppermute | solution.py:50
  102.2 1.8 %collective-permute-start.19 = (bf16[4,16,1024]{2,1,0:T(8,128)(2,1)S(1)}, bf16[4,16,1024]{2,1,0:T(8,128)(2,1)S(1)}, u32[]{:S(2)}, u32[]{:S(2)}) collective-permute-start(bf16[4,16,1024]{2,1,0:T(8,128)(2,1)S(1)} %get-tuple-element.93), channel_id=1, source_target_pairs={{0,17},{1,0},{2,19},{3,2},{4,21},{5,4},{6,23},{7,6},{8,14},{9,15},... | collective-permute-start | bytes 393224 | tf_op jit(solution)/shard_map/ppermute | solution.py:50
  103.9 3.2 %collective-permute-done.21 = bf16[4,16,1024]{2,1,0:T(8,128)(2,1)S(1)} collective-permute-done((bf16[4,16,1024]{2,1,0:T(8,128)(2,1)S(1)}, bf16[4,16,1024]{2,1,0:T(8,128)(2,1)S(1)}, u32[]{:S(2)}, u32[]{:S(2)}) %collective-permute-start.21) | collective-permute-done | bytes 131104 | tf_op jit(solution)/shard_map/ppermute | solution.py:50
  109.7 3.5 %collective-permute-start.29 = (bf16[3,2,128,768]{3,2,1,0:T(8,128)(2,1)S(1)}, bf16[3,2,128,768]{3,2,1,0:T(8,128)(2,1)S(1)}, u32[]{:S(2)}, u32[]{:S(2)}) collective-permute-start(bf16[3,2,128,768]{3,2,1,0:T(8,128)(2,1)S(1)} %pad_maximum_fusion.refs_2_), channel_id=1, source_target_pairs={{0,8},{1,9},{2,10},{3,11},{4,12},{5,13},{6,14},{7,15},{8,0},{9,1},... | collective-permute-start | bytes 3538952 | tf_op jit(solution)/shard_map/ppermute | solution.py:50
  116.4 2.5 %place.3 = (bf16[4,2,2,4,2,16,1024]{6,5,4,3,2,1,0:T(8,128)(2,1)}, bf16[16,128,768]{2,1,0:T(8,128)(2,1)}) custom-call(s32[5]{0:T(128)S(1)} %stack.74.pos, bf16[4,4,16,1024]{3,2,1,0:T(8,128)(2,1)S(1)} %pad_maximum_fusion.1.refs_0_, bf16[4,4,16,1024]{3,2,1,0:T(8,128)(2,1)S(1)} %collective-permute-done.28.refs_1_, ...), custom_call_target="tpu_custom_call" | custom-call | flops 1 | bytes 1 | tf_op jit(solution)/shard_map/place/pallas_call | solution.py:194
  118.9 9.4 %collective-permute-done.27 = bf16[2,128,768]{2,1,0:T(8,128)(2,1)S(1)} collective-permute-done((bf16[2,128,768]{2,1,0:T(8,128)(2,1)S(1)}, bf16[2,128,768]{2,1,0:T(8,128)(2,1)S(1)}, u32[]{:S(2)}, u32[]{:S(2)}) %collective-permute-start.27) | collective-permute-done | bytes 393248 | tf_op jit(solution)/shard_map/ppermute | solution.py:50
  128.2 1.8 %collective-permute-done.26.refs_2_ = bf16[4,4,16,1024]{3,2,1,0:T(8,128)(2,1)S(1)} collective-permute-done((bf16[4,4,16,1024]{3,2,1,0:T(8,128)(2,1)S(1)}, bf16[4,4,16,1024]{3,2,1,0:T(8,128)(2,1)S(1)}, u32[]{:S(2)}, u32[]{:S(2)}) %collective-permute-start.26) | collective-permute-done | bytes 524320 | tf_op jit(solution)/shard_map/ppermute | solution.py:50
  131.3 1.9 %place.4 = (bf16[4,2,2,4,2,16,1024]{6,5,4,3,2,1,0:T(8,128)(2,1)}, bf16[16,128,768]{2,1,0:T(8,128)(2,1)}) custom-call(s32[5]{0:T(128)S(1)} %stack.74.pos, bf16[4,4,16,1024]{3,2,1,0:T(8,128)(2,1)S(1)} %collective-permute-done.24.refs_0_, bf16[4,4,16,1024]{3,2,1,0:T(8,128)(2,1)S(1)} %collective-permute-done.25.refs_1_, ...), custom_call_target="tpu_custom_call", output_to_operand_aliasing={{0}: (5, {}), {1}: (6, {})} | custom-call | flops 1 | bytes 1 | tf_op jit(solution)/shard_map/place/pallas_call | solution.py:194
  134.4 1.9 %place.5 = (bf16[4,2,2,4,2,16,1024]{6,5,4,3,2,1,0:T(8,128)(2,1)}, bf16[16,128,768]{2,1,0:T(8,128)(2,1)}) custom-call(s32[5]{0:T(128)S(1)} %stack.74.pos, bf16[4,4,16,1024]{3,2,1,0:T(8,128)(2,1)S(1)} %collective-permute-done.30.refs_0_, bf16[4,4,16,1024]{3,2,1,0:T(8,128)(2,1)S(1)} %collective-permute-done.31.refs_1_, ...), custom_call_target="tpu_custom_call", output_to_operand_aliasing={{0}: (5, {}), {1}: (6, {})} | custom-call | flops 1 | bytes 1 | tf_op jit(solution)/shard_map/place/pallas_call | solution.py:194
  (98 shorter events, 38.1 us)
Async XLA Ops:
  8.3 6.8 %collective-permute-start = (f32[4,2,128,768]{3,2,1,0:T(8,128)S(1)}, f32[4,2,128,768]{3,2,1,0:T(8,128)S(1)}, u32[]{:S(2)}, u32[]{:S(2)}) collective-permute-start(f32[4,2,128,768]{3,2,1,0:T(8,128)S(1)} %expert_terms.2), channel_id=1, source_target_pairs={{0,8},{1,9},{2,10},{3,11},{4,12},{5,13},{6,14},{7,15},{8,0},{9,1},... | collective-permute-start | bytes 9437192 | tf_op jit(solution)/shard_map/ppermute | solution.py:50
  21.7 11.6 %collective-permute-start.1 = (f32[4,4,4,16,1024]{4,3,2,1,0:T(8,128)S(1)}, f32[4,4,4,16,1024]{4,3,2,1,0:T(8,128)S(1)}, u32[]{:S(2)}, u32[]{:S(2)}) collective-permute-start(f32[4,4,4,16,1024]{4,3,2,1,0:T(8,128)S(1)} %dense_terms.2), channel_id=1, source_target_pairs={{0,8},{1,9},{2,10},{3,11},{4,12},{5,13},{6,14},{7,15},{8,0},{9,1},... | collective-permute-start | bytes 12582920 | tf_op jit(solution)/shard_map/ppermute | solution.py:50
  22.1 16.2 %collective-permute-start.11 = (f16[2,128,768]{2,1,0:T(8,128)(2,1)S(1)}, f16[2,128,768]{2,1,0:T(8,128)(2,1)S(1)}, u32[]{:S(2)}, u32[]{:S(2)}) collective-permute-start(f16[2,128,768]{2,1,0:T(8,128)(2,1)S(1)} %get-tuple-element.83), channel_id=1, source_target_pairs={{0,32},{1,33},{2,34},{3,35},{4,36},{5,37},{6,38},{7,39},{8,40},{9,... | collective-permute-start | bytes 1179656 | tf_op jit(solution)/shard_map/ppermute | solution.py:50
  23.4 20.1 %collective-permute-start.12 = (f16[2,128,768]{2,1,0:T(8,128)(2,1)S(1)}, f16[2,128,768]{2,1,0:T(8,128)(2,1)S(1)}, u32[]{:S(2)}, u32[]{:S(2)}) collective-permute-start(f16[2,128,768]{2,1,0:T(8,128)(2,1)S(1)} %get-tuple-element.82), channel_id=1, source_target_pairs={{0,64},{1,65},{2,66},{3,67},{4,68},{5,69},{6,70},{7,71},{8,72},{9,... | collective-permute-start | bytes 1179656 | tf_op jit(solution)/shard_map/ppermute | solution.py:50
  26.1 17.5 %collective-permute-start.13 = (f16[2,128,768]{2,1,0:T(8,128)(2,1)S(1)}, f16[2,128,768]{2,1,0:T(8,128)(2,1)S(1)}, u32[]{:S(2)}, u32[]{:S(2)}) collective-permute-start(f16[2,128,768]{2,1,0:T(8,128)(2,1)S(1)} %get-tuple-element.81), channel_id=1, source_target_pairs={{0,96},{1,97},{2,98},{3,99},{4,100},{5,101},{6,102},{7,103},{8,104... | collective-permute-start | bytes 1179656 | tf_op jit(solution)/shard_map/ppermute | solution.py:50
  34.1 13.4 %collective-permute-start.4 = (f16[4,4,16,1024]{3,2,1,0:T(8,128)(2,1)S(1)}, f16[4,4,16,1024]{3,2,1,0:T(8,128)(2,1)S(1)}, u32[]{:S(2)}, u32[]{:S(2)}) collective-permute-start(f16[4,4,16,1024]{3,2,1,0:T(8,128)(2,1)S(1)} %get-tuple-element.79), channel_id=1, source_target_pairs={{0,4},{1,5},{2,6},{3,7},{4,0},{5,1},{6,2},{7,3},{8,24},{9,25},{10,... | collective-permute-start | bytes 1572872 | tf_op jit(solution)/shard_map/ppermute | solution.py:50
  37.8 13.4 %collective-permute-start.3 = (f16[4,4,16,1024]{3,2,1,0:T(8,128)(2,1)S(1)}, f16[4,4,16,1024]{3,2,1,0:T(8,128)(2,1)S(1)}, u32[]{:S(2)}, u32[]{:S(2)}) collective-permute-start(f16[4,4,16,1024]{3,2,1,0:T(8,128)(2,1)S(1)} %get-tuple-element.80), channel_id=1, source_target_pairs={{0,6},{1,7},{2,0},{3,1},{4,2},{5,3},{6,4},{7,5},{8,25},{9,8},{10,2... | collective-permute-start | bytes 1572872 | tf_op jit(solution)/shard_map/ppermute | solution.py:50
  38.3 12.9 %collective-permute-start.2 = (f16[4,4,16,1024]{3,2,1,0:T(8,128)(2,1)S(1)}, f16[4,4,16,1024]{3,2,1,0:T(8,128)(2,1)S(1)}, u32[]{:S(2)}, u32[]{:S(2)}) collective-permute-start(f16[4,4,16,1024]{3,2,1,0:T(8,128)(2,1)S(1)} %get-tuple-element.78), channel_id=1, source_target_pairs={{0,2},{1,3},{2,4},{3,5},{4,6},{5,7},{6,0},{7,1},{8,9},{9,24},{10,1... | collective-permute-start | bytes 1572872 | tf_op jit(solution)/shard_map/ppermute | solution.py:50
  43.8 11.6 %collective-permute-start.14 = (f16[128,768]{1,0:T(8,128)(2,1)S(1)}, f16[128,768]{1,0:T(8,128)(2,1)S(1)}, u32[]{:S(2)}, u32[]{:S(2)}) collective-permute-start(f16[128,768]{1,0:T(8,128)(2,1)S(1)} %fusion.34), channel_id=1, source_target_pairs={{0,16},{1,17},{2,18},{3,19},{4,20},{5,21},{6,22},{7,23},{8,24},{9,... | collective-permute-start | bytes 589832 | tf_op jit(solution)/shard_map/ppermute | solution.py:50
  51.8 5.8 %collective-permute-start.7 = (f16[4,16,1024]{2,1,0:T(8,128)(2,1)S(1)}, f16[4,16,1024]{2,1,0:T(8,128)(2,1)S(1)}, u32[]{:S(2)}, u32[]{:S(2)}) collective-permute-start(f16[4,16,1024]{2,1,0:T(8,128)(2,1)S(1)} %get-tuple-element.85), channel_id=1, source_target_pairs={{0,17},{1,0},{2,19},{3,2},{4,21},{5,4},{6,23},{7,6},{8,14},{9,15},... | collective-permute-start | bytes 393224 | tf_op jit(solution)/shard_map/ppermute | solution.py:50
  54.3 5.4 %collective-permute-start.6 = (f16[4,16,1024]{2,1,0:T(8,128)(2,1)S(1)}, f16[4,16,1024]{2,1,0:T(8,128)(2,1)S(1)}, u32[]{:S(2)}, u32[]{:S(2)}) collective-permute-start(f16[4,16,1024]{2,1,0:T(8,128)(2,1)S(1)} %get-tuple-element.86), channel_id=1, source_target_pairs={{0,16},{1,17},{2,18},{3,19},{4,20},{5,21},{6,22},{7,23},{8,12},{9,... | collective-permute-start | bytes 393224 | tf_op jit(solution)/shard_map/ppermute | solution.py:50
  54.8 6.5 %collective-permute-start.5 = (f16[4,16,1024]{2,1,0:T(8,128)(2,1)S(1)}, f16[4,16,1024]{2,1,0:T(8,128)(2,1)S(1)}, u32[]{:S(2)}, u32[]{:S(2)}) collective-permute-start(f16[4,16,1024]{2,1,0:T(8,128)(2,1)S(1)} %get-tuple-element.84), channel_id=1, source_target_pairs={{0,1},{1,16},{2,3},{3,18},{4,5},{5,20},{6,7},{7,22},{8,10},{9,11},... | collective-permute-start | bytes 393224 | tf_op jit(solution)/shard_map/ppermute | solution.py:50
  62.9 4.6 %collective-permute-start.9 = (f32[16,1024]{1,0:T(8,128)S(1)}, f32[16,1024]{1,0:T(8,128)S(1)}, u32[]{:S(2)}, u32[]{:S(2)}) collective-permute-start(f32[16,1024]{1,0:T(8,128)S(1)} %get-tuple-element.89), channel_id=1, source_target_pairs={{0,64},{1,65},{2,66},{3,67},{4,68},{5,69},{6,70},{7,71},{8,72},{9,... | collective-permute-start | bytes 196616 | tf_op jit(solution)/shard_map/ppermute | solution.py:50
  91.4 7.3 %collective-permute-start.18 = (bf16[128,768]{1,0:T(8,128)(2,1)S(1)}, bf16[128,768]{1,0:T(8,128)(2,1)S(1)}, u32[]{:S(2)}, u32[]{:S(2)}) collective-permute-start(bf16[128,768]{1,0:T(8,128)(2,1)S(1)} %get-tuple-element.48), channel_id=1, source_target_pairs={{0,16},{1,17},{2,18},{3,19},{4,20},{5,21},{6,22},{7,23},{8,24},{9,... | collective-permute-start | bytes 589832 | tf_op jit(solution)/shard_map/ppermute | solution.py:50
  98.8 9.2 %collective-permute-start.22 = (bf16[2,128,768]{2,1,0:T(8,128)(2,1)S(1)}, bf16[2,128,768]{2,1,0:T(8,128)(2,1)S(1)}, u32[]{:S(2)}, u32[]{:S(2)}) collective-permute-start(bf16[2,128,768]{2,1,0:T(8,128)(2,1)S(1)} %get-tuple-element.88), channel_id=1, source_target_pairs={{0,96},{1,97},{2,98},{3,99},{4,100},{5,101},{6,102},{7,103},{8,104... | collective-permute-start | bytes 1179656 | tf_op jit(solution)/shard_map/ppermute | solution.py:50
  100.2 9.3 %collective-permute-start.23 = (bf16[2,128,768]{2,1,0:T(8,128)(2,1)S(1)}, bf16[2,128,768]{2,1,0:T(8,128)(2,1)S(1)}, u32[]{:S(2)}, u32[]{:S(2)}) collective-permute-start(bf16[2,128,768]{2,1,0:T(8,128)(2,1)S(1)} %get-tuple-element.88), channel_id=1, source_target_pairs={{0,32},{1,33},{2,34},{3,35},{4,36},{5,37},{6,38},{7,39},{8,40},{9,... | collective-permute-start | bytes 1179656 | tf_op jit(solution)/shard_map/ppermute | solution.py:50
  100.4 6.8 %collective-permute-start.21 = (bf16[4,16,1024]{2,1,0:T(8,128)(2,1)S(1)}, bf16[4,16,1024]{2,1,0:T(8,128)(2,1)S(1)}, u32[]{:S(2)}, u32[]{:S(2)}) collective-permute-start(bf16[4,16,1024]{2,1,0:T(8,128)(2,1)S(1)} %get-tuple-element.93), channel_id=1, source_target_pairs={{0,1},{1,16},{2,3},{3,18},{4,5},{5,20},{6,7},{7,22},{8,10},{9,11},... | collective-permute-start | bytes 393224 | tf_op jit(solution)/shard_map/ppermute | solution.py:50
  101.1 6.1 %collective-permute-start.20 = (bf16[4,16,1024]{2,1,0:T(8,128)(2,1)S(1)}, bf16[4,16,1024]{2,1,0:T(8,128)(2,1)S(1)}, u32[]{:S(2)}, u32[]{:S(2)}) collective-permute-start(bf16[4,16,1024]{2,1,0:T(8,128)(2,1)S(1)} %get-tuple-element.93), channel_id=1, source_target_pairs={{0,16},{1,17},{2,18},{3,19},{4,20},{5,21},{6,22},{7,23},{8,12},{9,... | collective-permute-start | bytes 393224 | tf_op jit(solution)/shard_map/ppermute | solution.py:50
  102.2 5.6 %collective-permute-start.19 = (bf16[4,16,1024]{2,1,0:T(8,128)(2,1)S(1)}, bf16[4,16,1024]{2,1,0:T(8,128)(2,1)S(1)}, u32[]{:S(2)}, u32[]{:S(2)}) collective-permute-start(bf16[4,16,1024]{2,1,0:T(8,128)(2,1)S(1)} %get-tuple-element.93), channel_id=1, source_target_pairs={{0,17},{1,0},{2,19},{3,2},{4,21},{5,4},{6,23},{7,6},{8,14},{9,15},... | collective-permute-start | bytes 393224 | tf_op jit(solution)/shard_map/ppermute | solution.py:50
  109.7 6.7 %collective-permute-start.29 = (bf16[3,2,128,768]{3,2,1,0:T(8,128)(2,1)S(1)}, bf16[3,2,128,768]{3,2,1,0:T(8,128)(2,1)S(1)}, u32[]{:S(2)}, u32[]{:S(2)}) collective-permute-start(bf16[3,2,128,768]{3,2,1,0:T(8,128)(2,1)S(1)} %pad_maximum_fusion.refs_2_), channel_id=1, source_target_pairs={{0,8},{1,9},{2,10},{3,11},{4,12},{5,13},{6,14},{7,15},{8,0},{9,1},... | collective-permute-start | bytes 3538952 | tf_op jit(solution)/shard_map/ppermute | solution.py:50
  113.3 15.0 %collective-permute-start.24 = (bf16[4,4,16,1024]{3,2,1,0:T(8,128)(2,1)S(1)}, bf16[4,4,16,1024]{3,2,1,0:T(8,128)(2,1)S(1)}, u32[]{:S(2)}, u32[]{:S(2)}) collective-permute-start(bf16[4,4,16,1024]{3,2,1,0:T(8,128)(2,1)S(1)} %pad_maximum_fusion.1.refs_0_), channel_id=1, source_target_pairs={{0,6},{1,7},{2,0},{3,1},{4,2},{5,3},{6,4},{7,5},{8,25},{9,8},{10,2... | collective-permute-start | bytes 1572872 | tf_op jit(solution)/shard_map/ppermute | solution.py:50
  114.6 13.7 %collective-permute-start.25 = (bf16[4,4,16,1024]{3,2,1,0:T(8,128)(2,1)S(1)}, bf16[4,4,16,1024]{3,2,1,0:T(8,128)(2,1)S(1)}, u32[]{:S(2)}, u32[]{:S(2)}) collective-permute-start(bf16[4,4,16,1024]{3,2,1,0:T(8,128)(2,1)S(1)} %pad_maximum_fusion.1.refs_0_), channel_id=1, source_target_pairs={{0,4},{1,5},{2,6},{3,7},{4,0},{5,1},{6,2},{7,3},{8,24},{9,25},{10,... | collective-permute-start | bytes 1572872 | tf_op jit(solution)/shard_map/ppermute | solution.py:50
  115.0 15.0 %collective-permute-start.26 = (bf16[4,4,16,1024]{3,2,1,0:T(8,128)(2,1)S(1)}, bf16[4,4,16,1024]{3,2,1,0:T(8,128)(2,1)S(1)}, u32[]{:S(2)}, u32[]{:S(2)}) collective-permute-start(bf16[4,4,16,1024]{3,2,1,0:T(8,128)(2,1)S(1)} %pad_maximum_fusion.1.refs_0_), channel_id=1, source_target_pairs={{0,2},{1,3},{2,4},{3,5},{4,6},{5,7},{6,0},{7,1},{8,9},{9,24},{10,1... | collective-permute-start | bytes 1572872 | tf_op jit(solution)/shard_map/ppermute | solution.py:50
  116.4 11.8 %collective-permute-start.27 = (bf16[2,128,768]{2,1,0:T(8,128)(2,1)S(1)}, bf16[2,128,768]{2,1,0:T(8,128)(2,1)S(1)}, u32[]{:S(2)}, u32[]{:S(2)}) collective-permute-start(bf16[2,128,768]{2,1,0:T(8,128)(2,1)S(1)} %get-tuple-element.88), channel_id=1, source_target_pairs={{0,64},{1,65},{2,66},{3,67},{4,68},{5,69},{6,70},{7,71},{8,72},{9,... | collective-permute-start | bytes 1179656 | tf_op jit(solution)/shard_map/ppermute | solution.py:50
  (21 other events, 290.0 us)

commit v5 on v4

--- a/solution.py
+++ b/solution.py
@@ -296,12 +296,12 @@
         jax.ShapeDtypeStruct(DIMS + w.shape[2:], bf16),
         jax.ShapeDtypeStruct((16,) + ew.shape[1:], bf16),
     )
-    late = [send(w, FIRST[4 - m]) for m in (1, 2, 3)]
+    late = [send(w, FIRST[4 - m]) for m in (1, 3, 2)]
     early = {("dense", 0, 0): w, ("dense", 1, 0): send(w, CORE)}
     early |= {("expert", 0, (0, 1, 3)): near, ("expert", 1, (0, 1, 3)): send(near, CORE)}
     placed = place(pos, early, shapes)
     late, far, placed = lax.optimization_barrier((late, far, placed))
-    late = {("dense", 0, m + 1): v for m, v in enumerate(late)} | {("expert", 0, (2,)): far}
+    late = {("dense", 0, m): v for m, v in zip((1, 3, 2), late)} | {("expert", 0, (2,)): far}
     swaps = {(d, 1, m): send(v, CORE) for (d, _, m), v in late.items()}
     placed = place(pos, late, shapes, placed)
     dense_weight, expert_weight = place(pos, swaps, shapes, placed)

time: 137 us -> 136 us (level)
  no operation moved by 1% of the time
where the time goes in v5:
time: 136 us
  waiting for transfers between devices  40 us (29%)
  starting transfers between devices  38.7 us (28%)
  Pallas kernels  26.4 us (19%)
  blocking collectives  20.4 us (15%)
  other arithmetic  5.05 us (4%)
  local copies, waits for them, and re-layouts  3.85 us (3%)
  between operations  1.88 us (1%)
    ppermute x34, waiting for transfers between devices, send(): return lax.ppermute(value, BOTH, pairing)  40 us
    ppermute x34, starting transfers between devices, send(): return lax.ppermute(value, BOTH, pairing)  38.7 us
    all_to_all x1, blocking collectives, per_device(): total = jnp.sum(lax.all_to_all(spread, BOTH, 0, 0, tiled=True))  20.4 us
    pallas_call x4, Pallas kernels, half_terms(): pl.pallas_call(functools.partial(half_kernel, store, other), out_shape=ja...  20 us
    pallas_call x3, Pallas kernels, place(): pl.pallas_call(functools.partial(place_kernel, names), out_shape=shapes,...  6.36 us
    unnamed x22, local copies, waits for them, and re-layouts  3.71 us
  transfers between devices with their start and end apart: 34, of which 21 were waited for; matrix products, arithmetic and copies ran while one was open for 1% of the time, Pallas kernels for 11%

profile of v5, /device:TPU:1, one launch (start us, length us, event | category | flops | bytes accessed | tf_op | source)
XLA Modules:
  0.0 136.3 jit_solution(4258967451092906312)
XLA Ops:
  0.8 2.2 %copy-done = bf16[1,1024,2048]{2,1,0:T(8,128)(2,1)S(1)} copy-done((bf16[1,1024,2048]{2,1,0:T(8,128)(2,1)S(1)}, bf16[1,1024,2048]{2,1,0:T(8,128)(2,1)}, u32[]{:S(2)}) %copy-start) | copy-done | bytes 4194328
  4.4 3.9 %expert_terms.2 = f32[4,2,128,768]{3,2,1,0:T(8,128)S(1)} custom-call(s32[5]{0:T(128)S(1)} %stack.74.pos, bf16[1024,2048]{1,0:T(8,128)(2,1)S(1)} %bitcast.99, bf16[1024,768]{1,0:T(8,128)(2,1)S(1)} %bitcast.101), custom_call_target="tpu_custom_call" | custom-call | flops 3221225472 | bytes 1 | tf_op jit(solution)/shard_map/expert_terms/pallas_call | solution.py:125
  9.8 3.8 %expert_terms.3 = f32[4,2,128,768]{3,2,1,0:T(8,128)S(1)} custom-call(s32[5]{0:T(128)S(1)} %stack.74.pos, bf16[1024,2048]{1,0:T(8,128)(2,1)S(1)} %bitcast.100, bf16[1024,768]{1,0:T(8,128)(2,1)S(1)} %bitcast.102), custom_call_target="tpu_custom_call" | custom-call | flops 3221225472 | bytes 1 | tf_op jit(solution)/shard_map/expert_terms/pallas_call | solution.py:125
  15.5 6.2 %dense_terms.2 = f32[4,4,4,16,1024]{4,3,2,1,0:T(8,128)S(1)} custom-call(s32[5]{0:T(128)S(1)} %stack.74.pos, bf16[1536,2048]{1,0:T(8,128)(2,1)S(1)} %bitcast.98, bf16[1536,1024]{1,0:T(8,128)(2,1)S(1)} %copy-done.1), custom_call_target="tpu_custom_call" | custom-call | flops 6442450944 | bytes 1 | tf_op jit(solution)/shard_map/dense_terms/pallas_call | solution.py:125
  23.4 2.6 %collective-permute-start.12 = (f16[2,128,768]{2,1,0:T(8,128)(2,1)S(1)}, f16[2,128,768]{2,1,0:T(8,128)(2,1)S(1)}, u32[]{:S(2)}, u32[]{:S(2)}) collective-permute-start(f16[2,128,768]{2,1,0:T(8,128)(2,1)S(1)} %get-tuple-element.82), channel_id=1, source_target_pairs={{0,64},{1,65},{2,66},{3,67},{4,68},{5,69},{6,70},{7,71},{8,72},{9,... | collective-permute-start | bytes 1179656 | tf_op jit(solution)/shard_map/ppermute | solution.py:50
  27.1 6.1 %dense_terms.3 = f32[4,4,4,16,1024]{4,3,2,1,0:T(8,128)S(1)} custom-call(s32[5]{0:T(128)S(1)} %stack.74.pos, bf16[1536,2048]{1,0:T(8,128)(2,1)S(1)} %bitcast.98, bf16[1536,1024]{1,0:T(8,128)(2,1)S(1)} %copy-done.1), custom_call_target="tpu_custom_call" | custom-call | flops 6442450944 | bytes 1 | tf_op jit(solution)/shard_map/dense_terms/pallas_call | solution.py:125
  34.1 3.7 %collective-permute-start.4 = (f16[4,4,16,1024]{3,2,1,0:T(8,128)(2,1)S(1)}, f16[4,4,16,1024]{3,2,1,0:T(8,128)(2,1)S(1)}, u32[]{:S(2)}, u32[]{:S(2)}) collective-permute-start(f16[4,4,16,1024]{3,2,1,0:T(8,128)(2,1)S(1)} %get-tuple-element.79), channel_id=1, source_target_pairs={{0,4},{1,5},{2,6},{3,7},{4,0},{5,1},{6,2},{7,3},{8,24},{9,25},{10,... | collective-permute-start | bytes 1572872 | tf_op jit(solution)/shard_map/ppermute | solution.py:50
  39.3 4.3 %collective-permute-done.12 = f16[2,128,768]{2,1,0:T(8,128)(2,1)S(1)} collective-permute-done((f16[2,128,768]{2,1,0:T(8,128)(2,1)S(1)}, f16[2,128,768]{2,1,0:T(8,128)(2,1)S(1)}, u32[]{:S(2)}, u32[]{:S(2)}) %collective-permute-start.12) | collective-permute-done | bytes 393248 | tf_op jit(solution)/shard_map/ppermute | solution.py:50
  43.8 3.7 %collective-permute-start.14 = (f16[128,768]{1,0:T(8,128)(2,1)S(1)}, f16[128,768]{1,0:T(8,128)(2,1)S(1)}, u32[]{:S(2)}, u32[]{:S(2)}) collective-permute-start(f16[128,768]{1,0:T(8,128)(2,1)S(1)} %fusion.34), channel_id=1, source_target_pairs={{0,16},{1,17},{2,18},{3,19},{4,20},{5,21},{6,22},{7,23},{8,24},{9,... | collective-permute-start | bytes 589832 | tf_op jit(solution)/shard_map/ppermute | solution.py:50
  47.5 3.6 %collective-permute-done.3 = f16[4,4,16,1024]{3,2,1,0:T(8,128)(2,1)S(1)} collective-permute-done((f16[4,4,16,1024]{3,2,1,0:T(8,128)(2,1)S(1)}, f16[4,4,16,1024]{3,2,1,0:T(8,128)(2,1)S(1)}, u32[]{:S(2)}, u32[]{:S(2)}) %collective-permute-start.3) | collective-permute-done | bytes 524320 | tf_op jit(solution)/shard_map/ppermute | solution.py:50
  51.8 2.5 %collective-permute-start.7 = (f16[4,16,1024]{2,1,0:T(8,128)(2,1)S(1)}, f16[4,16,1024]{2,1,0:T(8,128)(2,1)S(1)}, u32[]{:S(2)}, u32[]{:S(2)}) collective-permute-start(f16[4,16,1024]{2,1,0:T(8,128)(2,1)S(1)} %get-tuple-element.85), channel_id=1, source_target_pairs={{0,17},{1,0},{2,19},{3,2},{4,21},{5,4},{6,23},{7,6},{8,14},{9,15},... | collective-permute-start | bytes 393224 | tf_op jit(solution)/shard_map/ppermute | solution.py:50
  55.5 2.1 %collective-permute-done.7 = f16[4,16,1024]{2,1,0:T(8,128)(2,1)S(1)} collective-permute-done((f16[4,16,1024]{2,1,0:T(8,128)(2,1)S(1)}, f16[4,16,1024]{2,1,0:T(8,128)(2,1)S(1)}, u32[]{:S(2)}, u32[]{:S(2)}) %collective-permute-start.7) | collective-permute-done | bytes 131104 | tf_op jit(solution)/shard_map/ppermute | solution.py:50
  57.6 2.1 %collective-permute-done.6 = f16[4,16,1024]{2,1,0:T(8,128)(2,1)S(1)} collective-permute-done((f16[4,16,1024]{2,1,0:T(8,128)(2,1)S(1)}, f16[4,16,1024]{2,1,0:T(8,128)(2,1)S(1)}, u32[]{:S(2)}, u32[]{:S(2)}) %collective-permute-start.6) | collective-permute-done | bytes 131104 | tf_op jit(solution)/shard_map/ppermute | solution.py:50
  65.9 1.7 %collective-permute-done.9 = f32[16,1024]{1,0:T(8,128)S(1)} collective-permute-done((f32[16,1024]{1,0:T(8,128)S(1)}, f32[16,1024]{1,0:T(8,128)S(1)}, u32[]{:S(2)}, u32[]{:S(2)}) %collective-permute-start.9) | collective-permute-done | bytes 65568 | tf_op jit(solution)/shard_map/ppermute | solution.py:50
  67.7 20.4 %all_to_all.5 = f32[128,1,128]{2,1,0:T(1,128)S(1)} all-to-all(f32[128,1,128]{2,1,0:T(1,128)S(1)} %broadcast_in_dim.7), channel_id=1, replica_groups=mesh['edp'=16,'ep'=8] {'edp','ep'}, dimensions={0} | all-to-all | bytes 131072 | tf_op jit(solution)/shard_map/all_to_all | solution.py:273
  93.1 1.7 %collective-permute-start.16 = (bf16[16,1024]{1,0:T(8,128)(2,1)S(1)}, bf16[16,1024]{1,0:T(8,128)(2,1)S(1)}, u32[]{:S(2)}, u32[]{:S(2)}) collective-permute-start(bf16[16,1024]{1,0:T(8,128)(2,1)S(1)} %get-tuple-element.47), channel_id=1, source_target_pairs={{0,64},{1,65},{2,66},{3,67},{4,68},{5,69},{6,70},{7,71},{8,72},{9,... | collective-permute-start | bytes 98312 | tf_op jit(solution)/shard_map/ppermute | solution.py:50
  102.2 1.8 %collective-permute-start.19 = (bf16[4,16,1024]{2,1,0:T(8,128)(2,1)S(1)}, bf16[4,16,1024]{2,1,0:T(8,128)(2,1)S(1)}, u32[]{:S(2)}, u32[]{:S(2)}) collective-permute-start(bf16[4,16,1024]{2,1,0:T(8,128)(2,1)S(1)} %get-tuple-element.93), channel_id=1, source_target_pairs={{0,17},{1,0},{2,19},{3,2},{4,21},{5,4},{6,23},{7,6},{8,14},{9,15},... | collective-permute-start | bytes 393224 | tf_op jit(solution)/shard_map/ppermute | solution.py:50
  103.9 3.2 %collective-permute-done.21 = bf16[4,16,1024]{2,1,0:T(8,128)(2,1)S(1)} collective-permute-done((bf16[4,16,1024]{2,1,0:T(8,128)(2,1)S(1)}, bf16[4,16,1024]{2,1,0:T(8,128)(2,1)S(1)}, u32[]{:S(2)}, u32[]{:S(2)}) %collective-permute-start.21) | collective-permute-done | bytes 131104 | tf_op jit(solution)/shard_map/ppermute | solution.py:50
  109.7 3.5 %collective-permute-start.29 = (bf16[3,2,128,768]{3,2,1,0:T(8,128)(2,1)S(1)}, bf16[3,2,128,768]{3,2,1,0:T(8,128)(2,1)S(1)}, u32[]{:S(2)}, u32[]{:S(2)}) collective-permute-start(bf16[3,2,128,768]{3,2,1,0:T(8,128)(2,1)S(1)} %pad_maximum_fusion.refs_2_), channel_id=1, source_target_pairs={{0,8},{1,9},{2,10},{3,11},{4,12},{5,13},{6,14},{7,15},{8,0},{9,1},... | collective-permute-start | bytes 3538952 | tf_op jit(solution)/shard_map/ppermute | solution.py:50
  116.5 2.5 %place.3 = (bf16[4,2,2,4,2,16,1024]{6,5,4,3,2,1,0:T(8,128)(2,1)}, bf16[16,128,768]{2,1,0:T(8,128)(2,1)}) custom-call(s32[5]{0:T(128)S(1)} %stack.74.pos, bf16[4,4,16,1024]{3,2,1,0:T(8,128)(2,1)S(1)} %pad_maximum_fusion.1.refs_0_, bf16[4,4,16,1024]{3,2,1,0:T(8,128)(2,1)S(1)} %collective-permute-done.28.refs_1_, ...), custom_call_target="tpu_custom_call" | custom-call | flops 1 | bytes 1 | tf_op jit(solution)/shard_map/place/pallas_call | solution.py:194
  119.0 8.8 %collective-permute-done.27 = bf16[2,128,768]{2,1,0:T(8,128)(2,1)S(1)} collective-permute-done((bf16[2,128,768]{2,1,0:T(8,128)(2,1)S(1)}, bf16[2,128,768]{2,1,0:T(8,128)(2,1)S(1)}, u32[]{:S(2)}, u32[]{:S(2)}) %collective-permute-start.27) | collective-permute-done | bytes 393248 | tf_op jit(solution)/shard_map/ppermute | solution.py:50
  127.8 1.9 %collective-permute-done.25.refs_1_ = bf16[4,4,16,1024]{3,2,1,0:T(8,128)(2,1)S(1)} collective-permute-done((bf16[4,4,16,1024]{3,2,1,0:T(8,128)(2,1)S(1)}, bf16[4,4,16,1024]{3,2,1,0:T(8,128)(2,1)S(1)}, u32[]{:S(2)}, u32[]{:S(2)}) %collective-permute-start.25) | collective-permute-done | bytes 524320 | tf_op jit(solution)/shard_map/ppermute | solution.py:50
  131.0 1.9 %place.4 = (bf16[4,2,2,4,2,16,1024]{6,5,4,3,2,1,0:T(8,128)(2,1)}, bf16[16,128,768]{2,1,0:T(8,128)(2,1)}) custom-call(s32[5]{0:T(128)S(1)} %stack.74.pos, bf16[4,4,16,1024]{3,2,1,0:T(8,128)(2,1)S(1)} %collective-permute-done.24.refs_0_, bf16[4,4,16,1024]{3,2,1,0:T(8,128)(2,1)S(1)} %collective-permute-done.25.refs_1_, ...), custom_call_target="tpu_custom_call", output_to_operand_aliasing={{0}: (5, {}), {1}: (6, {})} | custom-call | flops 1 | bytes 1 | tf_op jit(solution)/shard_map/place/pallas_call | solution.py:194
  134.1 2.0 %place.5 = (bf16[4,2,2,4,2,16,1024]{6,5,4,3,2,1,0:T(8,128)(2,1)}, bf16[16,128,768]{2,1,0:T(8,128)(2,1)}) custom-call(s32[5]{0:T(128)S(1)} %stack.74.pos, bf16[4,4,16,1024]{3,2,1,0:T(8,128)(2,1)S(1)} %collective-permute-done.30.refs_0_, bf16[4,4,16,1024]{3,2,1,0:T(8,128)(2,1)S(1)} %collective-permute-done.31.refs_1_, ...), custom_call_target="tpu_custom_call", output_to_operand_aliasing={{0}: (5, {}), {1}: (6, {})} | custom-call | flops 1 | bytes 1 | tf_op jit(solution)/shard_map/place/pallas_call | solution.py:194
  (98 shorter events, 38.2 us)
Async XLA Ops:
  8.3 6.8 %collective-permute-start = (f32[4,2,128,768]{3,2,1,0:T(8,128)S(1)}, f32[4,2,128,768]{3,2,1,0:T(8,128)S(1)}, u32[]{:S(2)}, u32[]{:S(2)}) collective-permute-start(f32[4,2,128,768]{3,2,1,0:T(8,128)S(1)} %expert_terms.2), channel_id=1, source_target_pairs={{0,8},{1,9},{2,10},{3,11},{4,12},{5,13},{6,14},{7,15},{8,0},{9,1},... | collective-permute-start | bytes 9437192 | tf_op jit(solution)/shard_map/ppermute | solution.py:50
  21.7 11.6 %collective-permute-start.1 = (f32[4,4,4,16,1024]{4,3,2,1,0:T(8,128)S(1)}, f32[4,4,4,16,1024]{4,3,2,1,0:T(8,128)S(1)}, u32[]{:S(2)}, u32[]{:S(2)}) collective-permute-start(f32[4,4,4,16,1024]{4,3,2,1,0:T(8,128)S(1)} %dense_terms.2), channel_id=1, source_target_pairs={{0,8},{1,9},{2,10},{3,11},{4,12},{5,13},{6,14},{7,15},{8,0},{9,1},... | collective-permute-start | bytes 12582920 | tf_op jit(solution)/shard_map/ppermute | solution.py:50
  22.1 16.2 %collective-permute-start.11 = (f16[2,128,768]{2,1,0:T(8,128)(2,1)S(1)}, f16[2,128,768]{2,1,0:T(8,128)(2,1)S(1)}, u32[]{:S(2)}, u32[]{:S(2)}) collective-permute-start(f16[2,128,768]{2,1,0:T(8,128)(2,1)S(1)} %get-tuple-element.83), channel_id=1, source_target_pairs={{0,32},{1,33},{2,34},{3,35},{4,36},{5,37},{6,38},{7,39},{8,40},{9,... | collective-permute-start | bytes 1179656 | tf_op jit(solution)/shard_map/ppermute | solution.py:50
  23.4 20.1 %collective-permute-start.12 = (f16[2,128,768]{2,1,0:T(8,128)(2,1)S(1)}, f16[2,128,768]{2,1,0:T(8,128)(2,1)S(1)}, u32[]{:S(2)}, u32[]{:S(2)}) collective-permute-start(f16[2,128,768]{2,1,0:T(8,128)(2,1)S(1)} %get-tuple-element.82), channel_id=1, source_target_pairs={{0,64},{1,65},{2,66},{3,67},{4,68},{5,69},{6,70},{7,71},{8,72},{9,... | collective-permute-start | bytes 1179656 | tf_op jit(solution)/shard_map/ppermute | solution.py:50
  26.1 17.5 %collective-permute-start.13 = (f16[2,128,768]{2,1,0:T(8,128)(2,1)S(1)}, f16[2,128,768]{2,1,0:T(8,128)(2,1)S(1)}, u32[]{:S(2)}, u32[]{:S(2)}) collective-permute-start(f16[2,128,768]{2,1,0:T(8,128)(2,1)S(1)} %get-tuple-element.81), channel_id=1, source_target_pairs={{0,96},{1,97},{2,98},{3,99},{4,100},{5,101},{6,102},{7,103},{8,104... | collective-permute-start | bytes 1179656 | tf_op jit(solution)/shard_map/ppermute | solution.py:50
  34.1 13.4 %collective-permute-start.4 = (f16[4,4,16,1024]{3,2,1,0:T(8,128)(2,1)S(1)}, f16[4,4,16,1024]{3,2,1,0:T(8,128)(2,1)S(1)}, u32[]{:S(2)}, u32[]{:S(2)}) collective-permute-start(f16[4,4,16,1024]{3,2,1,0:T(8,128)(2,1)S(1)} %get-tuple-element.79), channel_id=1, source_target_pairs={{0,4},{1,5},{2,6},{3,7},{4,0},{5,1},{6,2},{7,3},{8,24},{9,25},{10,... | collective-permute-start | bytes 1572872 | tf_op jit(solution)/shard_map/ppermute | solution.py:50
  37.8 13.4 %collective-permute-start.3 = (f16[4,4,16,1024]{3,2,1,0:T(8,128)(2,1)S(1)}, f16[4,4,16,1024]{3,2,1,0:T(8,128)(2,1)S(1)}, u32[]{:S(2)}, u32[]{:S(2)}) collective-permute-start(f16[4,4,16,1024]{3,2,1,0:T(8,128)(2,1)S(1)} %get-tuple-element.80), channel_id=1, source_target_pairs={{0,6},{1,7},{2,0},{3,1},{4,2},{5,3},{6,4},{7,5},{8,25},{9,8},{10,2... | collective-permute-start | bytes 1572872 | tf_op jit(solution)/shard_map/ppermute | solution.py:50
  38.3 12.9 %collective-permute-start.2 = (f16[4,4,16,1024]{3,2,1,0:T(8,128)(2,1)S(1)}, f16[4,4,16,1024]{3,2,1,0:T(8,128)(2,1)S(1)}, u32[]{:S(2)}, u32[]{:S(2)}) collective-permute-start(f16[4,4,16,1024]{3,2,1,0:T(8,128)(2,1)S(1)} %get-tuple-element.78), channel_id=1, source_target_pairs={{0,2},{1,3},{2,4},{3,5},{4,6},{5,7},{6,0},{7,1},{8,9},{9,24},{10,1... | collective-permute-start | bytes 1572872 | tf_op jit(solution)/shard_map/ppermute | solution.py:50
  43.8 11.6 %collective-permute-start.14 = (f16[128,768]{1,0:T(8,128)(2,1)S(1)}, f16[128,768]{1,0:T(8,128)(2,1)S(1)}, u32[]{:S(2)}, u32[]{:S(2)}) collective-permute-start(f16[128,768]{1,0:T(8,128)(2,1)S(1)} %fusion.34), channel_id=1, source_target_pairs={{0,16},{1,17},{2,18},{3,19},{4,20},{5,21},{6,22},{7,23},{8,24},{9,... | collective-permute-start | bytes 589832 | tf_op jit(solution)/shard_map/ppermute | solution.py:50
  51.8 5.8 %collective-permute-start.7 = (f16[4,16,1024]{2,1,0:T(8,128)(2,1)S(1)}, f16[4,16,1024]{2,1,0:T(8,128)(2,1)S(1)}, u32[]{:S(2)}, u32[]{:S(2)}) collective-permute-start(f16[4,16,1024]{2,1,0:T(8,128)(2,1)S(1)} %get-tuple-element.85), channel_id=1, source_target_pairs={{0,17},{1,0},{2,19},{3,2},{4,21},{5,4},{6,23},{7,6},{8,14},{9,15},... | collective-permute-start | bytes 393224 | tf_op jit(solution)/shard_map/ppermute | solution.py:50
  54.3 5.4 %collective-permute-start.6 = (f16[4,16,1024]{2,1,0:T(8,128)(2,1)S(1)}, f16[4,16,1024]{2,1,0:T(8,128)(2,1)S(1)}, u32[]{:S(2)}, u32[]{:S(2)}) collective-permute-start(f16[4,16,1024]{2,1,0:T(8,128)(2,1)S(1)} %get-tuple-element.86), channel_id=1, source_target_pairs={{0,16},{1,17},{2,18},{3,19},{4,20},{5,21},{6,22},{7,23},{8,12},{9,... | collective-permute-start | bytes 393224 | tf_op jit(solution)/shard_map/ppermute | solution.py:50
  54.8 6.5 %collective-permute-start.5 = (f16[4,16,1024]{2,1,0:T(8,128)(2,1)S(1)}, f16[4,16,1024]{2,1,0:T(8,128)(2,1)S(1)}, u32[]{:S(2)}, u32[]{:S(2)}) collective-permute-start(f16[4,16,1024]{2,1,0:T(8,128)(2,1)S(1)} %get-tuple-element.84), channel_id=1, source_target_pairs={{0,1},{1,16},{2,3},{3,18},{4,5},{5,20},{6,7},{7,22},{8,10},{9,11},... | collective-permute-start | bytes 393224 | tf_op jit(solution)/shard_map/ppermute | solution.py:50
  62.9 4.6 %collective-permute-start.9 = (f32[16,1024]{1,0:T(8,128)S(1)}, f32[16,1024]{1,0:T(8,128)S(1)}, u32[]{:S(2)}, u32[]{:S(2)}) collective-permute-start(f32[16,1024]{1,0:T(8,128)S(1)} %get-tuple-element.89), channel_id=1, source_target_pairs={{0,64},{1,65},{2,66},{3,67},{4,68},{5,69},{6,70},{7,71},{8,72},{9,... | collective-permute-start | bytes 196616 | tf_op jit(solution)/shard_map/ppermute | solution.py:50
  91.4 7.3 %collective-permute-start.18 = (bf16[128,768]{1,0:T(8,128)(2,1)S(1)}, bf16[128,768]{1,0:T(8,128)(2,1)S(1)}, u32[]{:S(2)}, u32[]{:S(2)}) collective-permute-start(bf16[128,768]{1,0:T(8,128)(2,1)S(1)} %get-tuple-element.48), channel_id=1, source_target_pairs={{0,16},{1,17},{2,18},{3,19},{4,20},{5,21},{6,22},{7,23},{8,24},{9,... | collective-permute-start | bytes 589832 | tf_op jit(solution)/shard_map/ppermute | solution.py:50
  98.8 9.2 %collective-permute-start.22 = (bf16[2,128,768]{2,1,0:T(8,128)(2,1)S(1)}, bf16[2,128,768]{2,1,0:T(8,128)(2,1)S(1)}, u32[]{:S(2)}, u32[]{:S(2)}) collective-permute-start(bf16[2,128,768]{2,1,0:T(8,128)(2,1)S(1)} %get-tuple-element.88), channel_id=1, source_target_pairs={{0,96},{1,97},{2,98},{3,99},{4,100},{5,101},{6,102},{7,103},{8,104... | collective-permute-start | bytes 1179656 | tf_op jit(solution)/shard_map/ppermute | solution.py:50
  100.2 9.3 %collective-permute-start.23 = (bf16[2,128,768]{2,1,0:T(8,128)(2,1)S(1)}, bf16[2,128,768]{2,1,0:T(8,128)(2,1)S(1)}, u32[]{:S(2)}, u32[]{:S(2)}) collective-permute-start(bf16[2,128,768]{2,1,0:T(8,128)(2,1)S(1)} %get-tuple-element.88), channel_id=1, source_target_pairs={{0,32},{1,33},{2,34},{3,35},{4,36},{5,37},{6,38},{7,39},{8,40},{9,... | collective-permute-start | bytes 1179656 | tf_op jit(solution)/shard_map/ppermute | solution.py:50
  100.4 6.8 %collective-permute-start.21 = (bf16[4,16,1024]{2,1,0:T(8,128)(2,1)S(1)}, bf16[4,16,1024]{2,1,0:T(8,128)(2,1)S(1)}, u32[]{:S(2)}, u32[]{:S(2)}) collective-permute-start(bf16[4,16,1024]{2,1,0:T(8,128)(2,1)S(1)} %get-tuple-element.93), channel_id=1, source_target_pairs={{0,1},{1,16},{2,3},{3,18},{4,5},{5,20},{6,7},{7,22},{8,10},{9,11},... | collective-permute-start | bytes 393224 | tf_op jit(solution)/shard_map/ppermute | solution.py:50
  101.1 6.1 %collective-permute-start.20 = (bf16[4,16,1024]{2,1,0:T(8,128)(2,1)S(1)}, bf16[4,16,1024]{2,1,0:T(8,128)(2,1)S(1)}, u32[]{:S(2)}, u32[]{:S(2)}) collective-permute-start(bf16[4,16,1024]{2,1,0:T(8,128)(2,1)S(1)} %get-tuple-element.93), channel_id=1, source_target_pairs={{0,16},{1,17},{2,18},{3,19},{4,20},{5,21},{6,22},{7,23},{8,12},{9,... | collective-permute-start | bytes 393224 | tf_op jit(solution)/shard_map/ppermute | solution.py:50
  102.2 5.6 %collective-permute-start.19 = (bf16[4,16,1024]{2,1,0:T(8,128)(2,1)S(1)}, bf16[4,16,1024]{2,1,0:T(8,128)(2,1)S(1)}, u32[]{:S(2)}, u32[]{:S(2)}) collective-permute-start(bf16[4,16,1024]{2,1,0:T(8,128)(2,1)S(1)} %get-tuple-element.93), channel_id=1, source_target_pairs={{0,17},{1,0},{2,19},{3,2},{4,21},{5,4},{6,23},{7,6},{8,14},{9,15},... | collective-permute-start | bytes 393224 | tf_op jit(solution)/shard_map/ppermute | solution.py:50
  109.7 6.8 %collective-permute-start.29 = (bf16[3,2,128,768]{3,2,1,0:T(8,128)(2,1)S(1)}, bf16[3,2,128,768]{3,2,1,0:T(8,128)(2,1)S(1)}, u32[]{:S(2)}, u32[]{:S(2)}) collective-permute-start(bf16[3,2,128,768]{3,2,1,0:T(8,128)(2,1)S(1)} %pad_maximum_fusion.refs_2_), channel_id=1, source_target_pairs={{0,8},{1,9},{2,10},{3,11},{4,12},{5,13},{6,14},{7,15},{8,0},{9,1},... | collective-permute-start | bytes 3538952 | tf_op jit(solution)/shard_map/ppermute | solution.py:50
  113.3 14.5 %collective-permute-start.24 = (bf16[4,4,16,1024]{3,2,1,0:T(8,128)(2,1)S(1)}, bf16[4,4,16,1024]{3,2,1,0:T(8,128)(2,1)S(1)}, u32[]{:S(2)}, u32[]{:S(2)}) collective-permute-start(bf16[4,4,16,1024]{3,2,1,0:T(8,128)(2,1)S(1)} %pad_maximum_fusion.1.refs_0_), channel_id=1, source_target_pairs={{0,6},{1,7},{2,0},{3,1},{4,2},{5,3},{6,4},{7,5},{8,25},{9,8},{10,2... | collective-permute-start | bytes 1572872 | tf_op jit(solution)/shard_map/ppermute | solution.py:50
  114.6 15.2 %collective-permute-start.25 = (bf16[4,4,16,1024]{3,2,1,0:T(8,128)(2,1)S(1)}, bf16[4,4,16,1024]{3,2,1,0:T(8,128)(2,1)S(1)}, u32[]{:S(2)}, u32[]{:S(2)}) collective-permute-start(bf16[4,4,16,1024]{3,2,1,0:T(8,128)(2,1)S(1)} %pad_maximum_fusion.1.refs_0_), channel_id=1, source_target_pairs={{0,2},{1,3},{2,4},{3,5},{4,6},{5,7},{6,0},{7,1},{8,9},{9,24},{10,1... | collective-permute-start | bytes 1572872 | tf_op jit(solution)/shard_map/ppermute | solution.py:50
  114.7 15.0 %collective-permute-start.26 = (bf16[4,4,16,1024]{3,2,1,0:T(8,128)(2,1)S(1)}, bf16[4,4,16,1024]{3,2,1,0:T(8,128)(2,1)S(1)}, u32[]{:S(2)}, u32[]{:S(2)}) collective-permute-start(bf16[4,4,16,1024]{3,2,1,0:T(8,128)(2,1)S(1)} %pad_maximum_fusion.1.refs_0_), channel_id=1, source_target_pairs={{0,4},{1,5},{2,6},{3,7},{4,0},{5,1},{6,2},{7,3},{8,24},{9,25},{10,... | collective-permute-start | bytes 1572872 | tf_op jit(solution)/shard_map/ppermute | solution.py:50
  116.4 11.4 %collective-permute-start.27 = (bf16[2,128,768]{2,1,0:T(8,128)(2,1)S(1)}, bf16[2,128,768]{2,1,0:T(8,128)(2,1)S(1)}, u32[]{:S(2)}, u32[]{:S(2)}) collective-permute-start(bf16[2,128,768]{2,1,0:T(8,128)(2,1)S(1)} %get-tuple-element.88), channel_id=1, source_target_pairs={{0,64},{1,65},{2,66},{3,67},{4,68},{5,69},{6,70},{7,71},{8,72},{9,... | collective-permute-start | bytes 1179656 | tf_op jit(solution)/shard_map/ppermute | solution.py:50
  (21 other events, 290.0 us)
